TPU v7x, 32 devices: a whole 2x2x4 slice. The times are simulated.
32 devices in a mesh: scene: 4 (over y, x), dom: 8 (over z, core).
Axes of the slice: x: 2, y: 2, z: 4, core: 2. Of those that a mesh axis runs over, the one named last changes fastest.
Arguments:
- features: bfloat16 [256, 64, 512], P(('scene', 'dom')), parts along dimension 0, may hold values from -6 to 6
- cotangent: bfloat16 [256, 64, 512], P(('scene', 'dom')), parts along dimension 0, may hold values from -6 to 6
- weight: bfloat16 [27, 64, 64], replicated, may hold values from -0.15625 to 0.15625
- mask_words: int32 [256, 18], P(('scene', 'dom')), parts along dimension 0, may hold values from 0 to 1073741823, as said below
- neighbors: int32 [256, 26], P(('scene', 'dom')), parts along dimension 0, may hold values from -1 to 63, as said below
Outputs:
- out_features: bfloat16 [256, 64, 512], P(('scene', 'dom')), parts along dimension 0
- in_grad: bfloat16 [256, 64, 512], P(('scene', 'dom')), parts along dimension 0
- weight_grad: float32 [108, 64, 64], P('scene'), parts along dimension 0
There are 4 independent parts, one for each index of `scene`. A program takes and returns all parts, laid end to end along the dimension named above; an argument that names none is the same for every part. Nothing has to cross between parts.
Inputs may be any that keep to these rules, and one draw needn't show every extreme that they name: `mask_words`: bit r of word w is voxel 30 w + r of the leaf; bits at or past 512 are 0; unused slots have all bits 0. An id is owner * 8 + slot, owner being the index along dom. All leaves at one leaf position along the first dimension have the same owner; a neighbor at first offset -1 is owned by the same device or the one below it, at +1 by the same device or the one above it. The table is symmetric: b is listed as a neighbor of a at offset (p, q, r) exactly when a is listed for b at (-p, -q, -r). Used slots of a device come first; unused slots list no neighbors. At most 4 leaves of one device have a neighbor owned by one given adjacent device, and some device reaches that in every draw; some device uses all 8 slots in every draw.
All inputs are finite; a program needn't handle non-finite values.
Results may differ from a plain program's by a relative error of at most 0.001.
Values may be sent and summed in bfloat16 or wider, within the bound.
No kernel may reach another device: no remote copies, remote signals or barrier semaphores. Data moves between devices by JAX's collectives and lax.ppermute only.
A program may use at most 256 MiB of HBM per device.

v0:
```python
import jax
import jax.numpy as jnp
import numpy as np
from jax import lax
from jax.sharding import PartitionSpec as P

LEAF = 8


def with_halo(shard, sides, width):
    for axis, dim in sides:
        size, length = (lax.axis_size(axis), shard.shape[dim])
        up = [(i, (i + 1) % size) for i in range(size - 1)]
        down = [(j, i) for i, j in up]
        last = lax.slice_in_dim(shard, length - width, length, axis=dim)
        leading = lax.slice_in_dim(shard, 0, width, axis=dim)
        before = lax.ppermute(last, axis, up)
        after = lax.ppermute(leading, axis, down)
        shard = jnp.concatenate([before, shard, after], axis=dim)
    return shard


def unpack_voxels(mask_words, voxel_count):
    bit_place = jnp.arange(30, dtype=jnp.int32)
    bit_values = jnp.right_shift(mask_words[:, :, None], bit_place[None, None, :]) & 1
    return bit_values.reshape(mask_words.shape[0], -1)[:, :voxel_count]


def column_of(shift_x, shift_y, shift_z):
    tap_number = (shift_x + 1) * 9 + (shift_y + 1) * 3 + shift_z + 1
    return tap_number if tap_number < 13 else tap_number - 1


def tap_offsets():
    return [
        (shift_x, shift_y, shift_z)
        for shift_x in (-1, 0, 1)
        for shift_y in (-1, 0, 1)
        for shift_z in (-1, 0, 1)
    ]


def axis_cells(shift_value, extent):
    if shift_value < 0:
        return ([0], [extent - 1])
    if shift_value > 0:
        return ([extent + 1], [0])
    return (list(range(1, extent + 1)), list(range(extent)))


def region_tables(offset, extent):
    side = extent + 2
    dest_a, src_a = axis_cells(offset[0], extent)
    dest_b, src_b = axis_cells(offset[1], extent)
    dest_c, src_c = axis_cells(offset[2], extent)
    dest_list = []
    src_list = []
    for index_a in range(len(dest_a)):
        for index_b in range(len(dest_b)):
            for index_c in range(len(dest_c)):
                dest_list.append(
                    (dest_a[index_a] * side + dest_b[index_b]) * side + dest_c[index_c]
                )
                if offset[0] == 0:
                    src_list.append(
                        (src_a[index_a] * extent + src_b[index_b]) * extent + src_c[index_c]
                    )
                else:
                    src_list.append(src_b[index_b] * extent + src_c[index_c])
    return (np.array(dest_list, dtype=np.int32), np.array(src_list, dtype=np.int32))


def take_rows(source, row_index, keep_rows):
    picked = jnp.take(source, jnp.clip(row_index, 0, source.shape[0] - 1), axis=0)
    return jnp.where(keep_rows[:, None, None], picked, jnp.zeros((), source.dtype))


def shards(features, cotangent, weight, mask_words, neighbors):
    leaf_count, channels, voxel_count = features.shape
    edge_cells = LEAF
    side = edge_cells + 2
    padded_cells = side**3
    span_start = side * side + side + 1
    span_cells = padded_cells - 2 * span_start
    face_cells = edge_cells * edge_cells
    device = lax.axis_index("dom")
    occupancy = unpack_voxels(mask_words, voxel_count).astype(features.dtype)
    masked_x = features * occupancy[:, None, :]
    masked_dy = cotangent * occupancy[:, None, :]
    plane_size = channels * face_cells
    low_planes = jnp.stack(
        [
            masked_x[:, :, :face_cells].reshape(leaf_count, plane_size),
            masked_dy[:, :, :face_cells].reshape(leaf_count, plane_size),
        ]
    )
    high_planes = jnp.stack(
        [
            masked_x[:, :, voxel_count - face_cells :].reshape(leaf_count, plane_size),
            masked_dy[:, :, voxel_count - face_cells :].reshape(leaf_count, plane_size),
        ]
    )
    present = neighbors >= 0
    owner_dev = jnp.where(present, neighbors // leaf_count, -2)
    local_here = present & (owner_dev == device)
    from_below = present & (owner_dev == device - 1)
    from_above = present & (owner_dev == device + 1)
    slot_here = neighbors - device * leaf_count
    slot_below = neighbors - (device - 1) * leaf_count
    slot_above = neighbors - (device + 1) * leaf_count
    outgoing = jnp.stack([low_planes, high_planes])
    received = with_halo(outgoing, (("dom", 0),), 1)
    offsets = tap_offsets()
    inner_dest, inner_src = region_tables((0, 0, 0), edge_cells)

    def padded_field(field_number, center):
        pool_high = jnp.concatenate(
            [high_planes[field_number], received[0, field_number]], axis=0
        ).reshape(-1, channels, face_cells)
        pool_low = jnp.concatenate(
            [low_planes[field_number], received[3, field_number]], axis=0
        ).reshape(-1, channels, face_cells)
        padded = (
            jnp.zeros((leaf_count, channels, padded_cells), center.dtype)
            .at[:, :, inner_dest]
            .set(center)
        )
        for offset in offsets:
            if offset == (0, 0, 0):
                continue
            dest_index, src_index = region_tables(offset, edge_cells)
            column = column_of(offset[0], offset[1], offset[2])
            if offset[0] == 0:
                source = jnp.take(center, src_index, axis=2)
                row_index = slot_here[:, column]
                keep_rows = local_here[:, column]
            elif offset[0] < 0:
                source = jnp.take(pool_high, src_index, axis=2)
                row_index = jnp.where(
                    local_here[:, column], slot_here[:, column], leaf_count + slot_below[:, column]
                )
                keep_rows = local_here[:, column] | from_below[:, column]
            else:
                source = jnp.take(pool_low, src_index, axis=2)
                row_index = jnp.where(
                    local_here[:, column], slot_here[:, column], leaf_count + slot_above[:, column]
                )
                keep_rows = local_here[:, column] | from_above[:, column]
            padded = padded.at[:, :, dest_index].set(take_rows(source, row_index, keep_rows))
        return padded

    padded_x = padded_field(0, masked_x)
    padded_dy = padded_field(1, masked_dy)
    span_dy = (
        jnp.zeros((leaf_count, channels, span_cells), masked_dy.dtype)
        .at[:, :, inner_dest - span_start]
        .set(masked_dy)
    )
    shift_list = [(offset[0] * side + offset[1]) * side + offset[2] for offset in offsets]
    group_size = max(1, leaf_count // 8)
    block_count = leaf_count // group_size
    flat_weight = weight.reshape(27 * channels, channels)
    turned_weight = jnp.transpose(weight, (1, 0, 2)).reshape(channels, 27 * channels)

    def block_terms(inputs):
        pad_x_block, pad_dy_block, dy_block = inputs
        stack_x = jnp.concatenate(
            [
                pad_x_block[:, :, span_start + shift : span_start + shift + span_cells]
                for shift in shift_list
            ],
            axis=1,
        )
        stack_dy = jnp.concatenate(
            [
                pad_dy_block[:, :, span_start - shift : span_start - shift + span_cells]
                for shift in shift_list
            ],
            axis=1,
        )
        out_block = jnp.einsum(
            "ko,lkv->lov", flat_weight, stack_x, preferred_element_type=jnp.float32
        )
        back_block = jnp.einsum(
            "ik,lkv->liv", turned_weight, stack_dy, preferred_element_type=jnp.float32
        )
        grad_block = jnp.einsum(
            "lkv,lov->ko", stack_x, dy_block, preferred_element_type=jnp.float32
        )
        return (out_block, back_block, grad_block)

    def regroup(array):
        return array.reshape((block_count, group_size) + array.shape[1:])

    out_parts, back_parts, grad_parts = lax.map(
        block_terms, (regroup(padded_x), regroup(padded_dy), regroup(span_dy))
    )
    out_sum = out_parts.reshape(leaf_count, channels, span_cells)
    back_sum = back_parts.reshape(leaf_count, channels, span_cells)
    grad_local = jnp.sum(grad_parts, axis=0).reshape(27, channels, channels)
    inner_span = inner_dest - span_start
    occupancy_wide = occupancy.astype(jnp.float32)[:, None, :]
    out_features = (jnp.take(out_sum, inner_span, axis=2) * occupancy_wide).astype(jnp.bfloat16)
    in_grad = (jnp.take(back_sum, inner_span, axis=2) * occupancy_wide).astype(jnp.bfloat16)
    grad_scale = float(lax.axis_size("dom") * leaf_count * voxel_count) ** (-0.5)
    summed_grad = lax.psum(grad_local.reshape(-1), "dom")
    weight_grad = summed_grad.reshape(27, channels, channels) * grad_scale
    return (out_features, in_grad, weight_grad)


def solution(mesh):
    placed = (
        P(("scene", "dom"), None, None),
        P(("scene", "dom"), None, None),
        P(),
        P(("scene", "dom"), None),
        P(("scene", "dom"), None),
    )
    return jax.shard_map(
        shards,
        mesh=mesh,
        in_specs=placed,
        out_specs=(
            P(("scene", "dom"), None, None),
            P(("scene", "dom"), None, None),
            P("scene", None, None),
        ),
        check_vma=False,
    )
```

profile of v0, /device:TPU:0, one launch (start us, length us, event | category | flops | bytes accessed | tf_op | source)
XLA Modules:
  0.0 511.3 jit_solution(5696457219207228298)
XLA Ops:
  8.4 1.8 copy.271
  12.0 1.7 broadcast_multiply_fusion
  18.0 3.7 collective-permute-start
  85.7 13.8 %scatter_fusion.38 = bf16[8,64,778]{1,0,2:T(8,128)(2,1)S(1)} fusion(bf16[8,64,778]{1,0,2:T(8,128)(2,1)S(1)} %broadcast_in_dim.665, s32[512]{0:T(512)} %constant.642.clone, bf16[512,8,64]{2,1,0:T(8,128)(2,1)S(1)} %bitcast.358), kind=kCustom, calls=%fused_computation.128 | custom fusion | bytes 1574912 | tf_op jit(solution)/shard_map/scatter | solution.py:157
  99.5 2.5 copy.356
  103.7 13.7 %scatter_fusion.19 = bf16[8,64,1000]{1,0,2:T(8,128)(2,1)S(1)} fusion(bf16[8,64,1000]{1,0,2:T(8,128)(2,1)S(1)} %broadcast.489.clone, s32[512]{0:T(512)} %constant.1068, bf16[512,8,64]{2,1,0:T(8,128)(2,1)S(1)} %bitcast.359), kind=kCustom, calls=%fused_computation.109 | custom fusion | bytes 1574912 | tf_op jit(solution)/shard_map/scatter | solution.py:126
  120.0 13.7 %scatter_fusion = bf16[8,64,1000]{1,0,2:T(8,128)(2,1)S(1)} fusion(bf16[8,64,1000]{1,0,2:T(8,128)(2,1)S(1)} %broadcast.489.clone.1, s32[512]{0:T(512)} %constant.1068, bf16[512,8,64]{2,1,0:T(8,128)(2,1)S(1)} %bitcast.361), kind=kCustom, calls=%fused_computation.90 | custom fusion | bytes 1574912 | tf_op jit(solution)/shard_map/scatter | solution.py:126
  173.9 1.9 gather_fusion
  175.8 2.0 gather_fusion.44
  179.9 1.9 gather_fusion.3
  181.8 1.9 gather_fusion.47
  186.6 2.2 select_bitcast_fusion
  193.4 1.8 fusion.34
  202.3 1.9 gather_fusion.10
  204.2 1.9 gather_fusion.54
  206.8 1.9 gather_fusion.13
  208.8 1.9 gather_fusion.57
  210.7 2.0 gather_fusion.30
  212.6 1.9 gather_fusion.74
  216.8 1.9 gather_fusion.33
  218.7 1.9 gather_fusion.77
  241.0 2.1 scatter_fusion.20
  245.3 2.1 scatter_fusion.21
  247.4 2.7 scatter_fusion.3
  250.1 6.5 %scatter_fusion.22 = bf16[8,64,1000]{1,0,2:T(8,128)(2,1)} fusion(bf16[8,64,1000]{1,0,2:T(8,128)(2,1)} %scatter_fusion.21, s32[64]{0:T(128)S(1)} %copy-done.81, bf16[64,8,64]{2,1,0:T(8,128)(2,1)S(1)} %copy-done.47), kind=kCustom, calls=%fused_computation.112 | custom fusion | bytes 196864 | tf_op jit(solution)/shard_map/scatter | solution.py:149
  257.4 1.9 scatter_fusion.23
  260.7 1.9 scatter_fusion.24
  264.1 1.9 scatter_fusion.25
  266.0 2.6 scatter_fusion.7
  268.6 6.9 %scatter_fusion.26 = bf16[8,64,1000]{1,0,2:T(8,128)(2,1)} fusion(bf16[8,64,1000]{1,0,2:T(8,128)(2,1)} %scatter_fusion.25, s32[64]{0:T(128)S(1)} %copy-done.77, bf16[64,8,64]{2,1,0:T(8,128)(2,1)} %copy.329), kind=kCustom, calls=%fused_computation.116 | custom fusion | bytes 196864 | tf_op jit(solution)/shard_map/scatter | solution.py:149
  276.3 1.9 scatter_fusion.27
  278.2 2.4 scatter_fusion.9
  280.7 6.9 %scatter_fusion.28 = bf16[8,64,1000]{1,0,2:T(8,128)(2,1)} fusion(bf16[8,64,1000]{1,0,2:T(8,128)(2,1)} %scatter_fusion.27, s32[64]{0:T(128)S(1)} %copy-done.75, bf16[64,8,64]{2,1,0:T(8,128)(2,1)} %copy.333), kind=kCustom, calls=%fused_computation.118 | custom fusion | bytes 196864 | tf_op jit(solution)/shard_map/scatter | solution.py:149
  287.5 2.4 scatter_fusion.10
  290.0 6.6 %scatter_fusion.29 = bf16[8,64,1000]{1,0,2:T(8,128)(2,1)} fusion(bf16[8,64,1000]{1,0,2:T(8,128)(2,1)} %scatter_fusion.28, s32[64]{0:T(128)S(1)} %copy-done.74, bf16[64,8,64]{2,1,0:T(8,128)(2,1)S(1)} %copy-done.44), kind=kCustom, calls=%fused_computation.119 | custom fusion | bytes 196864 | tf_op jit(solution)/shard_map/scatter | solution.py:149
  297.3 1.9 scatter_fusion.30
  299.2 2.4 scatter_fusion.12
  301.7 6.6 %scatter_fusion.31 = bf16[8,64,1000]{1,0,2:T(8,128)(2,1)} fusion(bf16[8,64,1000]{1,0,2:T(8,128)(2,1)} %scatter_fusion.30, s32[64]{0:T(128)S(1)} %copy-done.72, bf16[64,8,64]{2,1,0:T(8,128)(2,1)S(1)} %copy-done.42), kind=kCustom, calls=%fused_computation.121 | custom fusion | bytes 196864 | tf_op jit(solution)/shard_map/scatter | solution.py:149
  309.1 1.9 scatter_fusion.32
  312.4 1.9 scatter_fusion.33
  315.7 1.9 scatter_fusion.34
  317.6 2.4 scatter_fusion.16
  320.0 6.5 %scatter_fusion.35 = bf16[8,64,1000]{1,0,2:T(8,128)(2,1)} fusion(bf16[8,64,1000]{1,0,2:T(8,128)(2,1)} %scatter_fusion.34, s32[64]{0:T(128)S(1)} %copy-done.68, bf16[64,8,64]{2,1,0:T(8,128)(2,1)S(1)} %copy-done.46), kind=kCustom, calls=%fused_computation.125 | custom fusion | bytes 196864 | tf_op jit(solution)/shard_map/scatter | solution.py:149
  327.3 1.9 scatter_fusion.36
  330.5 1.9 scatter_fusion.37
  333.1 1.9 copy.354
  335.0 2.6 copy.355
  337.6 89.4 %while.31 = (s32[]{:T(128)}, f32[8,1,64,778]{3,2,1,0:T(8,128)}, f32[8,1,64,778]{3,2,1,0:T(8,128)}, f32[8,1728,64]{1,2,0:T(8,128)}, bf16[8,1,64,1000]{3,2,1,0:T(8...) while((s32[]{:T(128)}, f32[8,1,64,778]{3,2,1,0:T(8,128)}, ...), condition=%wide.region_56.67_spmd, body=%wide.region_55.66_spmd.sunk | while | flops 516243456 | bytes 22411112 | solution.py:195
  345.0 2.7 fusion.141
  356.1 2.7 fusion.141
  367.3 2.7 fusion.141
  378.4 2.7 fusion.141
  389.5 2.7 fusion.141
  400.7 2.7 fusion.141
  411.8 2.7 fusion.141
  422.9 2.7 fusion.141
  427.0 3.6 copy.357
  430.6 2.8 copy.359
  433.4 4.2 gather_fusion.88
  437.6 2.7 gather_fusion.89
  440.3 2.3 reduce_sum.9
  444.4 2.8 fusion.27
  447.1 2.6 copy.361
  451.3 50.6 %all-reduce.2.cloned.1.call-done = f32[110592]{0:T(1024)} async-done(((f32[110592]{0:T(1024)}), f32[110592]{0:T(1024)}) %all-reduce.2.cloned.1.call-update) | async-done | bytes 442384 | tf_op jit(solution)/shard_map/psum | solution.py:206
  (1026 shorter events, 238.7 us)
Async XLA Ops:
  7.2 494.7 %all-reduce.2.cloned.1.call-start = ((), (), s32[]{:S(2)}) async-start(), calls=%async_computation | async-start | bytes 884736 | tf_op jit(solution)/shard_map/psum | solution.py:206
  13.7 26.4 %copy-start.3 = (bf16[8,64,512]{1,0,2:T(8,128)(2,1)}, bf16[8,64,512]{1,0,2:T(8,128)(2,1)S(1)}, u32[]{:S(2)}) copy-start(bf16[8,64,512]{1,0,2:T(8,128)(2,1)S(1)} %get-tuple-element.404) | copy-start | bytes 1572868
  15.2 131.4 %collective-permute-start.1 = (bf16[1,2,8,4096]{3,2,1,0:T(8,128)(2,1)}, bf16[1,2,8,4096]{3,2,1,0:T(8,128)(2,1)}, u32[]{:S(2)}, u32[]{:S(2)}) collective-permute-start(bf16[1,2,8,4096]{3,2,1,0:T(8,128)(2,1)} %maximum_bitcast_fusion.1), channel_id=1, source_target_pairs={{1,0},{2,1},{3,2},{4,3},{5,4},{6,5},{7,6},{9,8},{10,9},{11,10},{12... | collective-permute-start | bytes 393224 | tf_op jit(solution)/shard_map/ppermute | solution.py:18
  18.0 116.6 %collective-permute-start = (bf16[1,2,8,4096]{3,2,1,0:T(8,128)(2,1)}, bf16[1,2,8,4096]{3,2,1,0:T(8,128)(2,1)}, u32[]{:S(2)}, u32[]{:S(2)}) collective-permute-start(bf16[1,2,8,4096]{3,2,1,0:T(8,128)(2,1)} %maximum_bitcast_fusion), channel_id=1, source_target_pairs={{0,1},{1,2},{2,3},{3,4},{4,5},{5,6},{6,7},{8,9},{9,10},{10,11},{11... | collective-permute-start | bytes 393224 | tf_op jit(solution)/shard_map/ppermute | solution.py:17
  46.8 95.8 %copy-start.52 = (s32[1024]{0:T(1024)}, s32[1024]{0:T(1024)S(1)}, u32[]{:S(2)}) copy-start(s32[1024]{0:T(1024)S(1)} %pad_clamp_fusion.38) | copy-start | bytes 12292
  48.0 96.9 %copy-start.53 = (s32[1024]{0:T(1024)}, s32[1024]{0:T(1024)S(1)}, u32[]{:S(2)}) copy-start(s32[1024]{0:T(1024)S(1)} %pad_clamp_fusion.35) | copy-start | bytes 12292
  191.9 31.0 %copy-start.37 = (bf16[16,64,64]{1,0,2:T(8,128)(2,1)S(1)}, bf16[16,64,64]{1,0,2:T(8,128)(2,1)}, u32[]{:S(2)}) copy-start(bf16[16,64,64]{1,0,2:T(8,128)(2,1)} %get-tuple-element.472) | copy-start | bytes 393220
  193.4 30.5 %copy-start.36 = (bf16[16,64,64]{1,0,2:T(8,128)(2,1)S(1)}, bf16[16,64,64]{1,0,2:T(8,128)(2,1)}, u32[]{:S(2)}) copy-start(bf16[16,64,64]{1,0,2:T(8,128)(2,1)} %get-tuple-element.471) | copy-start | bytes 393220
  197.7 29.6 %copy-start.101 = (pred[8]{0:T(512)(128)(4,1)S(1)}, pred[8]{0:T(512)(128)(4,1)}, u32[]{:S(2)}) copy-start(pred[8]{0:T(512)(128)(4,1)} %get-tuple-element.335) | copy-start | bytes 28
  197.7 29.6 %copy-start.102 = (pred[8]{0:T(512)(128)(4,1)S(1)}, pred[8]{0:T(512)(128)(4,1)}, u32[]{:S(2)}) copy-start(pred[8]{0:T(512)(128)(4,1)} %get-tuple-element.511) | copy-start | bytes 28
  201.5 27.5 %copy-start.49 = (bf16[16,64,8]{1,0,2:T(8,128)(2,1)S(1)}, bf16[16,64,8]{1,0,2:T(8,128)(2,1)}, u32[]{:S(2)}) copy-start(bf16[16,64,8]{1,0,2:T(8,128)(2,1)} %get-tuple-element.468) | copy-start | bytes 49156
  228.2 21.9 %copy-start.47 = (bf16[64,8,64]{2,1,0:T(8,128)(2,1)S(1)}, bf16[64,8,64]{2,1,0:T(8,128)(2,1)}, u32[]{:S(2)}) copy-start(bf16[64,8,64]{2,1,0:T(8,128)(2,1)} %copy.321) | copy-start | bytes 196612
  229.8 26.8 %copy-start.80 = (s32[8]{0:T(128)S(1)}, s32[8]{0:T(128)}, u32[]{:S(2)}) copy-start(s32[8]{0:T(128)} %constant.1072) | copy-start | bytes 100
  232.9 26.4 %copy-start.64 = (bf16[8,64]{1,0:T(8,128)(2,1)S(1)}, bf16[8,64]{1,0:T(8,128)(2,1)}, u32[]{:S(2)}) copy-start(bf16[8,64]{1,0:T(8,128)(2,1)} %gather_fusion.10) | copy-start | bytes 3076
  232.9 26.4 %copy-start.65 = (bf16[8,64]{1,0:T(8,128)(2,1)S(1)}, bf16[8,64]{1,0:T(8,128)(2,1)}, u32[]{:S(2)}) copy-start(bf16[8,64]{1,0:T(8,128)(2,1)} %gather_fusion.54) | copy-start | bytes 3076
  232.9 26.4 %copy-start.93 = (pred[8]{0:T(512)(128)(4,1)S(1)}, pred[8]{0:T(512)(128)(4,1)}, u32[]{:S(2)}) copy-start(pred[8]{0:T(512)(128)(4,1)} %get-tuple-element.342) | copy-start | bytes 28
  232.9 26.4 %copy-start.97 = (pred[8]{0:T(512)(128)(4,1)S(1)}, pred[8]{0:T(512)(128)(4,1)}, u32[]{:S(2)}) copy-start(pred[8]{0:T(512)(128)(4,1)} %get-tuple-element.527) | copy-start | bytes 28
  232.9 27.1 %copy-start.79 = (s32[8]{0:T(128)S(1)}, s32[8]{0:T(128)}, u32[]{:S(2)}) copy-start(s32[8]{0:T(128)} %constant.1073) | copy-start | bytes 100
  236.4 26.2 %copy-start.62 = (bf16[8,64]{1,0:T(8,128)(2,1)S(1)}, bf16[8,64]{1,0:T(8,128)(2,1)}, u32[]{:S(2)}) copy-start(bf16[8,64]{1,0:T(8,128)(2,1)} %gather_fusion.13) | copy-start | bytes 3076
  236.5 26.2 %copy-start.63 = (bf16[8,64]{1,0:T(8,128)(2,1)S(1)}, bf16[8,64]{1,0:T(8,128)(2,1)}, u32[]{:S(2)}) copy-start(bf16[8,64]{1,0:T(8,128)(2,1)} %gather_fusion.57) | copy-start | bytes 3076
  236.5 26.1 %copy-start.92 = (pred[8]{0:T(512)(128)(4,1)S(1)}, pred[8]{0:T(512)(128)(4,1)}, u32[]{:S(2)}) copy-start(pred[8]{0:T(512)(128)(4,1)} %get-tuple-element.340) | copy-start | bytes 28
  236.5 26.1 %copy-start.94 = (pred[8]{0:T(512)(128)(4,1)S(1)}, pred[8]{0:T(512)(128)(4,1)}, u32[]{:S(2)}) copy-start(pred[8]{0:T(512)(128)(4,1)} %get-tuple-element.525) | copy-start | bytes 28
  236.5 26.8 %copy-start.30 = (bf16[8,8,64]{2,1,0:T(8,128)(2,1)S(1)}, bf16[8,8,64]{2,1,0:T(8,128)(2,1)}, u32[]{:S(2)}) copy-start(bf16[8,8,64]{2,1,0:T(8,128)(2,1)} %copy.287) | copy-start | bytes 24580
  236.5 26.8 %copy-start.78 = (s32[8]{0:T(128)S(1)}, s32[8]{0:T(128)}, u32[]{:S(2)}) copy-start(s32[8]{0:T(128)} %constant.1074) | copy-start | bytes 100
  240.0 24.1 %copy-start.32 = (bf16[8,8,64]{2,1,0:T(8,128)(2,1)S(1)}, bf16[8,8,64]{2,1,0:T(8,128)(2,1)}, u32[]{:S(2)}) copy-start(bf16[8,8,64]{2,1,0:T(8,128)(2,1)} %copy.327) | copy-start | bytes 24580
  240.9 25.0 %copy-start.43 = (bf16[64,8,64]{2,1,0:T(8,128)(2,1)S(1)}, bf16[64,8,64]{2,1,0:T(8,128)(2,1)}, u32[]{:S(2)}) copy-start(bf16[64,8,64]{2,1,0:T(8,128)(2,1)} %copy.289) | copy-start | bytes 196612
  241.0 25.0 %copy-start.77 = (s32[64]{0:T(128)S(1)}, s32[64]{0:T(128)}, u32[]{:S(2)}) copy-start(s32[64]{0:T(128)} %constant.1075) | copy-start | bytes 772
  245.3 30.2 %copy-start.28 = (bf16[8,8,64]{2,1,0:T(8,128)(2,1)S(1)}, bf16[8,8,64]{2,1,0:T(8,128)(2,1)}, u32[]{:S(2)}) copy-start(bf16[8,8,64]{2,1,0:T(8,128)(2,1)} %copy.291) | copy-start | bytes 24580
  245.3 30.2 %copy-start.76 = (s32[8]{0:T(128)S(1)}, s32[8]{0:T(128)}, u32[]{:S(2)}) copy-start(s32[8]{0:T(128)} %constant.1076) | copy-start | bytes 100
  247.4 28.8 %copy-start.31 = (bf16[8,8,64]{2,1,0:T(8,128)(2,1)S(1)}, bf16[8,8,64]{2,1,0:T(8,128)(2,1)}, u32[]{:S(2)}) copy-start(bf16[8,8,64]{2,1,0:T(8,128)(2,1)} %copy.331) | copy-start | bytes 24580
  250.1 28.0 %copy-start.41 = (bf16[64,8,64]{2,1,0:T(8,128)(2,1)S(1)}, bf16[64,8,64]{2,1,0:T(8,128)(2,1)}, u32[]{:S(2)}) copy-start(bf16[64,8,64]{2,1,0:T(8,128)(2,1)} %copy.293) | copy-start | bytes 196612
  250.1 28.0 %copy-start.75 = (s32[64]{0:T(128)S(1)}, s32[64]{0:T(128)}, u32[]{:S(2)}) copy-start(s32[64]{0:T(128)} %constant.1077) | copy-start | bytes 772
  257.4 30.1 %copy-start.40 = (bf16[64,8,64]{2,1,0:T(8,128)(2,1)S(1)}, bf16[64,8,64]{2,1,0:T(8,128)(2,1)}, u32[]{:S(2)}) copy-start(bf16[64,8,64]{2,1,0:T(8,128)(2,1)} %copy.295) | copy-start | bytes 196612
  257.4 30.1 %copy-start.74 = (s32[64]{0:T(128)S(1)}, s32[64]{0:T(128)}, u32[]{:S(2)}) copy-start(s32[64]{0:T(128)} %constant.1078) | copy-start | bytes 772
  260.0 30.0 %copy-start.44 = (bf16[64,8,64]{2,1,0:T(8,128)(2,1)S(1)}, bf16[64,8,64]{2,1,0:T(8,128)(2,1)}, u32[]{:S(2)}) copy-start(bf16[64,8,64]{2,1,0:T(8,128)(2,1)} %copy.335) | copy-start | bytes 196612
  260.7 35.9 %copy-start.26 = (bf16[8,8,64]{2,1,0:T(8,128)(2,1)S(1)}, bf16[8,8,64]{2,1,0:T(8,128)(2,1)}, u32[]{:S(2)}) copy-start(bf16[8,8,64]{2,1,0:T(8,128)(2,1)} %copy.297) | copy-start | bytes 24580
  260.7 35.9 %copy-start.73 = (s32[8]{0:T(128)S(1)}, s32[8]{0:T(128)}, u32[]{:S(2)}) copy-start(s32[8]{0:T(128)} %constant.1079) | copy-start | bytes 100
  263.3 34.0 %copy-start.29 = (bf16[8,8,64]{2,1,0:T(8,128)(2,1)S(1)}, bf16[8,8,64]{2,1,0:T(8,128)(2,1)}, u32[]{:S(2)}) copy-start(bf16[8,8,64]{2,1,0:T(8,128)(2,1)} %copy.337) | copy-start | bytes 24580
  264.0 35.2 %copy-start.39 = (bf16[64,8,64]{2,1,0:T(8,128)(2,1)S(1)}, bf16[64,8,64]{2,1,0:T(8,128)(2,1)}, u32[]{:S(2)}) copy-start(bf16[64,8,64]{2,1,0:T(8,128)(2,1)} %copy.299) | copy-start | bytes 196612
  264.1 35.2 %copy-start.72 = (s32[64]{0:T(128)S(1)}, s32[64]{0:T(128)}, u32[]{:S(2)}) copy-start(s32[64]{0:T(128)} %constant.1080) | copy-start | bytes 772
  266.0 35.7 %copy-start.42 = (bf16[64,8,64]{2,1,0:T(8,128)(2,1)S(1)}, bf16[64,8,64]{2,1,0:T(8,128)(2,1)}, u32[]{:S(2)}) copy-start(bf16[64,8,64]{2,1,0:T(8,128)(2,1)} %copy.339) | copy-start | bytes 196612
  268.6 39.7 %copy-start.25 = (bf16[8,8,64]{2,1,0:T(8,128)(2,1)S(1)}, bf16[8,8,64]{2,1,0:T(8,128)(2,1)}, u32[]{:S(2)}) copy-start(bf16[8,8,64]{2,1,0:T(8,128)(2,1)} %copy.301) | copy-start | bytes 24580
  268.6 39.7 %copy-start.71 = (s32[8]{0:T(128)S(1)}, s32[8]{0:T(128)}, u32[]{:S(2)}) copy-start(s32[8]{0:T(128)} %constant.1081) | copy-start | bytes 100
  275.5 33.5 %copy-start.27 = (bf16[8,8,64]{2,1,0:T(8,128)(2,1)S(1)}, bf16[8,8,64]{2,1,0:T(8,128)(2,1)}, u32[]{:S(2)}) copy-start(bf16[8,8,64]{2,1,0:T(8,128)(2,1)} %copy.341) | copy-start | bytes 24580
  276.2 34.7 %copy-start.57 = (bf16[8,64]{1,0:T(8,128)(2,1)S(1)}, bf16[8,64]{1,0:T(8,128)(2,1)}, u32[]{:S(2)}) copy-start(bf16[8,64]{1,0:T(8,128)(2,1)} %gather_fusion.30) | copy-start | bytes 3076
  276.2 34.7 %copy-start.58 = (bf16[8,64]{1,0:T(8,128)(2,1)S(1)}, bf16[8,64]{1,0:T(8,128)(2,1)}, u32[]{:S(2)}) copy-start(bf16[8,64]{1,0:T(8,128)(2,1)} %gather_fusion.74) | copy-start | bytes 3076
  276.3 34.7 %copy-start.91 = (pred[8]{0:T(512)(128)(4,1)S(1)}, pred[8]{0:T(512)(128)(4,1)}, u32[]{:S(2)}) copy-start(pred[8]{0:T(512)(128)(4,1)} %get-tuple-element.339) | copy-start | bytes 28
  276.3 34.7 %copy-start.99 = (pred[8]{0:T(512)(128)(4,1)S(1)}, pred[8]{0:T(512)(128)(4,1)}, u32[]{:S(2)}) copy-start(pred[8]{0:T(512)(128)(4,1)} %get-tuple-element.515) | copy-start | bytes 28
  276.3 35.4 %copy-start.70 = (s32[8]{0:T(128)S(1)}, s32[8]{0:T(128)}, u32[]{:S(2)}) copy-start(s32[8]{0:T(128)} %constant.1082) | copy-start | bytes 100
  280.6 33.7 %copy-start.59 = (bf16[8,64]{1,0:T(8,128)(2,1)S(1)}, bf16[8,64]{1,0:T(8,128)(2,1)}, u32[]{:S(2)}) copy-start(bf16[8,64]{1,0:T(8,128)(2,1)} %gather_fusion.33) | copy-start | bytes 3076
  280.6 33.7 %copy-start.60 = (bf16[8,64]{1,0:T(8,128)(2,1)S(1)}, bf16[8,64]{1,0:T(8,128)(2,1)}, u32[]{:S(2)}) copy-start(bf16[8,64]{1,0:T(8,128)(2,1)} %gather_fusion.77) | copy-start | bytes 3076
  280.6 33.7 %copy-start.90 = (pred[8]{0:T(512)(128)(4,1)S(1)}, pred[8]{0:T(512)(128)(4,1)}, u32[]{:S(2)}) copy-start(pred[8]{0:T(512)(128)(4,1)} %get-tuple-element.337) | copy-start | bytes 28
  280.6 33.6 %copy-start.98 = (pred[8]{0:T(512)(128)(4,1)S(1)}, pred[8]{0:T(512)(128)(4,1)}, u32[]{:S(2)}) copy-start(pred[8]{0:T(512)(128)(4,1)} %get-tuple-element.513) | copy-start | bytes 28
  280.6 34.3 %copy-start.69 = (s32[8]{0:T(128)S(1)}, s32[8]{0:T(128)}, u32[]{:S(2)}) copy-start(s32[8]{0:T(128)} %constant.1083) | copy-start | bytes 100
  290.0 27.6 %copy-start.45 = (bf16[64,8,64]{2,1,0:T(8,128)(2,1)S(1)}, bf16[64,8,64]{2,1,0:T(8,128)(2,1)}, u32[]{:S(2)}) copy-start(bf16[64,8,64]{2,1,0:T(8,128)(2,1)} %copy.310) | copy-start | bytes 196612
  290.0 27.6 %copy-start.68 = (s32[64]{0:T(128)S(1)}, s32[64]{0:T(128)}, u32[]{:S(2)}) copy-start(s32[64]{0:T(128)} %constant.1084) | copy-start | bytes 772
  296.6 23.4 %copy-start.46 = (bf16[64,8,64]{2,1,0:T(8,128)(2,1)S(1)}, bf16[64,8,64]{2,1,0:T(8,128)(2,1)}, u32[]{:S(2)}) copy-start(bf16[64,8,64]{2,1,0:T(8,128)(2,1)} %copy.348) | copy-start | bytes 196612
  297.3 29.2 %copy-start.67 = (s32[8]{0:T(128)S(1)}, s32[8]{0:T(128)}, u32[]{:S(2)}) copy-start(s32[8]{0:T(128)} %constant.1085) | copy-start | bytes 100
  301.7 27.5 %copy-start.61 = (bf16[8,64]{1,0:T(8,128)(2,1)S(1)}, bf16[8,64]{1,0:T(8,128)(2,1)}, u32[]{:S(2)}) copy-start(bf16[8,64]{1,0:T(8,128)(2,1)} %gather_fusion.40) | copy-start | bytes 3076
  301.7 27.5 %copy-start.89 = (pred[8]{0:T(512)(128)(4,1)S(1)}, pred[8]{0:T(512)(128)(4,1)}, u32[]{:S(2)}) copy-start(pred[8]{0:T(512)(128)(4,1)} %get-tuple-element.333) | copy-start | bytes 28
  301.7 27.5 %copy-start.96 = (pred[8]{0:T(512)(128)(4,1)S(1)}, pred[8]{0:T(512)(128)(4,1)}, u32[]{:S(2)}) copy-start(pred[8]{0:T(512)(128)(4,1)} %get-tuple-element.509) | copy-start | bytes 28
  301.7 28.1 %copy-start.66 = (s32[8]{0:T(128)S(1)}, s32[8]{0:T(128)}, u32[]{:S(2)}) copy-start(s32[8]{0:T(128)} %constant.1086) | copy-start | bytes 100
  309.0 23.4 %copy-start.88 = (pred[8]{0:T(512)(128)(4,1)S(1)}, pred[8]{0:T(512)(128)(4,1)}, u32[]{:S(2)}) copy-start(pred[8]{0:T(512)(128)(4,1)} %get-tuple-element.331) | copy-start | bytes 28
  309.0 23.4 %copy-start.95 = (pred[8]{0:T(512)(128)(4,1)S(1)}, pred[8]{0:T(512)(128)(4,1)}, u32[]{:S(2)}) copy-start(pred[8]{0:T(512)(128)(4,1)} %get-tuple-element.507) | copy-start | bytes 28
  (60 other events, 702.7 us)
Sparse Core Ops, SparseCore 0:
  444.0 57.7 all-reduce.1
where the time goes:
time: 522 us; the launch traced here: 511 us
  local copies, waits for them, and re-layouts  326 us (62%)
  other arithmetic  68.5 us (13%)
  waiting for transfers between devices  50.6 us (10%)
  matrix products  42.5 us (8%)
  between operations  16.9 us (3%)
    scatter x36, local copies, waits for them, and re-layouts, padded_field(): padded.at[:, :, dest_index].set(take_rows(source, row_index, keep_rows))  87.1 us
    gather x52, local copies, waits for them, and re-layouts, take_rows(): jnp.take(source, jnp.clip(row_index, 0, source.shape[0] - 1), axis=0)  52.1 us
    psum x1, waiting for transfers between devices, shards(): summed_grad = lax.psum(grad_local.reshape(-1), 'dom')  50.6 us
    while x416, local copies, waits for them, and re-layouts  43.8 us
    scatter x2, local copies, waits for them, and re-layouts, padded_field(): padded = jnp.zeros((leaf_count, channels, padded_cells), center.dtype).at...  27.4 us
    dot_general x8, matrix products, block_terms(): jnp.einsum('lkv,lov->ko', stack_x, dy_block, preferred_element_type=jnp.f...  21.6 us
    select_n x36, local copies, waits for them, and re-layouts, take_rows(): jnp.where(keep_rows[:, None, None], picked, jnp.zeros((), source.dtype))  16.9 us
    gather x40, other arithmetic  15.1 us
  transfers between devices with their start and end apart: 3, of which 1 were waited for; matrix products, arithmetic and copies ran while one was open for 25% of the time, Pallas kernels for 0%

commit v1 on v0

v1 whole, which is shorter than its diff:
```python
import functools

import jax
import jax.numpy as jnp
from jax import lax
from jax.experimental import pallas as pl
from jax.experimental.pallas import tpu as pltpu
from jax.sharding import PartitionSpec as P

BITS = 30
EDGE = 8
FACE = EDGE * EDGE
TILE = 128
CH = 64
GROUP = 8
KROWS = 9 * CH
VMEM_LIMIT = 48 * 1024 * 1024
BF = jnp.bfloat16
F32 = jnp.float32


def column_of(p, q, r):
    tap = (p + 1) * 9 + (q + 1) * 3 + r + 1
    return tap if tap < 13 else tap - 1


SHIFTS = [(p, q) for p in (-1, 0, 1) for q in (-1, 0)] + [(p, 1) for p in (-1, 0, 1)]


def lane_ids(rows):
    return lax.broadcasted_iota(jnp.int32, (rows, TILE), 1)


def occupancy_tile(words, tile):
    lane = lane_ids(words.shape[0]) + tile * TILE
    first, last = (tile * TILE) // BITS, (tile * TILE + TILE - 1) // BITS
    word = jnp.broadcast_to(words[:, first : first + 1], lane.shape)
    place = lane - first * BITS
    for w in range(first + 1, last + 1):
        past = lane >= w * BITS
        word = jnp.where(past, jnp.broadcast_to(words[:, w : w + 1], lane.shape), word)
        place = jnp.where(past, lane - w * BITS, place)
    return (jnp.right_shift(word, place) & 1).astype(F32)


def spread(occ, leaf):
    return jnp.broadcast_to(occ[leaf : leaf + 1, :], (CH, TILE)).astype(BF)


def roll(value, amount):
    return pltpu.roll(value, amount % TILE, 1)


def edges_kernel(words_ref, x_lo, x_hi, d_lo, d_hi, up_ref, down_ref):
    words = words_ref[...]
    occ_lo = occupancy_tile(words, 0)
    occ_hi = occupancy_tile(words, 3)
    left = lane_ids(CH) < FACE
    for leaf in range(x_lo.shape[0]):
        low, high = spread(occ_lo, leaf), spread(occ_hi, leaf)
        up_ref[leaf] = jnp.where(left, roll(d_hi[leaf] * high, FACE), x_hi[leaf] * high)
        down_ref[leaf] = jnp.where(left, x_lo[leaf] * low, roll(d_lo[leaf] * low, FACE))


def edges(words, x, dy):
    leaves = x.shape[0]
    block = (leaves, CH, TILE)
    lo = pl.BlockSpec(block, lambda i: (0, 0, 0))
    hi = pl.BlockSpec(block, lambda i: (0, 0, 3))
    shape = jax.ShapeDtypeStruct(block, BF)
    return pl.pallas_call(
        edges_kernel,
        grid=(1,),
        out_shape=(shape, shape),
        in_specs=[pl.BlockSpec(words.shape, lambda i: (0, 0)), lo, hi, lo, hi],
        out_specs=(lo, lo),
        cost_estimate=pl.CostEstimate(flops=10**6, bytes_accessed=10**6, transcendentals=0),
        compiler_params=pltpu.CompilerParams(vmem_limit_bytes=VMEM_LIMIT),
        name="edges",
    )(words, x, x, dy, dy)


def fill(store, field_ref, occ, below_ref, above_ref, turned):
    leaves = field_ref.shape[0]
    for leaf in range(leaves):
        for k in range(4):
            at = slice(k * TILE, (k + 1) * TILE)
            store[leaf, :, at] = field_ref[leaf, :, at] * spread(occ[k], leaf)
    for leaf in range(leaves):
        low, high = above_ref[leaf], below_ref[leaf]
        store[leaves + leaf, :, 0:TILE] = roll(low, FACE) if turned else low
        store[leaves + leaf, :, 3 * TILE : 4 * TILE] = roll(high, FACE) if turned else high
    store[2 * leaves] = jnp.zeros(store.shape[1:], BF)


def stacked(store, near_ref, leaf, z, device, leaves):
    def place(p, q):
        if (p, q, z) == (0, 0, 0):
            return leaf
        ident = near_ref[leaf, column_of(p, q, z)]
        owner = ident // leaves
        slot = ident - owner * leaves
        slot = jnp.where(owner == device, slot, slot + leaves)
        return jnp.where(ident < 0, 2 * leaves, slot)

    lane = lane_ids(CH)
    left = lane < FACE
    row_b = (lane // EDGE) % EDGE
    first, last = row_b == 0, row_b == EDGE - 1
    tiles = {}
    for q in (-1, 0, 1):
        mid = place(0, q)
        tiles[q] = [store[mid, :, k * TILE : (k + 1) * TILE] for k in range(4)]
        after = store[place(1, q), :, 0:TILE]
        before = store[place(-1, q), :, 3 * TILE : 4 * TILE]
        tiles[q].append(jnp.where(left, after, before))
    moved = {
        -1: [
            jnp.where(first, roll(m, FACE + EDGE), roll(c, EDGE))
            for m, c in zip(tiles[-1], tiles[0])
        ],
        0: tiles[0],
        1: [
            jnp.where(last, roll(m, -FACE - EDGE), roll(c, -EDGE))
            for m, c in zip(tiles[1], tiles[0])
        ],
    }
    swapped = {q: [roll(t, FACE) for t in moved[q]] for q in (-1, 0, 1)}

    def piece(p, q):
        if p == 0:
            parts = moved[q][:4]
        elif p == 1:
            parts = [jnp.where(left, swapped[q][k], swapped[q][k + 1]) for k in range(4)]
        else:
            parts = [jnp.where(left, swapped[q][(k - 1) % 5], swapped[q][k]) for k in range(4)]
        return jnp.concatenate(parts, axis=1)

    return jnp.concatenate([piece(p, q) for p, q in SHIFTS], axis=0)


def c_index():
    return lane_ids(CH) % EDGE


def shift_c(value, r, fill_from=None):
    if r == 0:
        return value
    edge = c_index() == (EDGE - 1 if r > 0 else 0)
    zero = jnp.zeros((CH, TILE), value.dtype)
    parts = [
        jnp.where(edge, zero, roll(value[:, k * TILE : (k + 1) * TILE], -r)) for k in range(4)
    ]
    return jnp.concatenate(parts, axis=1)


def across_c(value, z):
    edge = c_index() == (EDGE - 1 if z > 0 else 0)
    zero = jnp.zeros((CH, TILE), value.dtype)
    parts = [
        jnp.where(edge, roll(value[:, k * TILE : (k + 1) * TILE], z * (EDGE - 1)), zero)
        for k in range(4)
    ]
    return jnp.concatenate(parts, axis=1)


def listed(near_ref, leaf, z):
    found = jnp.int32(-1)
    for p in (-1, 0, 1):
        for q in (-1, 0, 1):
            found = jnp.maximum(found, near_ref[leaf, column_of(p, q, z)])
    return found >= 0


def grad_kernel(
    near_ref, words_ref, x_ref, d_ref, below_ref, above_ref, keep_ref, send_ref, store, total, packed
):
    leaves = x_ref.shape[0]
    device = lax.axis_index("dom")
    words = words_ref[...]
    occ = [occupancy_tile(words, k) for k in range(4)]
    fill(store, d_ref, occ, below_ref, above_ref, True)

    def masked_x(leaf):
        return jnp.concatenate(
            [x_ref[leaf, :, k * TILE : (k + 1) * TILE] * spread(occ[k], leaf) for k in range(4)],
            axis=1,
        )

    contract = (((1,), (1,)), ((), ()))
    for leaf in range(leaves):
        near_dy = stacked(store, near_ref, leaf, 0, device, leaves)
        center = masked_x(leaf)
        wide = jnp.concatenate([shift_c(center, r) for r in (-1, 0, 1)], axis=0)
        term = lax.dot_general(wide, near_dy, contract, preferred_element_type=F32)
        if leaf == 0:
            total[...] = term
        else:
            total[...] += term

    for z in (-1, 1):
        for leaf in range(leaves):

            @pl.when(listed(near_ref, leaf, z))
            def _():
                near_dy = stacked(store, near_ref, leaf, z, device, leaves)
                edge = across_c(masked_x(leaf), -z)
                rows = pl.ds((-z + 1) * CH, CH)
                total[rows, :] += lax.dot_general(
                    edge, near_dy, contract, preferred_element_type=F32
                )

    for k in range(4):
        packed[k * 3 * CH : (k + 1) * 3 * CH, :] = total[:, k * TILE : (k + 1) * TILE]
    half = 3 * CH // 2
    packed[12 * CH : 12 * CH + half, 0:CH] = total[0:half, 4 * TILE :]
    packed[12 * CH : 12 * CH + half, CH:] = total[half:, 4 * TILE :]
    packed[12 * CH + half :, :] = jnp.zeros((packed.shape[0] - 12 * CH - half, TILE), F32)
    core = lax.rem(device, 2)
    rows = packed.shape[0] // 2
    keep_ref[...] = packed[pl.ds(pl.multiple_of(core * rows, 8), rows), :]
    send_ref[...] = packed[pl.ds(pl.multiple_of((1 - core) * rows, 8), rows), :]


def grad_terms(near, words, x, dy, below, above):
    leaves = x.shape[0]
    rows = 14 * CH
    vmem = pl.BlockSpec(memory_space=pltpu.VMEM)
    smem = pl.BlockSpec(memory_space=pltpu.SMEM)
    shape = jax.ShapeDtypeStruct((rows // 2, TILE), F32)
    return pl.pallas_call(
        grad_kernel,
        out_shape=(shape, shape),
        in_specs=[smem, vmem, vmem, vmem, vmem, vmem],
        out_specs=(vmem, vmem),
        scratch_shapes=[
            pltpu.VMEM((2 * leaves + 1, CH, 4 * TILE), BF),
            pltpu.VMEM((3 * CH, KROWS), F32),
            pltpu.VMEM((rows, TILE), F32),
        ],
        cost_estimate=pl.CostEstimate(flops=10**9, bytes_accessed=2 * 10**6, transcendentals=0),
        compiler_params=pltpu.CompilerParams(vmem_limit_bytes=VMEM_LIMIT),
        name="grad_terms",
    )(near, words, x, dy, below, above)


def conv_kernel(turned, near_ref, words_ref, x_ref, below_ref, above_ref, w_ref, out_ref, store):
    leaves = x_ref.shape[0]
    device = lax.axis_index("dom")
    words = words_ref[...]
    occ = [occupancy_tile(words, k) for k in range(4)]
    fill(store, x_ref, occ, below_ref, above_ref, turned)
    taps = w_ref[...]

    def masked(leaf, value):
        return jnp.concatenate(
            [
                value[:, k * TILE : (k + 1) * TILE]
                * jnp.broadcast_to(occ[k][leaf : leaf + 1, :], (CH, TILE))
                for k in range(4)
            ],
            axis=1,
        )

    for leaf in range(leaves):
        near_x = stacked(store, near_ref, leaf, 0, device, leaves)
        wide = jnp.dot(taps, near_x, preferred_element_type=F32)
        total = wide[CH : 2 * CH]
        for r in (-1, 1):
            total = total + shift_c(wide[(r + 1) * CH : (r + 2) * CH], r)
        out_ref[leaf] = masked(leaf, total).astype(BF)

    for leaf in range(leaves):

        @pl.when(listed(near_ref, leaf, -1) | listed(near_ref, leaf, 1))
        def _():
            near_x = stacked(store, near_ref, leaf, 0, device, leaves)
            wide = jnp.dot(taps, near_x, preferred_element_type=F32)
            total = wide[CH : 2 * CH]
            for r in (-1, 1):
                total = total + shift_c(wide[(r + 1) * CH : (r + 2) * CH], r)
            for z in (-1, 1):
                near_z = stacked(store, near_ref, leaf, z, device, leaves)
                part = jnp.dot(
                    taps[(z + 1) * CH : (z + 2) * CH], near_z, preferred_element_type=F32
                )
                total = total + across_c(part, z)
            out_ref[leaf] = masked(leaf, total).astype(BF)


def conv(near, words, x, below, above, taps, turned):
    leaves = x.shape[0]
    vmem = pl.BlockSpec(memory_space=pltpu.VMEM)
    smem = pl.BlockSpec(memory_space=pltpu.SMEM)
    return pl.pallas_call(
        functools.partial(conv_kernel, turned),
        out_shape=jax.ShapeDtypeStruct(x.shape, BF),
        in_specs=[smem, vmem, vmem, vmem, vmem, vmem],
        out_specs=vmem,
        scratch_shapes=[pltpu.VMEM((2 * leaves + 1, CH, 4 * TILE), BF)],
        cost_estimate=pl.CostEstimate(flops=2 * 10**9, bytes_accessed=2 * 10**6, transcendentals=0),
        compiler_params=pltpu.CompilerParams(vmem_limit_bytes=VMEM_LIMIT),
        name="in_grad_conv" if turned else "out_conv",
    )(near, words, x, below, above, taps)


def unpack_kernel(scale, halves_ref, out_ref):
    core = lax.rem(lax.axis_index("dom"), 2)
    own, other = halves_ref[0], halves_ref[1]
    first = jnp.where(core == 0, own, other)
    second = jnp.where(core == 0, other, own)
    total = jnp.concatenate([first, second], axis=0) * scale
    for index, (p, q) in enumerate(SHIFTS):
        for r in (-1, 0, 1):
            tap = (-p + 1) * 9 + (-q + 1) * 3 + r + 1
            if index < 8:
                row = (index // 2) * 3 * CH + (r + 1) * CH
                side = index % 2
                out_ref[tap] = total[row : row + CH, side * CH : (side + 1) * CH]
            else:
                base, half = 12 * CH, 3 * CH // 2
                start = (r + 1) * CH
                parts = []
                for begin in range(start, start + CH, CH // 2):
                    side, row = begin // half, base + begin % half
                    parts.append(total[row : row + CH // 2, side * CH : (side + 1) * CH])
                out_ref[tap] = jnp.concatenate(parts, axis=0)


def unpack(halves, scale):
    vmem = pl.BlockSpec(memory_space=pltpu.VMEM)
    return pl.pallas_call(
        functools.partial(unpack_kernel, scale),
        out_shape=jax.ShapeDtypeStruct((27, CH, CH), F32),
        in_specs=[vmem],
        out_specs=vmem,
        cost_estimate=pl.CostEstimate(flops=10**6, bytes_accessed=10**6, transcendentals=0),
        compiler_params=pltpu.CompilerParams(vmem_limit_bytes=VMEM_LIMIT),
        name="unpack_grad",
    )(halves)


def exchange(array, mask, size):
    return lax.ppermute(array, "dom", [(i, i ^ mask) for i in range(size)])


def shards(features, cotangent, weight, mask_words, neighbors):
    leaves, channels, voxels = features.shape
    size = lax.axis_size("dom")
    device = lax.axis_index("dom")
    up = [(i, i + 1) for i in range(size - 1)]
    down = [(i + 1, i) for i in range(size - 1)]
    to_above, to_below = edges(mask_words, features, cotangent)
    below = lax.ppermute(to_above, "dom", up)
    above = lax.ppermute(to_below, "dom", down)

    cube = weight.reshape(3, 3, 3, channels, channels)
    order = lambda c: jnp.concatenate([c[:, :2].reshape(6, *c.shape[2:]), c[:, 2]], axis=0)
    taps_out = order(cube).transpose(1, 3, 0, 2).reshape(3 * channels, KROWS)
    taps_back = order(cube[::-1, ::-1, ::-1]).transpose(1, 2, 0, 3).reshape(3 * channels, KROWS)

    keep, send = grad_terms(neighbors, mask_words, features, cotangent, below, above)
    keep = keep + exchange(send, 1, size)
    rows = keep.shape[0] // 4
    lane = (device // 2) % 4
    chunk = lambda index: lax.dynamic_slice_in_dim(keep, index * rows, rows, axis=0)
    got = [exchange(chunk(lane ^ m), 2 * m, size) for m in (1, 2, 3)]
    out_features = conv(neighbors, mask_words, features, below, above, taps_out, False)
    own = chunk(lane) + got[0] + got[1] + got[2]
    if size > GROUP:
        groups = [[j * GROUP + i for j in range(size // GROUP)] for i in range(GROUP)]
        own = lax.psum(own, "dom", axis_index_groups=groups)
    back = [exchange(own, 2 * m, size) for m in (1, 2, 3)]
    in_grad = conv(neighbors, mask_words, cotangent, below, above, taps_back, True)
    half = jnp.zeros((4, rows, TILE), F32)
    for m, part in zip((0, 1, 2, 3), [own] + back):
        half = lax.dynamic_update_slice_in_dim(half, part[None], lane ^ m, axis=0)
    half = half.reshape(4 * rows, TILE)
    other = exchange(half, 1, size)
    scale = float(size * leaves * voxels) ** -0.5
    weight_grad = unpack(jnp.stack([half, other]), scale)
    return (out_features, in_grad, weight_grad)


def solution(mesh):
    split = P(("scene", "dom"), None, None)
    flat = P(("scene", "dom"), None)
    return jax.shard_map(
        shards,
        mesh=mesh,
        in_specs=(split, split, P(), flat, flat),
        out_specs=(split, split, P("scene", None, None)),
        check_vma=False,
    )
```

time: 522 us -> 52.2 us (0.10); the launches traced: 511 us -> 51.9 us
  local copies, waits for them, and re-layouts: 326 us -> 4.79 us
  other arithmetic: 68.5 us -> 0.27 us
  matrix products: 42.5 us -> 0 us
  waiting for transfers between devices: 50.6 us -> 14 us
  between operations: 16.9 us -> 0.94 us
  Pallas kernels: 0 us -> 15.6 us
  starting transfers between devices: 5.13 us -> 16.3 us
    scatter x39 -> x0, local copies, waits for them, and re-layouts: 128 us -> none  [the longest x36 87.1 us: padded_field(): padded.at[:, :, dest_index].set(take_rows(source, row_index, keep_rows))]
    gather x110 -> x0, local copies, waits for them, and re-layouts: 92.4 us -> none  [the longest x52 52.1 us: take_rows(): jnp.take(source, jnp.clip(row_index, 0, source.shape[0] - 1), axis=0)]
    while x421 -> x0, local copies, waits for them, and re-layouts: 57.3 us -> none
    psum x1 -> x0, waiting for transfers between devices: 50.6 us -> none  [shards(): summed_grad = lax.psum(grad_local.reshape(-1), 'dom')]
    dot_general x24 -> x0, matrix products: 42.5 us -> none  [the longest x8 21.6 us: block_terms(): jnp.einsum('lkv,lov->ko', stack_x, dy_block, preferred_element_type=jnp.f...]
    select_n x52 -> x0, local copies, waits for them, and re-layouts: 21.7 us -> none  [the longest x36 16.9 us: take_rows(): jnp.where(keep_rows[:, None, None], picked, jnp.zeros((), source.dtype))]
    select_n x38 -> x0, other arithmetic: 18.2 us -> none  [the longest x18 10.6 us: take_rows(): jnp.where(keep_rows[:, None, None], picked, jnp.zeros((), source.dtype))]
    pallas_call x0 -> x5, Pallas kernels: none -> 15.6 us  [the longest x2 9.76 us: conv(): pl.pallas_call(functools.partial(conv_kernel, turned), out_shape=jax.Shap...]
  transfers between devices with their start and end apart: 3 -> 10, of which waited for: 1 -> 6; matrix products, arithmetic and copies ran while one was open for 25% -> 4% of each run, Pallas kernels for 0% -> 19%
where the time goes in v1:
time: 52.2 us; the launch traced here: 51.9 us
  starting transfers between devices  16.3 us (31%)
  Pallas kernels  15.6 us (30%)
  waiting for transfers between devices  14 us (27%)
  local copies, waits for them, and re-layouts  4.79 us (9%)
  between operations  0.94 us (2%)
    ppermute x8, starting transfers between devices, exchange(): return lax.ppermute(array, 'dom', [(i, i ^ mask) for i in range(size)])  12.6 us
    ppermute x8, waiting for transfers between devices, exchange(): return lax.ppermute(array, 'dom', [(i, i ^ mask) for i in range(size)])  9.99 us
    pallas_call x2, Pallas kernels, conv(): pl.pallas_call(functools.partial(conv_kernel, turned), out_shape=jax.Shap...  9.76 us
    pallas_call x1, Pallas kernels, grad_terms(): pl.pallas_call(grad_kernel, out_shape=(shape, shape), in_specs=[smem, vme...  4.51 us
    ppermute x1, waiting for transfers between devices, shards(): above = lax.ppermute(to_below, 'dom', down)  3.99 us
    unnamed x16, local copies, waits for them, and re-layouts  2.79 us
    ppermute x1, starting transfers between devices, shards(): below = lax.ppermute(to_above, 'dom', up)  2.36 us
    ppermute x1, starting transfers between devices, shards(): above = lax.ppermute(to_below, 'dom', down)  1.29 us
  transfers between devices with their start and end apart: 10, of which 6 were waited for; matrix products, arithmetic and copies ran while one was open for 4% of the time, Pallas kernels for 19%

profile of v1, /device:TPU:0, one launch (start us, length us, event | category | flops | bytes accessed | tf_op | source)
XLA Modules:
  0.0 51.9 jit_solution(12817634318813302231)
XLA Ops:
  0.6 0.0 copy-start
  0.6 1.0 %copy-done = bf16[8,64,512]{2,1,0:T(8,128)(2,1)S(1)} copy-done((bf16[8,64,512]{2,1,0:T(8,128)(2,1)S(1)}, bf16[8,64,512]{2,1,0:T(8,128)(2,1)}, u32[]{:S(2)}) %copy-start) | copy-done | bytes 524312
  1.7 0.0 copy-start.2
  1.7 1.0 %copy-done.2 = bf16[8,64,512]{2,1,0:T(8,128)(2,1)S(1)} copy-done((bf16[8,64,512]{2,1,0:T(8,128)(2,1)S(1)}, bf16[8,64,512]{2,1,0:T(8,128)(2,1)}, u32[]{:S(2)}) %copy-start.2) | copy-done | bytes 524312
  2.7 0.0 copy-start.4
  2.7 0.7 %copy-done.4 = s32[8,18]{1,0:T(8,128)S(1)} copy-done((s32[8,18]{1,0:T(8,128)S(1)}, s32[8,18]{1,0:T(8,128)}, u32[]{:S(2)}) %copy-start.4) | copy-done | bytes 600
  3.4 0.0 copy-start.7
  3.4 0.2 edges.1
  3.6 2.4 %collective-permute-start = (bf16[8,64,128]{2,1,0:T(8,128)(2,1)S(1)}, bf16[8,64,128]{2,1,0:T(8,128)(2,1)S(1)}, u32[]{:S(2)}, u32[]{:S(2)}) collective-permute-start(bf16[8,64,128]{2,1,0:T(8,128)(2,1)S(1)} %get-tuple-element.7), channel_id=1, source_target_pairs={{0,1},{1,2},{2,3},{3,4},{4,5},{5,6},{6,7},{8,9},{9,10},{10,11},{11... | collective-permute-start | bytes 393224 | tf_op jit(solution)/shard_map/ppermute | solution.py:354
  6.0 1.3 %collective-permute-start.1 = (bf16[8,64,128]{2,1,0:T(8,128)(2,1)S(1)}, bf16[8,64,128]{2,1,0:T(8,128)(2,1)S(1)}, u32[]{:S(2)}, u32[]{:S(2)}) collective-permute-start(bf16[8,64,128]{2,1,0:T(8,128)(2,1)S(1)} %get-tuple-element.8), channel_id=1, source_target_pairs={{1,0},{2,1},{3,2},{4,3},{5,4},{6,5},{7,6},{9,8},{10,9},{11,10},{12... | collective-permute-start | bytes 393224 | tf_op jit(solution)/shard_map/ppermute | solution.py:355
  7.3 0.0 copy-done.7
  7.3 0.0 copy-start.6
  7.3 0.1 fusion
  7.4 0.0 collective-permute-done.below_ref
  7.4 4.0 %collective-permute-done.1.above_ref = bf16[8,64,128]{2,1,0:T(8,128)(2,1)S(1)} collective-permute-done((bf16[8,64,128]{2,1,0:T(8,128)(2,1)S(1)}, bf16[8,64,128]{2,1,0:T(8,128)(2,1)S(1)}, u32[]{:S(2)}, u32[]{:S(2)}) %collective-permute-start.1) | collective-permute-done | bytes 131104 | tf_op jit(solution)/shard_map/ppermute | solution.py:355
  11.4 0.0 copy-done.6
  11.4 4.5 %grad_terms.1 = (f32[448,128]{1,0:T(8,128)S(1)}, f32[448,128]{1,0:T(8,128)S(1)}) custom-call(s32[8,26]{1,0:T(8,128)S(1)} %copy-done.6, s32[8,18]{1,0:T(8,128)S(1)} %copy-done.4, bf16[8,64,512]{2,1,0:T(8,128)(2,1)S(1)} %copy-done, bf16[8,64,512]{2,1,0:T(8,128)(2,1)S(1)} %copy-done.2, bf16[8,64,128]{2,1,0:T(8,128)(2,1)S(1)} %collective-permute-done.below_ref, ...), custom_call_target="tpu_custom_call" | custom-call | flops 1000000000 | bytes 2000000 | tf_op jit(solution)/shard_map/grad_terms/pallas_call | solution.py:231
  15.9 3.6 %collective-permute-start.2 = (f32[448,128]{1,0:T(8,128)S(1)}, f32[448,128]{1,0:T(8,128)S(1)}, u32[]{:S(2)}, u32[]{:S(2)}) collective-permute-start(f32[448,128]{1,0:T(8,128)S(1)} %get-tuple-element.10), channel_id=1, source_target_pairs={{0,1},{1,0},{2,3},{3,2},{4,5},{5,4},{6,7},{7,6},{8,9},{9,8},{10,11... | collective-permute-start | bytes 688136 | tf_op jit(solution)/shard_map/ppermute | solution.py:344
  19.6 0.1 maximum_bitcast_fusion
  19.7 0.9 %collective-permute-done.2 = f32[448,128]{1,0:T(8,128)S(1)} collective-permute-done((f32[448,128]{1,0:T(8,128)S(1)}, f32[448,128]{1,0:T(8,128)S(1)}, u32[]{:S(2)}, u32[]{:S(2)}) %collective-permute-start.2) | collective-permute-done | bytes 229408 | tf_op jit(solution)/shard_map/ppermute | solution.py:344
  20.7 2.2 %collective-permute-start.5 = (f32[112,128]{1,0:T(8,128)S(1)}, f32[112,128]{1,0:T(8,128)S(1)}, u32[]{:S(2)}, u32[]{:S(2)}) collective-permute-start(f32[112,128]{1,0:T(8,128)S(1)} %get-tuple-element.18), channel_id=1, source_target_pairs={{0,6},{1,7},{2,4},{3,5},{4,2},{5,3},{6,0},{7,1},{8,14},{9,15},{10,... | collective-permute-start | bytes 172040 | tf_op jit(solution)/shard_map/ppermute | solution.py:344
  23.0 0.9 %collective-permute-start.4 = (f32[112,128]{1,0:T(8,128)S(1)}, f32[112,128]{1,0:T(8,128)S(1)}, u32[]{:S(2)}, u32[]{:S(2)}) collective-permute-start(f32[112,128]{1,0:T(8,128)S(1)} %get-tuple-element.19), channel_id=1, source_target_pairs={{0,4},{1,5},{2,6},{3,7},{4,0},{5,1},{6,2},{7,3},{8,12},{9,13},{10,... | collective-permute-start | bytes 172040 | tf_op jit(solution)/shard_map/ppermute | solution.py:344
  23.9 1.3 %collective-permute-start.3 = (f32[112,128]{1,0:T(8,128)S(1)}, f32[112,128]{1,0:T(8,128)S(1)}, u32[]{:S(2)}, u32[]{:S(2)}) collective-permute-start(f32[112,128]{1,0:T(8,128)S(1)} %get-tuple-element.17), channel_id=1, source_target_pairs={{0,2},{1,3},{2,0},{3,1},{4,6},{5,7},{6,4},{7,5},{8,10},{9,11},{10,... | collective-permute-start | bytes 172040 | tf_op jit(solution)/shard_map/ppermute | solution.py:344
  25.3 1.7 %collective-permute-done.5 = f32[112,128]{1,0:T(8,128)S(1)} collective-permute-done((f32[112,128]{1,0:T(8,128)S(1)}, f32[112,128]{1,0:T(8,128)S(1)}, u32[]{:S(2)}, u32[]{:S(2)}) %collective-permute-start.5) | collective-permute-done | bytes 57376 | tf_op jit(solution)/shard_map/ppermute | solution.py:344
  27.0 2.7 %collective-permute-done.4 = f32[112,128]{1,0:T(8,128)S(1)} collective-permute-done((f32[112,128]{1,0:T(8,128)S(1)}, f32[112,128]{1,0:T(8,128)S(1)}, u32[]{:S(2)}, u32[]{:S(2)}) %collective-permute-start.4) | collective-permute-done | bytes 57376 | tf_op jit(solution)/shard_map/ppermute | solution.py:344
  29.7 0.0 collective-permute-done.3
  29.8 0.1 collective-permute-start.6
  29.8 0.1 maximum_bitcast_fusion.1
  29.9 0.6 %copy.22 = bf16[3,64,9,64]{3,2,1,0:T(8,128)(2,1)S(1)} copy(bf16[3,64,9,64]{1,3,0,2:T(8,128)(2,1)S(1)} %maximum_bitcast_fusion) | data formatting | bytes 442368 | tf_op jit(solution)/shard_map/reshape | solution.py:359
  30.6 0.4 reshape.30.w_ref
  31.0 0.3 copy.23
  31.3 0.0 copy-start.1
  31.3 0.4 reshape.31.w_ref
  31.8 3.1 %collective-permute-start.7 = (f32[112,128]{1,0:T(8,128)S(1)}, f32[112,128]{1,0:T(8,128)S(1)}, u32[]{:S(2)}, u32[]{:S(2)}) collective-permute-start(f32[112,128]{1,0:T(8,128)S(1)} %get-tuple-element.12), channel_id=1, source_target_pairs={{0,4},{1,5},{2,6},{3,7},{4,0},{5,1},{6,2},{7,3},{8,12},{9,13},{10,... | collective-permute-start | bytes 172040 | tf_op jit(solution)/shard_map/ppermute | solution.py:344
  34.9 1.3 %collective-permute-start.8 = (f32[112,128]{1,0:T(8,128)S(1)}, f32[112,128]{1,0:T(8,128)S(1)}, u32[]{:S(2)}, u32[]{:S(2)}) collective-permute-start(f32[112,128]{1,0:T(8,128)S(1)} %get-tuple-element.12), channel_id=1, source_target_pairs={{0,6},{1,7},{2,4},{3,5},{4,2},{5,3},{6,0},{7,1},{8,14},{9,15},{10,... | collective-permute-start | bytes 172040 | tf_op jit(solution)/shard_map/ppermute | solution.py:344
  36.2 0.0 collective-permute-done.6
  36.2 3.1 %collective-permute-done.7 = f32[112,128]{1,0:T(8,128)S(1)} collective-permute-done((f32[112,128]{1,0:T(8,128)S(1)}, f32[112,128]{1,0:T(8,128)S(1)}, u32[]{:S(2)}, u32[]{:S(2)}) %collective-permute-start.7) | collective-permute-done | bytes 57376 | tf_op jit(solution)/shard_map/ppermute | solution.py:344
  39.4 0.0 copy-start.5
  39.4 1.5 %collective-permute-done.8 = f32[112,128]{1,0:T(8,128)S(1)} collective-permute-done((f32[112,128]{1,0:T(8,128)S(1)}, f32[112,128]{1,0:T(8,128)S(1)}, u32[]{:S(2)}, u32[]{:S(2)}) %collective-permute-start.8) | collective-permute-done | bytes 57376 | tf_op jit(solution)/shard_map/ppermute | solution.py:344
  40.9 0.0 copy-start.3
  40.9 0.1 collective-permute-start.9
  41.0 0.0 copy-done.1
  41.0 0.0 copy-done.5
  41.0 4.7 %out_conv.1 = bf16[8,64,512]{2,1,0:T(8,128)(2,1)} custom-call(s32[8,26]{1,0:T(8,128)S(1)} %copy-done.6, s32[8,18]{1,0:T(8,128)S(1)} %copy-done.5, bf16[8,64,512]{2,1,0:T(8,128)(2,1)S(1)} %copy-done.1, bf16[8,64,128]{2,1,0:T(8,128)(2,1)S(1)} %collective-permute-done.below_ref, bf16[8,64,128]{2,1,0:T(8,128)(2,1)S(1)} %collective-permute-done.1.above_ref, ...), custom_call_target="tpu_custom_call" | custom-call | flops 2000000000 | bytes 2000000 | tf_op jit(solution)/shard_map/out_conv/pallas_call | solution.py:295
  45.7 0.0 copy-done.3
  45.7 5.0 %in_grad_conv.1 = bf16[8,64,512]{2,1,0:T(8,128)(2,1)} custom-call(s32[8,26]{1,0:T(8,128)S(1)} %copy-done.6, s32[8,18]{1,0:T(8,128)S(1)} %copy-done.5, bf16[8,64,512]{2,1,0:T(8,128)(2,1)S(1)} %copy-done.3, bf16[8,64,128]{2,1,0:T(8,128)(2,1)S(1)} %collective-permute-done.below_ref, bf16[8,64,128]{2,1,0:T(8,128)(2,1)S(1)} %collective-permute-done.1.above_ref, ...), custom_call_target="tpu_custom_call" | custom-call | flops 2000000000 | bytes 2000000 | tf_op jit(solution)/shard_map/in_grad_conv/pallas_call | solution.py:295
  50.8 0.0 collective-permute-done.9
  50.8 1.1 %unpack_grad.1 = f32[27,64,64]{2,1,0:T(8,128)} custom-call(f32[2,448,128]{2,1,0:T(8,128)S(1)} %pad_maximum_fusion.halves_ref), custom_call_target="tpu_custom_call" | custom-call | flops 1000000 | bytes 1000000 | tf_op jit(solution)/shard_map/unpack_grad/pallas_call | solution.py:332
  (11 shorter events, 0.2 us)
Async XLA Ops:
  0.6 1.0 %copy-start = (bf16[8,64,512]{2,1,0:T(8,128)(2,1)S(1)}, bf16[8,64,512]{2,1,0:T(8,128)(2,1)}, u32[]{:S(2)}) copy-start(bf16[8,64,512]{2,1,0:T(8,128)(2,1)} %x_ref.5) | copy-start | bytes 1572868
  1.7 1.0 %copy-start.2 = (bf16[8,64,512]{2,1,0:T(8,128)(2,1)S(1)}, bf16[8,64,512]{2,1,0:T(8,128)(2,1)}, u32[]{:S(2)}) copy-start(bf16[8,64,512]{2,1,0:T(8,128)(2,1)} %d_ref.1) | copy-start | bytes 1572868
  2.7 0.7 %copy-start.4 = (s32[8,18]{1,0:T(8,128)S(1)}, s32[8,18]{1,0:T(8,128)}, u32[]{:S(2)}) copy-start(s32[8,18]{1,0:T(8,128)} %words_ref.7) | copy-start | bytes 1732
  3.4 3.9 %copy-start.7 = (bf16[27,64,64]{2,1,0:T(8,128)(2,1)S(1)}, bf16[27,64,64]{2,1,0:T(8,128)(2,1)}, u32[]{:S(2)}) copy-start(bf16[27,64,64]{2,1,0:T(8,128)(2,1)} %param.7) | copy-start | bytes 663556
  3.6 3.8 %collective-permute-start = (bf16[8,64,128]{2,1,0:T(8,128)(2,1)S(1)}, bf16[8,64,128]{2,1,0:T(8,128)(2,1)S(1)}, u32[]{:S(2)}, u32[]{:S(2)}) collective-permute-start(bf16[8,64,128]{2,1,0:T(8,128)(2,1)S(1)} %get-tuple-element.7), channel_id=1, source_target_pairs={{0,1},{1,2},{2,3},{3,4},{4,5},{5,6},{6,7},{8,9},{9,10},{10,11},{11... | collective-permute-start | bytes 393224 | tf_op jit(solution)/shard_map/ppermute | solution.py:354
  6.0 5.4 %collective-permute-start.1 = (bf16[8,64,128]{2,1,0:T(8,128)(2,1)S(1)}, bf16[8,64,128]{2,1,0:T(8,128)(2,1)S(1)}, u32[]{:S(2)}, u32[]{:S(2)}) collective-permute-start(bf16[8,64,128]{2,1,0:T(8,128)(2,1)S(1)} %get-tuple-element.8), channel_id=1, source_target_pairs={{1,0},{2,1},{3,2},{4,3},{5,4},{6,5},{7,6},{9,8},{10,9},{11,10},{12... | collective-permute-start | bytes 393224 | tf_op jit(solution)/shard_map/ppermute | solution.py:355
  7.3 4.1 %copy-start.6 = (s32[8,26]{1,0:T(8,128)S(1)}, s32[8,26]{1,0:T(8,128)}, u32[]{:S(2)}) copy-start(s32[8,26]{1,0:T(8,128)} %near_ref.5) | copy-start | bytes 2500
  15.9 4.7 %collective-permute-start.2 = (f32[448,128]{1,0:T(8,128)S(1)}, f32[448,128]{1,0:T(8,128)S(1)}, u32[]{:S(2)}, u32[]{:S(2)}) collective-permute-start(f32[448,128]{1,0:T(8,128)S(1)} %get-tuple-element.10), channel_id=1, source_target_pairs={{0,1},{1,0},{2,3},{3,2},{4,5},{5,4},{6,7},{7,6},{8,9},{9,8},{10,11... | collective-permute-start | bytes 688136 | tf_op jit(solution)/shard_map/ppermute | solution.py:344
  20.7 6.2 %collective-permute-start.5 = (f32[112,128]{1,0:T(8,128)S(1)}, f32[112,128]{1,0:T(8,128)S(1)}, u32[]{:S(2)}, u32[]{:S(2)}) collective-permute-start(f32[112,128]{1,0:T(8,128)S(1)} %get-tuple-element.18), channel_id=1, source_target_pairs={{0,6},{1,7},{2,4},{3,5},{4,2},{5,3},{6,0},{7,1},{8,14},{9,15},{10,... | collective-permute-start | bytes 172040 | tf_op jit(solution)/shard_map/ppermute | solution.py:344
  23.0 6.7 %collective-permute-start.4 = (f32[112,128]{1,0:T(8,128)S(1)}, f32[112,128]{1,0:T(8,128)S(1)}, u32[]{:S(2)}, u32[]{:S(2)}) collective-permute-start(f32[112,128]{1,0:T(8,128)S(1)} %get-tuple-element.19), channel_id=1, source_target_pairs={{0,4},{1,5},{2,6},{3,7},{4,0},{5,1},{6,2},{7,3},{8,12},{9,13},{10,... | collective-permute-start | bytes 172040 | tf_op jit(solution)/shard_map/ppermute | solution.py:344
  23.9 5.8 %collective-permute-start.3 = (f32[112,128]{1,0:T(8,128)S(1)}, f32[112,128]{1,0:T(8,128)S(1)}, u32[]{:S(2)}, u32[]{:S(2)}) collective-permute-start(f32[112,128]{1,0:T(8,128)S(1)} %get-tuple-element.17), channel_id=1, source_target_pairs={{0,2},{1,3},{2,0},{3,1},{4,6},{5,7},{6,4},{7,5},{8,10},{9,11},{10,... | collective-permute-start | bytes 172040 | tf_op jit(solution)/shard_map/ppermute | solution.py:344
  29.8 6.5 %collective-permute-start.6 = (f32[112,128]{1,0:T(8,128)S(1)}, f32[112,128]{1,0:T(8,128)S(1)}, u32[]{:S(2)}, u32[]{:S(2)}) collective-permute-start(f32[112,128]{1,0:T(8,128)S(1)} %get-tuple-element.12), channel_id=1, source_target_pairs={{0,2},{1,3},{2,0},{3,1},{4,6},{5,7},{6,4},{7,5},{8,10},{9,11},{10,... | collective-permute-start | bytes 172040 | tf_op jit(solution)/shard_map/ppermute | solution.py:344
  31.3 9.6 %copy-start.1 = (bf16[8,64,512]{2,1,0:T(8,128)(2,1)S(1)}, bf16[8,64,512]{2,1,0:T(8,128)(2,1)}, u32[]{:S(2)}) copy-start(bf16[8,64,512]{2,1,0:T(8,128)(2,1)} %x_ref.5) | copy-start | bytes 1572868
  31.8 7.6 %collective-permute-start.7 = (f32[112,128]{1,0:T(8,128)S(1)}, f32[112,128]{1,0:T(8,128)S(1)}, u32[]{:S(2)}, u32[]{:S(2)}) collective-permute-start(f32[112,128]{1,0:T(8,128)S(1)} %get-tuple-element.12), channel_id=1, source_target_pairs={{0,4},{1,5},{2,6},{3,7},{4,0},{5,1},{6,2},{7,3},{8,12},{9,13},{10,... | collective-permute-start | bytes 172040 | tf_op jit(solution)/shard_map/ppermute | solution.py:344
  34.9 6.0 %collective-permute-start.8 = (f32[112,128]{1,0:T(8,128)S(1)}, f32[112,128]{1,0:T(8,128)S(1)}, u32[]{:S(2)}, u32[]{:S(2)}) collective-permute-start(f32[112,128]{1,0:T(8,128)S(1)} %get-tuple-element.12), channel_id=1, source_target_pairs={{0,6},{1,7},{2,4},{3,5},{4,2},{5,3},{6,0},{7,1},{8,14},{9,15},{10,... | collective-permute-start | bytes 172040 | tf_op jit(solution)/shard_map/ppermute | solution.py:344
  39.4 1.6 %copy-start.5 = (s32[8,18]{1,0:T(8,128)S(1)}, s32[8,18]{1,0:T(8,128)}, u32[]{:S(2)}) copy-start(s32[8,18]{1,0:T(8,128)} %words_ref.7) | copy-start | bytes 1732
  40.9 4.9 %copy-start.3 = (bf16[8,64,512]{2,1,0:T(8,128)(2,1)S(1)}, bf16[8,64,512]{2,1,0:T(8,128)(2,1)}, u32[]{:S(2)}) copy-start(bf16[8,64,512]{2,1,0:T(8,128)(2,1)} %d_ref.1) | copy-start | bytes 1572868
  40.9 9.9 %collective-permute-start.9 = (f32[448,128]{1,0:T(8,128)S(1)}, f32[448,128]{1,0:T(8,128)S(1)}, u32[]{:S(2)}, u32[]{:S(2)}) collective-permute-start(f32[448,128]{1,0:T(8,128)S(1)} %bitcast.26), channel_id=1, source_target_pairs={{0,1},{1,0},{2,3},{3,2},{4,5},{5,4},{6,7},{7,6},{8,9},{9,8},{10,11... | collective-permute-start | bytes 688136 | tf_op jit(solution)/shard_map/ppermute | solution.py:344

commit v2 on v1

v2 whole, which is shorter than its diff:
```python
import functools

import jax
import jax.numpy as jnp
from jax import lax
from jax.experimental import pallas as pl
from jax.experimental.pallas import tpu as pltpu
from jax.sharding import PartitionSpec as P

BITS = 30
EDGE = 8
FACE = EDGE * EDGE
TILE = 128
CH = 64
GROUP = 8
KROWS = 9 * CH
SPLIT = 5 * CH
VMEM_LIMIT = 40 * 1024 * 1024
EDGES_VMEM = 60 * 1024 * 1024
BF = jnp.bfloat16
F32 = jnp.float32


def column_of(p, q, r):
    tap = (p + 1) * 9 + (q + 1) * 3 + r + 1
    return tap if tap < 13 else tap - 1


SHIFTS = [(p, q) for p in (-1, 0, 1) for q in (-1, 0)] + [(p, 1) for p in (-1, 0, 1)]


def lane_ids(rows):
    return lax.broadcasted_iota(jnp.int32, (rows, TILE), 1)


def occupancy_tile(words, tile):
    lane = lane_ids(words.shape[0]) + tile * TILE
    first, last = (tile * TILE) // BITS, (tile * TILE + TILE - 1) // BITS
    word = jnp.broadcast_to(words[:, first : first + 1], lane.shape)
    place = lane - first * BITS
    for w in range(first + 1, last + 1):
        past = lane >= w * BITS
        word = jnp.where(past, jnp.broadcast_to(words[:, w : w + 1], lane.shape), word)
        place = jnp.where(past, lane - w * BITS, place)
    return (jnp.right_shift(word, place) & 1).astype(F32)


def spread(occ, leaf):
    return jnp.broadcast_to(occ[leaf : leaf + 1, :], (CH, TILE)).astype(BF)


def roll(value, amount):
    return pltpu.roll(value, amount % TILE, 1)


def edges_kernel(words_ref, x_lo, x_hi, d_lo, d_hi, cross_ref, chip_ref):
    words = words_ref[...]
    occ_lo = occupancy_tile(words, 0)
    occ_hi = occupancy_tile(words, 3)
    left = lane_ids(CH) < FACE
    first_core = lax.rem(lax.axis_index("dom"), 2) == 0
    for leaf in range(x_lo.shape[0]):
        low, high = spread(occ_lo, leaf), spread(occ_hi, leaf)
        up = jnp.where(left, roll(d_hi[leaf] * high, FACE), x_hi[leaf] * high)
        down = jnp.where(left, x_lo[leaf] * low, roll(d_lo[leaf] * low, FACE))

        @pl.when(first_core)
        def _():
            cross_ref[leaf] = down
            chip_ref[leaf] = up

        @pl.when(jnp.logical_not(first_core))
        def _():
            cross_ref[leaf] = up
            chip_ref[leaf] = down


def edges(words, x, dy):
    leaves = x.shape[0]
    block = (leaves, CH, TILE)
    lo = pl.BlockSpec(block, lambda i: (0, 0, 0))
    hi = pl.BlockSpec(block, lambda i: (0, 0, 3))
    shape = jax.ShapeDtypeStruct(block, BF)
    return pl.pallas_call(
        edges_kernel,
        grid=(1,),
        out_shape=(shape, shape),
        in_specs=[pl.BlockSpec(words.shape, lambda i: (0, 0)), lo, hi, lo, hi],
        out_specs=(lo, lo),
        cost_estimate=pl.CostEstimate(flops=10**6, bytes_accessed=10**6, transcendentals=0),
        compiler_params=pltpu.CompilerParams(vmem_limit_bytes=EDGES_VMEM),
        name="edges",
    )(words, x, x, dy, dy)


def fill(store, field_ref, occ, cross_ref, chip_ref, turned):
    leaves = field_ref.shape[0]
    first_core = lax.rem(lax.axis_index("dom"), 2) == 0
    for leaf in range(leaves):
        for k in range(4):
            at = slice(k * TILE, (k + 1) * TILE)
            store[leaf, :, at] = field_ref[leaf, :, at] * spread(occ[k], leaf)

    def far(above_ref, below_ref):
        for leaf in range(leaves):
            low, high = above_ref[leaf], below_ref[leaf]
            store[leaves + leaf, :, 0:TILE] = roll(low, FACE) if turned else low
            store[leaves + leaf, :, 3 * TILE : 4 * TILE] = roll(high, FACE) if turned else high

    pl.when(first_core)(lambda: far(chip_ref, cross_ref))
    pl.when(jnp.logical_not(first_core))(lambda: far(cross_ref, chip_ref))
    store[2 * leaves] = jnp.zeros(store.shape[1:], BF)


def stacked(store, near_ref, leaf, z, device, leaves):
    def place(p, q):
        if (p, q, z) == (0, 0, 0):
            return leaf
        ident = near_ref[leaf, column_of(p, q, z)]
        owner = ident // leaves
        slot = ident - owner * leaves
        slot = jnp.where(owner == device, slot, slot + leaves)
        return jnp.where(ident < 0, 2 * leaves, slot)

    lane = lane_ids(CH)
    left = lane < FACE
    row_b = (lane // EDGE) % EDGE
    first, last = row_b == 0, row_b == EDGE - 1
    tiles = {}
    for q in (-1, 0, 1):
        mid = place(0, q)
        tiles[q] = [store[mid, :, k * TILE : (k + 1) * TILE] for k in range(4)]
        after = store[place(1, q), :, 0:TILE]
        before = store[place(-1, q), :, 3 * TILE : 4 * TILE]
        tiles[q].append(jnp.where(left, after, before))
    moved = {
        -1: [
            jnp.where(first, roll(m, FACE + EDGE), roll(c, EDGE))
            for m, c in zip(tiles[-1], tiles[0])
        ],
        0: tiles[0],
        1: [
            jnp.where(last, roll(m, -FACE - EDGE), roll(c, -EDGE))
            for m, c in zip(tiles[1], tiles[0])
        ],
    }
    swapped = {q: [roll(t, FACE) for t in moved[q]] for q in (-1, 0, 1)}

    def piece(p, q):
        if p == 0:
            parts = moved[q][:4]
        elif p == 1:
            parts = [jnp.where(left, swapped[q][k], swapped[q][k + 1]) for k in range(4)]
        else:
            parts = [jnp.where(left, swapped[q][(k - 1) % 5], swapped[q][k]) for k in range(4)]
        return jnp.concatenate(parts, axis=1)

    return jnp.concatenate([piece(p, q) for p, q in SHIFTS], axis=0)


def c_index():
    return lane_ids(CH) % EDGE


def shift_c(value, r):
    if r == 0:
        return value
    edge = c_index() == (EDGE - 1 if r > 0 else 0)
    zero = jnp.zeros((CH, TILE), value.dtype)
    parts = [
        jnp.where(edge, zero, roll(value[:, k * TILE : (k + 1) * TILE], -r)) for k in range(4)
    ]
    return jnp.concatenate(parts, axis=1)


def across_c(value, z):
    edge = c_index() == (EDGE - 1 if z > 0 else 0)
    zero = jnp.zeros((CH, TILE), value.dtype)
    parts = [
        jnp.where(edge, roll(value[:, k * TILE : (k + 1) * TILE], z * (EDGE - 1)), zero)
        for k in range(4)
    ]
    return jnp.concatenate(parts, axis=1)


def listed(near_ref, leaf, z):
    found = jnp.int32(-1)
    for p in (-1, 0, 1):
        for q in (-1, 0, 1):
            found = jnp.maximum(found, near_ref[leaf, column_of(p, q, z)])
    return found >= 0


def grad_kernel(
    near_ref, words_ref, x_ref, d_ref, cross_ref, chip_ref, keep_ref, send_ref, store, total, packed
):
    leaves = x_ref.shape[0]
    device = lax.axis_index("dom")
    words = words_ref[...]
    occ = [occupancy_tile(words, k) for k in range(4)]
    fill(store, x_ref, occ, cross_ref, chip_ref, False)

    def masked_dy(leaf):
        return jnp.concatenate(
            [d_ref[leaf, :, k * TILE : (k + 1) * TILE] * spread(occ[k], leaf) for k in range(4)],
            axis=1,
        )

    contract = (((1,), (1,)), ((), ()))
    for leaf in range(leaves):
        near_x = stacked(store, near_ref, leaf, 0, device, leaves)
        center = masked_dy(leaf)
        wide = jnp.concatenate([shift_c(center, -r) for r in (-1, 0, 1)], axis=0)
        term = lax.dot_general(near_x, wide, contract, preferred_element_type=F32)
        if leaf == 0:
            total[...] = term
        else:
            total[...] += term

    for z in (-1, 1):
        for leaf in range(leaves):

            @pl.when(listed(near_ref, leaf, z))
            def _():
                near_x = stacked(store, near_ref, leaf, z, device, leaves)
                edge = across_c(masked_dy(leaf), -z)
                at = slice((z + 1) * CH, (z + 2) * CH)
                total[:, at] += lax.dot_general(
                    near_x, edge, contract, preferred_element_type=F32
                )

    packed[0:KROWS, :] = total[:, 0:TILE]
    packed[KROWS:, 0:CH] = total[0:SPLIT, TILE:]
    packed[KROWS : 2 * KROWS - SPLIT, CH:] = total[SPLIT:, TILE:]
    packed[2 * KROWS - SPLIT :, CH:] = jnp.zeros((2 * SPLIT - KROWS, CH), F32)
    core = lax.rem(device, 2)
    rows = packed.shape[0] // 2
    keep_ref[...] = packed[pl.ds(pl.multiple_of(core * rows, 8), rows), :]
    send_ref[...] = packed[pl.ds(pl.multiple_of((1 - core) * rows, 8), rows), :]


def vmem_spec():
    return pl.BlockSpec(memory_space=pltpu.VMEM)


def any_spec():
    return pl.BlockSpec(memory_space=pl.ANY)


def smem_spec():
    return pl.BlockSpec(memory_space=pltpu.SMEM)


def params():
    return pltpu.CompilerParams(vmem_limit_bytes=VMEM_LIMIT)


def cost(flops, bytes_accessed):
    return pl.CostEstimate(flops=flops, bytes_accessed=bytes_accessed, transcendentals=0)


def grad_terms(near, words, x, dy, cross, chip):
    leaves = x.shape[0]
    rows = KROWS + SPLIT
    shape = jax.ShapeDtypeStruct((rows // 2, TILE), F32)
    return pl.pallas_call(
        grad_kernel,
        out_shape=(shape, shape),
        in_specs=[smem_spec()] + [vmem_spec()] * 5,
        out_specs=(vmem_spec(), vmem_spec()),
        scratch_shapes=[
            pltpu.VMEM((2 * leaves + 1, CH, 4 * TILE), BF),
            pltpu.VMEM((KROWS, 3 * CH), F32),
            pltpu.VMEM((rows, TILE), F32),
        ],
        cost_estimate=cost(10**9, 2 * 10**6),
        compiler_params=params(),
        name="grad_terms",
    )(near, words, x, dy, cross, chip)


def conv_kernel(
    turned, near_ref, words_ref, x_ref, cross_ref, chip_ref, w_ref, _, out_ref, done_ref, store, taps_ref
):
    leaves = x_ref.shape[0]
    device = lax.axis_index("dom")
    words = words_ref[...]
    occ = [occupancy_tile(words, k) for k in range(4)]
    fill(store, x_ref, occ, cross_ref, chip_ref, turned)
    for index, (p, q) in enumerate(SHIFTS):
        for r in (-1, 0, 1):
            tap = (p + 1) * 9 + (q + 1) * 3 + r + 1
            block = w_ref[26 - tap] if turned else w_ref[tap].T
            taps_ref[(r + 1) * CH : (r + 2) * CH, index * CH : (index + 1) * CH] = block
    taps = taps_ref[...]
    done_ref[...] = jnp.zeros(done_ref.shape, F32)

    def masked(leaf, value):
        return jnp.concatenate(
            [
                value[:, k * TILE : (k + 1) * TILE]
                * jnp.broadcast_to(occ[k][leaf : leaf + 1, :], (CH, TILE))
                for k in range(4)
            ],
            axis=1,
        )

    for leaf in range(leaves):
        near_x = stacked(store, near_ref, leaf, 0, device, leaves)
        wide = jnp.dot(taps, near_x, preferred_element_type=F32)
        total = wide[CH : 2 * CH]
        for r in (-1, 1):
            total = total + shift_c(wide[(r + 1) * CH : (r + 2) * CH], r)
        out_ref[leaf] = masked(leaf, total).astype(BF)

    for leaf in range(leaves):

        @pl.when(listed(near_ref, leaf, -1) | listed(near_ref, leaf, 1))
        def _():
            near_x = stacked(store, near_ref, leaf, 0, device, leaves)
            wide = jnp.dot(taps, near_x, preferred_element_type=F32)
            total = wide[CH : 2 * CH]
            for r in (-1, 1):
                total = total + shift_c(wide[(r + 1) * CH : (r + 2) * CH], r)
            for z in (-1, 1):
                near_z = stacked(store, near_ref, leaf, z, device, leaves)
                part = jnp.dot(
                    taps[(z + 1) * CH : (z + 2) * CH], near_z, preferred_element_type=F32
                )
                total = total + across_c(part, z)
            out_ref[leaf] = masked(leaf, total).astype(BF)


def conv(near, words, x, cross, chip, weight, after, turned):
    leaves = x.shape[0]
    return pl.pallas_call(
        functools.partial(conv_kernel, turned),
        out_shape=(jax.ShapeDtypeStruct(x.shape, BF), jax.ShapeDtypeStruct((8, TILE), F32)),
        in_specs=[smem_spec()] + [vmem_spec()] * 5 + [any_spec()],
        out_specs=(vmem_spec(), vmem_spec()),
        scratch_shapes=[
            pltpu.VMEM((2 * leaves + 1, CH, 4 * TILE), BF),
            pltpu.VMEM((3 * CH, KROWS), BF),
        ],
        cost_estimate=cost(2 * 10**9, 2 * 10**6),
        compiler_params=params(),
        name="in_grad_conv" if turned else "out_conv",
    )(near, words, x, cross, chip, weight, after)


def sum_kernel(own_ref, *refs):
    *got_refs, _, out_ref = refs
    total = own_ref[...]
    for got_ref in got_refs:
        total = total + got_ref[...]
    out_ref[...] = total


def sum_chunks(own, got, after):
    return pl.pallas_call(
        sum_kernel,
        out_shape=jax.ShapeDtypeStruct(own.shape, F32),
        in_specs=[vmem_spec()] * (1 + len(got)) + [any_spec()],
        out_specs=vmem_spec(),
        cost_estimate=cost(10**5, 3 * 10**5),
        compiler_params=params(),
        name="sum_chunks",
    )(own, *got, after)


def join_kernel(*refs):
    *parts, _, out_ref = refs
    lane = lax.rem(lax.axis_index("dom") // 2, 4)
    rows = parts[0].shape[0]
    for mask, part in enumerate(parts):
        at = pl.multiple_of(jnp.bitwise_xor(lane, mask) * rows, 8)
        out_ref[pl.ds(at, rows), :] = part[...]


def join_chunks(parts, after):
    rows = parts[0].shape[0]
    return pl.pallas_call(
        join_kernel,
        out_shape=jax.ShapeDtypeStruct((len(parts) * rows, TILE), F32),
        in_specs=[vmem_spec()] * len(parts) + [any_spec()],
        out_specs=vmem_spec(),
        cost_estimate=cost(10**5, 5 * 10**5),
        compiler_params=params(),
        name="join_chunks",
    )(*parts, after)


def unpack_kernel(scale, own_ref, other_ref, out_ref, total):
    core = lax.rem(lax.axis_index("dom"), 2)
    rows = own_ref.shape[0]
    total[pl.ds(pl.multiple_of(core * rows, 8), rows), :] = own_ref[...] * scale
    total[pl.ds(pl.multiple_of((1 - core) * rows, 8), rows), :] = other_ref[...] * scale
    for index, (p, q) in enumerate(SHIFTS):
        for r in (-1, 0, 1):
            tap = (p + 1) * 9 + (q + 1) * 3 + r + 1
            row, side = index * CH, r + 1
            if r == 1:
                row, side = (KROWS + row, 0) if row < SPLIT else (KROWS + row - SPLIT, 1)
            out_ref[tap] = total[row : row + CH, side * CH : (side + 1) * CH]


def unpack(own, other, scale):
    return pl.pallas_call(
        functools.partial(unpack_kernel, scale),
        out_shape=jax.ShapeDtypeStruct((27, CH, CH), F32),
        in_specs=[vmem_spec(), vmem_spec()],
        out_specs=vmem_spec(),
        scratch_shapes=[pltpu.VMEM((2 * own.shape[0], TILE), F32)],
        cost_estimate=cost(10**6, 10**6),
        compiler_params=params(),
        name="unpack_grad",
    )(own, other)


def exchange(array, mask, size):
    return lax.ppermute(array, "dom", [(i, i ^ mask) for i in range(size)])


def shards(features, cotangent, weight, mask_words, neighbors):
    leaves, channels, voxels = features.shape
    size = lax.axis_size("dom")
    device = lax.axis_index("dom")
    to_cross, to_chip = edges(mask_words, features, cotangent)
    between = [(i, i + 1) for i in range(1, size - 1, 2)]
    cross = lax.ppermute(to_cross, "dom", between + [(j, i) for i, j in between])
    chip = exchange(to_chip, 1, size)

    keep, send = grad_terms(neighbors, mask_words, features, cotangent, cross, chip)
    keep = keep + exchange(send, 1, size)
    rows = keep.shape[0] // 4
    lane = (device // 2) % 4
    chunk = lambda index: lax.dynamic_slice_in_dim(keep, index * rows, rows, axis=0)
    to_send = [chunk(lane ^ m) for m in (1, 2, 3)]
    own = chunk(lane)
    got = [exchange(part, 2 * m, size) for m, part in zip((1, 2, 3), to_send)]
    out_features, out_done = conv(
        neighbors, mask_words, features, cross, chip, weight, to_send[2], False
    )
    own = sum_chunks(own, got, out_done)
    if size > GROUP:
        groups = [[j * GROUP + i for j in range(size // GROUP)] for i in range(GROUP)]
        own = lax.psum(own, "dom", axis_index_groups=groups)
    back = [exchange(own, 2 * m, size) for m in (1, 2, 3)]
    in_grad, in_done = conv(neighbors, mask_words, cotangent, cross, chip, weight, own, True)
    half = join_chunks([own] + back, in_done)
    other = exchange(half, 1, size)
    scale = float(size * leaves * voxels) ** -0.5
    return (out_features, in_grad, unpack(half, other, scale))


def solution(mesh):
    split = P(("scene", "dom"), None, None)
    flat = P(("scene", "dom"), None)
    return jax.shard_map(
        shards,
        mesh=mesh,
        in_specs=(split, split, P(), flat, flat),
        out_specs=(split, split, P("scene", None, None)),
        check_vma=False,
    )
```

time: 52.2 us -> 40.4 us (0.77)
  waiting for transfers between devices: 14 us -> 3.8 us
  local copies, waits for them, and re-layouts: 4.79 us -> 0.05 us
  Pallas kernels: 15.6 us -> 19.6 us
    ppermute x8 -> x9, waiting for transfers between devices: 9.99 us -> 3.8 us  [exchange(): return lax.ppermute(array, 'dom', [(i, i ^ mask) for i in range(size)])]
    ppermute x2 -> x1, waiting for transfers between devices: 3.99 us -> 0.01 us  [shards(): lax.ppermute(to_cross, 'dom', between + [(j, i) for i, j in between])]
    ppermute x2 -> x1, starting transfers between devices: 3.66 us -> 0.66 us  [shards(): lax.ppermute(to_cross, 'dom', between + [(j, i) for i, j in between])]
    unnamed x16 -> x10, local copies, waits for them, and re-layouts: 2.79 us -> 0.02 us
    ppermute x8 -> x9, starting transfers between devices: 12.6 us -> 15.4 us  [exchange(): return lax.ppermute(array, 'dom', [(i, i ^ mask) for i in range(size)])]
    pallas_call x1, Pallas kernels: 0.22 us -> 2.63 us  [edges(): pl.pallas_call(edges_kernel, grid=(1,), out_shape=(shape, shape), in_spec...]
    reshape x4 -> x0, local copies, waits for them, and re-layouts: 1.8 us -> none  [the longest x2 1.04 us: shards(): taps_out = order(cube).transpose(1, 3, 0, 2).reshape(3 * channels, KROWS)]
    pallas_call x3 -> x5, Pallas kernels: 14.3 us -> 15.8 us  [the longest x2 11.9 us: conv(): pl.pallas_call(functools.partial(conv_kernel, turned), out_shape=(jax.Sha...]
  transfers between devices with their start and end apart: 10 -> 10, of which waited for: 6 -> 3; matrix products, arithmetic and copies ran while one was open for 4% -> 0% of each run, Pallas kernels for 19% -> 30%
where the time goes in v2:
time: 40.4 us; the launch traced here: 40.2 us
  Pallas kernels  19.6 us (49%)
  starting transfers between devices  16 us (40%)
  waiting for transfers between devices  3.8 us (9%)
  between operations  0.72 us (2%)
    ppermute x9, starting transfers between devices, exchange(): return lax.ppermute(array, 'dom', [(i, i ^ mask) for i in range(size)])  15.4 us
    pallas_call x2, Pallas kernels, conv(): pl.pallas_call(functools.partial(conv_kernel, turned), out_shape=(jax.Sha...  11.9 us
    pallas_call x1, Pallas kernels, grad_terms(): pl.pallas_call(grad_kernel, out_shape=(shape, shape), in_specs=[smem_spec...  3.82 us
    ppermute x9, waiting for transfers between devices, exchange(): return lax.ppermute(array, 'dom', [(i, i ^ mask) for i in range(size)])  3.8 us
    pallas_call x1, Pallas kernels, edges(): pl.pallas_call(edges_kernel, grid=(1,), out_shape=(shape, shape), in_spec...  2.63 us
    pallas_call x1, Pallas kernels, unpack(): pl.pallas_call(functools.partial(unpack_kernel, scale), out_shape=jax.Sha...  1.16 us
  transfers between devices with their start and end apart: 10, of which 3 were waited for; matrix products, arithmetic and copies ran while one was open for 0% of the time, Pallas kernels for 30%

profile of v2, /device:TPU:0, one launch (start us, length us, event | category | flops | bytes accessed | tf_op | source)
XLA Modules:
  0.0 40.2 jit_solution(14067081898953371065)
XLA Ops:
  0.6 0.0 copy-start.2
  0.6 0.0 copy-start.1
  0.7 0.0 copy-start
  0.7 0.0 copy-start.4
  0.7 2.6 %edges.1 = (bf16[8,64,128]{2,1,0:T(8,128)(2,1)}, bf16[8,64,128]{2,1,0:T(8,128)(2,1)}) custom-call(s32[8,18]{1,0:T(8,128)} %words_ref.7, bf16[8,64,512]{2,1,0:T(8,128)(2,1)} %x_ref.4, bf16[8,64,512]{2,1,0:T(8,128)(2,1)} %x_ref.4, bf16[8,64,512]{2,1,0:T(8,128)(2,1)} %x_ref.5, bf16[8,64,512]{2,1,0:T(8,128)(2,1)} %x_ref.5), custom_call_target="tpu_custom_call" | custom-call | flops 1000000 | bytes 1000000 | tf_op jit(solution)/shard_map/edges/pallas_call | solution.py:84
  3.3 0.7 %collective-permute-start = (bf16[8,64,128]{2,1,0:T(8,128)(2,1)}, bf16[8,64,128]{2,1,0:T(8,128)(2,1)S(1)}, u32[]{:S(2)}, u32[]{:S(2)}) collective-permute-start(bf16[8,64,128]{2,1,0:T(8,128)(2,1)} %get-tuple-element.11), channel_id=1, source_target_pairs={{1,2},{3,4},{5,6},{2,1},{4,3},{6,5},{9,10},{11,12},{13,14},{10,9},... | collective-permute-start | bytes 393224 | tf_op jit(solution)/shard_map/ppermute | solution.py:430
  4.0 4.4 %collective-permute-start.1 = (bf16[8,64,128]{2,1,0:T(8,128)(2,1)}, bf16[8,64,128]{2,1,0:T(8,128)(2,1)S(1)}, u32[]{:S(2)}, u32[]{:S(2)}) collective-permute-start(bf16[8,64,128]{2,1,0:T(8,128)(2,1)} %get-tuple-element.12), channel_id=1, source_target_pairs={{0,1},{1,0},{2,3},{3,2},{4,5},{5,4},{6,7},{7,6},{8,9},{9,8},{10,11... | collective-permute-start | bytes 393224 | tf_op jit(solution)/shard_map/ppermute | solution.py:421
  8.4 0.0 collective-permute-done.cross_ref
  8.4 1.2 %collective-permute-done.1.chip_ref = bf16[8,64,128]{2,1,0:T(8,128)(2,1)S(1)} collective-permute-done((bf16[8,64,128]{2,1,0:T(8,128)(2,1)}, bf16[8,64,128]{2,1,0:T(8,128)(2,1)S(1)}, u32[]{:S(2)}, u32[]{:S(2)}) %collective-permute-start.1) | collective-permute-done | bytes 131104 | tf_op jit(solution)/shard_map/ppermute | solution.py:421
  9.6 0.0 copy-done.2
  9.6 0.0 copy-done.1
  9.6 0.0 copy-done
  9.6 0.0 copy-done.4
  9.6 3.8 %grad_terms.1 = (f32[448,128]{1,0:T(8,128)S(1)}, f32[448,128]{1,0:T(8,128)S(1)}) custom-call(s32[8,26]{1,0:T(8,128)S(1)} %copy-done.4, s32[8,18]{1,0:T(8,128)S(1)} %copy-done.2, bf16[8,64,512]{2,1,0:T(8,128)(2,1)S(1)} %copy-done, bf16[8,64,512]{2,1,0:T(8,128)(2,1)S(1)} %copy-done.1, bf16[8,64,128]{2,1,0:T(8,128)(2,1)S(1)} %collective-permute-done.cross_ref, ...), custom_call_target="tpu_custom_call" | custom-call | flops 1000000000 | bytes 2000000 | tf_op jit(solution)/shard_map/grad_terms/pallas_call | solution.py:266
  13.5 1.7 %collective-permute-start.2 = (f32[448,128]{1,0:T(8,128)S(1)}, f32[448,128]{1,0:T(8,128)S(1)}, u32[]{:S(2)}, u32[]{:S(2)}) collective-permute-start(f32[448,128]{1,0:T(8,128)S(1)} %get-tuple-element.14), channel_id=1, source_target_pairs={{0,1},{1,0},{2,3},{3,2},{4,5},{5,4},{6,7},{7,6},{8,9},{9,8},{10,11... | collective-permute-start | bytes 688136 | tf_op jit(solution)/shard_map/ppermute | solution.py:421
  15.1 1.1 %collective-permute-done.2 = f32[448,128]{1,0:T(8,128)S(1)} collective-permute-done((f32[448,128]{1,0:T(8,128)S(1)}, f32[448,128]{1,0:T(8,128)S(1)}, u32[]{:S(2)}, u32[]{:S(2)}) %collective-permute-start.2) | collective-permute-done | bytes 229408 | tf_op jit(solution)/shard_map/ppermute | solution.py:421
  16.2 0.0 copy-start.3
  16.3 3.1 %collective-permute-start.4 = (f32[112,128]{1,0:T(8,128)S(1)}, f32[112,128]{1,0:T(8,128)S(1)}, u32[]{:S(2)}, u32[]{:S(2)}) collective-permute-start(f32[112,128]{1,0:T(8,128)S(1)} %get-tuple-element.19), channel_id=1, source_target_pairs={{0,4},{1,5},{2,6},{3,7},{4,0},{5,1},{6,2},{7,3},{8,12},{9,13},{10,... | collective-permute-start | bytes 172040 | tf_op jit(solution)/shard_map/ppermute | solution.py:421
  19.4 1.6 %collective-permute-start.3 = (f32[112,128]{1,0:T(8,128)S(1)}, f32[112,128]{1,0:T(8,128)S(1)}, u32[]{:S(2)}, u32[]{:S(2)}) collective-permute-start(f32[112,128]{1,0:T(8,128)S(1)} %get-tuple-element.20), channel_id=1, source_target_pairs={{0,2},{1,3},{2,0},{3,1},{4,6},{5,7},{6,4},{7,5},{8,10},{9,11},{10,... | collective-permute-start | bytes 172040 | tf_op jit(solution)/shard_map/ppermute | solution.py:421
  21.0 0.0 collective-permute-start.5
  21.0 0.0 copy-done.3
  21.0 6.1 %out_conv.1 = (bf16[8,64,512]{2,1,0:T(8,128)(2,1)}, f32[8,128]{1,0:T(8,128)S(1)}) custom-call(s32[8,26]{1,0:T(8,128)S(1)} %copy-done.4, s32[8,18]{1,0:T(8,128)S(1)} %copy-done.2, bf16[8,64,512]{2,1,0:T(8,128)(2,1)S(1)} %copy-done, bf16[8,64,128]{2,1,0:T(8,128)(2,1)S(1)} %collective-permute-done.cross_ref, ...), custom_call_target="tpu_custom_call" | custom-call | flops 2000000000 | bytes 2000000 | tf_op jit(solution)/shard_map/out_conv/pallas_call | solution.py:336
  27.0 0.0 collective-permute-done.4.refs_1_
  27.0 0.0 collective-permute-done.3.refs_0_
  27.1 0.0 collective-permute-done.5.refs_2_
  27.1 3.9 %collective-permute-start.8 = (f32[112,128]{1,0:T(8,128)S(1)}, f32[112,128]{1,0:T(8,128)S(1)}, u32[]{:S(2)}, u32[]{:S(2)}) collective-permute-start(f32[112,128]{1,0:T(8,128)S(1)} %sum_chunks.1._.refs_0_), channel_id=1, source_target_pairs={{0,6},{1,7},{2,4},{3,5},{4,2},{5,3},{6,0},{7,1},{8,14},{9,15},{10,... | collective-permute-start | bytes 172040 | tf_op jit(solution)/shard_map/ppermute | solution.py:421
  31.0 0.0 collective-permute-start.7
  31.0 0.6 %collective-permute-start.6 = (f32[112,128]{1,0:T(8,128)S(1)}, f32[112,128]{1,0:T(8,128)S(1)}, u32[]{:S(2)}, u32[]{:S(2)}) collective-permute-start(f32[112,128]{1,0:T(8,128)S(1)} %sum_chunks.1._.refs_0_), channel_id=1, source_target_pairs={{0,2},{1,3},{2,0},{3,1},{4,6},{5,7},{6,4},{7,5},{8,10},{9,11},{10,... | collective-permute-start | bytes 172040 | tf_op jit(solution)/shard_map/ppermute | solution.py:421
  31.6 5.8 %in_grad_conv.1 = (bf16[8,64,512]{2,1,0:T(8,128)(2,1)}, f32[8,128]{1,0:T(8,128)S(1)}) custom-call(s32[8,26]{1,0:T(8,128)S(1)} %copy-done.4, s32[8,18]{1,0:T(8,128)S(1)} %copy-done.2, bf16[8,64,512]{2,1,0:T(8,128)(2,1)S(1)} %copy-done.1, bf16[8,64,128]{2,1,0:T(8,128)(2,1)S(1)} %collective-permute-done.cross_ref, ...), custom_call_target="tpu_custom_call" | custom-call | flops 2000000000 | bytes 2000000 | tf_op jit(solution)/shard_map/in_grad_conv/pallas_call | solution.py:336
  37.4 0.0 collective-permute-done.8.refs_3_
  37.4 0.0 collective-permute-done.7.refs_2_
  37.4 0.0 collective-permute-done.6.refs_1_
  37.5 0.1 collective-permute-start.9
  37.6 1.5 %collective-permute-done.9.other_ref = f32[448,128]{1,0:T(8,128)S(1)} collective-permute-done((f32[448,128]{1,0:T(8,128)S(1)}, f32[448,128]{1,0:T(8,128)S(1)}, u32[]{:S(2)}, u32[]{:S(2)}) %collective-permute-start.9) | collective-permute-done | bytes 229408 | tf_op jit(solution)/shard_map/ppermute | solution.py:421
  39.0 1.2 %unpack_grad.1 = f32[27,64,64]{2,1,0:T(8,128)} custom-call(f32[448,128]{1,0:T(8,128)S(1)} %join_chunks.1.own_ref, f32[448,128]{1,0:T(8,128)S(1)} %collective-permute-done.9.other_ref), custom_call_target="tpu_custom_call" | custom-call | flops 1000000 | bytes 1000000 | tf_op jit(solution)/shard_map/unpack_grad/pallas_call | solution.py:408
  (4 shorter events, 0.1 us)
Async XLA Ops:
  0.6 9.0 %copy-start.2 = (s32[8,18]{1,0:T(8,128)S(1)}, s32[8,18]{1,0:T(8,128)}, u32[]{:S(2)}) copy-start(s32[8,18]{1,0:T(8,128)} %words_ref.7) | copy-start | bytes 1732
  0.6 9.0 %copy-start.1 = (bf16[8,64,512]{2,1,0:T(8,128)(2,1)S(1)}, bf16[8,64,512]{2,1,0:T(8,128)(2,1)}, u32[]{:S(2)}) copy-start(bf16[8,64,512]{2,1,0:T(8,128)(2,1)} %x_ref.5) | copy-start | bytes 1572868
  0.7 9.0 %copy-start = (bf16[8,64,512]{2,1,0:T(8,128)(2,1)S(1)}, bf16[8,64,512]{2,1,0:T(8,128)(2,1)}, u32[]{:S(2)}) copy-start(bf16[8,64,512]{2,1,0:T(8,128)(2,1)} %x_ref.4) | copy-start | bytes 1572868
  0.7 9.0 %copy-start.4 = (s32[8,26]{1,0:T(8,128)S(1)}, s32[8,26]{1,0:T(8,128)}, u32[]{:S(2)}) copy-start(s32[8,26]{1,0:T(8,128)} %near_ref.5) | copy-start | bytes 2500
  3.3 5.1 %collective-permute-start = (bf16[8,64,128]{2,1,0:T(8,128)(2,1)}, bf16[8,64,128]{2,1,0:T(8,128)(2,1)S(1)}, u32[]{:S(2)}, u32[]{:S(2)}) collective-permute-start(bf16[8,64,128]{2,1,0:T(8,128)(2,1)} %get-tuple-element.11), channel_id=1, source_target_pairs={{1,2},{3,4},{5,6},{2,1},{4,3},{6,5},{9,10},{11,12},{13,14},{10,9},... | collective-permute-start | bytes 393224 | tf_op jit(solution)/shard_map/ppermute | solution.py:430
  4.0 5.6 %collective-permute-start.1 = (bf16[8,64,128]{2,1,0:T(8,128)(2,1)}, bf16[8,64,128]{2,1,0:T(8,128)(2,1)S(1)}, u32[]{:S(2)}, u32[]{:S(2)}) collective-permute-start(bf16[8,64,128]{2,1,0:T(8,128)(2,1)} %get-tuple-element.12), channel_id=1, source_target_pairs={{0,1},{1,0},{2,3},{3,2},{4,5},{5,4},{6,7},{7,6},{8,9},{9,8},{10,11... | collective-permute-start | bytes 393224 | tf_op jit(solution)/shard_map/ppermute | solution.py:421
  13.5 2.8 %collective-permute-start.2 = (f32[448,128]{1,0:T(8,128)S(1)}, f32[448,128]{1,0:T(8,128)S(1)}, u32[]{:S(2)}, u32[]{:S(2)}) collective-permute-start(f32[448,128]{1,0:T(8,128)S(1)} %get-tuple-element.14), channel_id=1, source_target_pairs={{0,1},{1,0},{2,3},{3,2},{4,5},{5,4},{6,7},{7,6},{8,9},{9,8},{10,11... | collective-permute-start | bytes 688136 | tf_op jit(solution)/shard_map/ppermute | solution.py:421
  16.2 4.7 %copy-start.3 = (bf16[27,64,64]{2,1,0:T(8,128)(2,1)S(1)}, bf16[27,64,64]{2,1,0:T(8,128)(2,1)}, u32[]{:S(2)}) copy-start(bf16[27,64,64]{2,1,0:T(8,128)(2,1)} %w_ref.3) | copy-start | bytes 663556
  16.3 10.7 %collective-permute-start.4 = (f32[112,128]{1,0:T(8,128)S(1)}, f32[112,128]{1,0:T(8,128)S(1)}, u32[]{:S(2)}, u32[]{:S(2)}) collective-permute-start(f32[112,128]{1,0:T(8,128)S(1)} %get-tuple-element.19), channel_id=1, source_target_pairs={{0,4},{1,5},{2,6},{3,7},{4,0},{5,1},{6,2},{7,3},{8,12},{9,13},{10,... | collective-permute-start | bytes 172040 | tf_op jit(solution)/shard_map/ppermute | solution.py:421
  19.4 7.7 %collective-permute-start.3 = (f32[112,128]{1,0:T(8,128)S(1)}, f32[112,128]{1,0:T(8,128)S(1)}, u32[]{:S(2)}, u32[]{:S(2)}) collective-permute-start(f32[112,128]{1,0:T(8,128)S(1)} %get-tuple-element.20), channel_id=1, source_target_pairs={{0,2},{1,3},{2,0},{3,1},{4,6},{5,7},{6,4},{7,5},{8,10},{9,11},{10,... | collective-permute-start | bytes 172040 | tf_op jit(solution)/shard_map/ppermute | solution.py:421
  21.0 6.1 %collective-permute-start.5 = (f32[112,128]{1,0:T(8,128)S(1)}, f32[112,128]{1,0:T(8,128)S(1)}, u32[]{:S(2)}, u32[]{:S(2)}) collective-permute-start(f32[112,128]{1,0:T(8,128)S(1)} %get-tuple-element.22._), channel_id=1, source_target_pairs={{0,6},{1,7},{2,4},{3,5},{4,2},{5,3},{6,0},{7,1},{8,14},{9,15},{10,... | collective-permute-start | bytes 172040 | tf_op jit(solution)/shard_map/ppermute | solution.py:421
  27.1 10.4 %collective-permute-start.8 = (f32[112,128]{1,0:T(8,128)S(1)}, f32[112,128]{1,0:T(8,128)S(1)}, u32[]{:S(2)}, u32[]{:S(2)}) collective-permute-start(f32[112,128]{1,0:T(8,128)S(1)} %sum_chunks.1._.refs_0_), channel_id=1, source_target_pairs={{0,6},{1,7},{2,4},{3,5},{4,2},{5,3},{6,0},{7,1},{8,14},{9,15},{10,... | collective-permute-start | bytes 172040 | tf_op jit(solution)/shard_map/ppermute | solution.py:421
  31.0 6.5 %collective-permute-start.7 = (f32[112,128]{1,0:T(8,128)S(1)}, f32[112,128]{1,0:T(8,128)S(1)}, u32[]{:S(2)}, u32[]{:S(2)}) collective-permute-start(f32[112,128]{1,0:T(8,128)S(1)} %sum_chunks.1._.refs_0_), channel_id=1, source_target_pairs={{0,4},{1,5},{2,6},{3,7},{4,0},{5,1},{6,2},{7,3},{8,12},{9,13},{10,... | collective-permute-start | bytes 172040 | tf_op jit(solution)/shard_map/ppermute | solution.py:421
  31.0 6.5 %collective-permute-start.6 = (f32[112,128]{1,0:T(8,128)S(1)}, f32[112,128]{1,0:T(8,128)S(1)}, u32[]{:S(2)}, u32[]{:S(2)}) collective-permute-start(f32[112,128]{1,0:T(8,128)S(1)} %sum_chunks.1._.refs_0_), channel_id=1, source_target_pairs={{0,2},{1,3},{2,0},{3,1},{4,6},{5,7},{6,4},{7,5},{8,10},{9,11},{10,... | collective-permute-start | bytes 172040 | tf_op jit(solution)/shard_map/ppermute | solution.py:421
  37.5 1.6 %collective-permute-start.9 = (f32[448,128]{1,0:T(8,128)S(1)}, f32[448,128]{1,0:T(8,128)S(1)}, u32[]{:S(2)}, u32[]{:S(2)}) collective-permute-start(f32[448,128]{1,0:T(8,128)S(1)} %join_chunks.1.own_ref), channel_id=1, source_target_pairs={{0,1},{1,0},{2,3},{3,2},{4,5},{5,4},{6,7},{7,6},{8,9},{9,8},{10,11... | collective-permute-start | bytes 688136 | tf_op jit(solution)/shard_map/ppermute | solution.py:421

commit v3 on v2

v3 whole, which is shorter than its diff:
```python
import functools

import jax
import jax.numpy as jnp
from jax import lax
from jax.experimental import pallas as pl
from jax.experimental.pallas import tpu as pltpu
from jax.sharding import PartitionSpec as P

BITS = 30
EDGE = 8
FACE = EDGE * EDGE
TILE = 128
CH = 64
GROUP = 8
KROWS = 9 * CH
SPLIT = 5 * CH
VMEM_LIMIT = 40 * 1024 * 1024
EDGES_VMEM = 63000000
BF = jnp.bfloat16
F32 = jnp.float32


def column_of(p, q, r):
    tap = (p + 1) * 9 + (q + 1) * 3 + r + 1
    return tap if tap < 13 else tap - 1


SHIFTS = [(p, q) for p in (-1, 0, 1) for q in (-1, 0)] + [(p, 1) for p in (-1, 0, 1)]


def lane_ids(rows):
    return lax.broadcasted_iota(jnp.int32, (rows, TILE), 1)


def occupancy_tile(words, tile):
    lane = lane_ids(words.shape[0]) + tile * TILE
    first, last = (tile * TILE) // BITS, (tile * TILE + TILE - 1) // BITS
    word = jnp.broadcast_to(words[:, first : first + 1], lane.shape)
    place = lane - first * BITS
    for w in range(first + 1, last + 1):
        past = lane >= w * BITS
        word = jnp.where(past, jnp.broadcast_to(words[:, w : w + 1], lane.shape), word)
        place = jnp.where(past, lane - w * BITS, place)
    return (jnp.right_shift(word, place) & 1).astype(F32)


def spread(occ, leaf):
    return jnp.broadcast_to(occ[leaf : leaf + 1, :], (CH, TILE)).astype(BF)


def roll(value, amount):
    return pltpu.roll(value, amount % TILE, 1)


def edges_kernel(words_hbm, x_hbm, d_hbm, cross_ref, chip_ref, words_ref, tiles, sems):
    leaves = x_hbm.shape[0]
    copies = [pltpu.make_async_copy(words_hbm, words_ref, sems.at[4])]
    for i, (field, k) in enumerate(((x_hbm, 0), (x_hbm, 3), (d_hbm, 0), (d_hbm, 3))):
        source = field.at[:, :, pl.ds(k * TILE, TILE)]
        copies.append(pltpu.make_async_copy(source, tiles.at[i], sems.at[i]))
    for copy in copies:
        copy.start()
    left = lane_ids(CH) < FACE
    first_core = lax.rem(lax.axis_index("dom"), 2) == 0
    for copy in copies:
        copy.wait()
    words = words_ref[...]
    occ_lo = occupancy_tile(words, 0)
    occ_hi = occupancy_tile(words, 3)
    for leaf in range(leaves):
        low, high = spread(occ_lo, leaf), spread(occ_hi, leaf)
        up = jnp.where(left, roll(tiles[3, leaf] * high, FACE), tiles[1, leaf] * high)
        down = jnp.where(left, tiles[0, leaf] * low, roll(tiles[2, leaf] * low, FACE))
        cross_ref[leaf] = jnp.where(first_core, down, up)
        chip_ref[leaf] = jnp.where(first_core, up, down)


def edges(words, x, dy):
    leaves = x.shape[0]
    shape = jax.ShapeDtypeStruct((leaves, CH, TILE), BF)
    return pl.pallas_call(
        edges_kernel,
        out_shape=(shape, shape),
        in_specs=[pl.BlockSpec(memory_space=pltpu.HBM)] * 3,
        out_specs=(vmem_spec(), vmem_spec()),
        scratch_shapes=[
            pltpu.VMEM(words.shape, jnp.int32),
            pltpu.VMEM((4, leaves, CH, TILE), BF),
            pltpu.SemaphoreType.DMA((5,)),
        ],
        cost_estimate=cost(10**6, 10**6),
        compiler_params=pltpu.CompilerParams(vmem_limit_bytes=EDGES_VMEM),
        name="edges",
    )(words, x, dy)


def fill(store, field_ref, occ, halo, turned):
    leaves = field_ref.shape[0]
    for leaf in range(leaves):
        for k in range(4):
            at = slice(k * TILE, (k + 1) * TILE)
            store[leaf, :, at] = field_ref[leaf, :, at] * spread(occ[k], leaf)
    if halo:
        cross_ref, chip_ref = halo
        first_core = lax.rem(lax.axis_index("dom"), 2) == 0
        for leaf in range(leaves):
            low = jnp.where(first_core, chip_ref[leaf], cross_ref[leaf])
            high = jnp.where(first_core, cross_ref[leaf], chip_ref[leaf])
            store[leaves + leaf, :, 0:TILE] = roll(low, FACE) if turned else low
            store[leaves + leaf, :, 3 * TILE : 4 * TILE] = roll(high, FACE) if turned else high
    store[store.shape[0] - 1] = jnp.zeros(store.shape[1:], BF)


def place(near_ref, leaf, p, q, z, device, leaves, which):
    if (p, q, z) == (0, 0, 0):
        return leaf
    ident = near_ref[leaf, column_of(p, q, z)]
    owner = ident // leaves
    slot = ident - owner * leaves
    absent = ident < 0
    if which == "all":
        slot = jnp.where(owner == device, slot, slot + leaves)
        return jnp.where(absent, 2 * leaves, slot)
    here = owner == device
    if which == "far":
        here = jnp.logical_not(here)
    return jnp.where(jnp.logical_and(here, jnp.logical_not(absent)), slot, leaves)


def moved_tiles(tiles):
    row_b = (lane_ids(CH) // EDGE) % EDGE
    first, last = row_b == 0, row_b == EDGE - 1
    return {
        -1: [
            jnp.where(first, roll(m, FACE + EDGE), roll(c, EDGE))
            for m, c in zip(tiles[-1], tiles[0])
        ],
        0: tiles[0],
        1: [
            jnp.where(last, roll(m, -FACE - EDGE), roll(c, -EDGE))
            for m, c in zip(tiles[1], tiles[0])
        ],
    }


def stacked(store, near_ref, leaf, z, device, leaves, which="all"):
    where = lambda p, q: place(near_ref, leaf, p, q, z, device, leaves, which)
    left = lane_ids(CH) < FACE
    tiles = {}
    for q in (-1, 0, 1):
        mid = where(0, q)
        tiles[q] = [store[mid, :, k * TILE : (k + 1) * TILE] for k in range(4)]
        after = store[where(1, q), :, 0:TILE]
        before = store[where(-1, q), :, 3 * TILE : 4 * TILE]
        tiles[q].append(jnp.where(left, after, before))
    moved = moved_tiles(tiles)
    swapped = {q: [roll(t, FACE) for t in moved[q]] for q in (-1, 0, 1)}

    def piece(p, q):
        if p == 0:
            parts = moved[q][:4]
        elif p == 1:
            parts = [jnp.where(left, swapped[q][k], swapped[q][k + 1]) for k in range(4)]
        else:
            parts = [jnp.where(left, swapped[q][(k - 1) % 5], swapped[q][k]) for k in range(4)]
        return jnp.concatenate(parts, axis=1)

    return jnp.concatenate([piece(p, q) for p, q in SHIFTS], axis=0)


def c_index():
    return lane_ids(CH) % EDGE


def shift_c(value, r):
    if r == 0:
        return value
    edge = c_index() == (EDGE - 1 if r > 0 else 0)
    zero = jnp.zeros((CH, TILE), value.dtype)
    parts = [
        jnp.where(edge, zero, roll(value[:, k * TILE : (k + 1) * TILE], -r)) for k in range(4)
    ]
    return jnp.concatenate(parts, axis=1)


def across_c(value, z):
    edge = c_index() == (EDGE - 1 if z > 0 else 0)
    zero = jnp.zeros((CH, TILE), value.dtype)
    parts = [
        jnp.where(edge, roll(value[:, k * TILE : (k + 1) * TILE], z * (EDGE - 1)), zero)
        for k in range(4)
    ]
    return jnp.concatenate(parts, axis=1)


def listed(near_ref, leaf, z):
    found = jnp.int32(-1)
    for p in (-1, 0, 1):
        for q in (-1, 0, 1):
            found = jnp.maximum(found, near_ref[leaf, column_of(p, q, z)])
    return found >= 0


def masked_field(field_ref, occ, leaf):
    return jnp.concatenate(
        [field_ref[leaf, :, k * TILE : (k + 1) * TILE] * spread(occ[k], leaf) for k in range(4)],
        axis=1,
    )


CONTRACT_LANES = (((1,), (1,)), ((), ()))


def dot_lanes(a, b):
    return lax.dot_general(a, b, CONTRACT_LANES, preferred_element_type=F32)


def grad_kernel(near_ref, words_ref, x_ref, d_ref, total, store):
    leaves = x_ref.shape[0]
    device = lax.axis_index("dom")
    words = words_ref[...]
    occ = [occupancy_tile(words, k) for k in range(4)]
    fill(store, x_ref, occ, None, False)
    for leaf in range(leaves):
        near_x = stacked(store, near_ref, leaf, 0, device, leaves, "near")
        center = masked_field(d_ref, occ, leaf)
        wide = jnp.concatenate([shift_c(center, -r) for r in (-1, 0, 1)], axis=0)
        term = dot_lanes(near_x, wide)
        if leaf == 0:
            total[...] = term
        else:
            total[...] += term

    for z in (-1, 1):
        for leaf in range(leaves):

            @pl.when(listed(near_ref, leaf, z))
            def _():
                near_x = stacked(store, near_ref, leaf, z, device, leaves, "near")
                edge = across_c(masked_field(d_ref, occ, leaf), -z)
                total[:, (z + 1) * CH : (z + 2) * CH] += dot_lanes(near_x, edge)


def grad_terms(near, words, x, dy):
    leaves = x.shape[0]
    return pl.pallas_call(
        grad_kernel,
        out_shape=jax.ShapeDtypeStruct((KROWS, 3 * CH), F32),
        in_specs=[smem_spec()] + [vmem_spec()] * 3,
        out_specs=vmem_spec(),
        scratch_shapes=[pltpu.VMEM((leaves + 1, CH, 4 * TILE), BF)],
        cost_estimate=cost(10**9, 2 * 10**6),
        compiler_params=params(),
        name="grad_terms",
    )(near, words, x, dy)


def grad_far_kernel(
    near_ref, words_ref, d_ref, cross_ref, chip_ref, near_total, keep_ref, send_ref, store, total, packed
):
    leaves = d_ref.shape[0]
    device = lax.axis_index("dom")
    first_core = lax.rem(device, 2) == 0
    words = words_ref[...]
    occ_lo, occ_hi = occupancy_tile(words, 0), occupancy_tile(words, 3)
    left = lane_ids(CH) < FACE
    zero = jnp.zeros((CH, TILE), BF)
    for leaf in range(leaves):
        low = jnp.where(first_core, chip_ref[leaf], cross_ref[leaf])
        high = jnp.where(first_core, cross_ref[leaf], chip_ref[leaf])
        store[leaf] = jnp.where(left, low, high)
    store[leaves] = zero

    def far_rows(leaf, z):
        where = lambda p, q: place(near_ref, leaf, p, q, z, device, leaves, "far")
        tiles = {q: [jnp.where(left, store[where(1, q)], store[where(-1, q)])] for q in (-1, 0, 1)}
        moved = moved_tiles(tiles)
        after = [jnp.where(left, moved[q][0], zero) for q in (-1, 0, 1)]
        before = [jnp.where(left, zero, moved[q][0]) for q in (-1, 0, 1)]
        return jnp.concatenate(after + before, axis=0)

    def end_planes(leaf):
        low = d_ref[leaf, :, 0:TILE] * spread(occ_lo, leaf)
        high = d_ref[leaf, :, 3 * TILE : 4 * TILE] * spread(occ_hi, leaf)
        return roll(jnp.where(left, low, high), FACE)

    def wide(leaf):
        plane = end_planes(leaf)
        cell = c_index()
        last = jnp.where(cell == EDGE - 1, zero, roll(plane, -1))
        first = jnp.where(cell == 0, zero, roll(plane, 1))
        return jnp.concatenate([last, plane, first], axis=0)

    rows = jnp.concatenate([far_rows(leaf, 0) for leaf in range(leaves)], axis=1)
    columns = jnp.concatenate([wide(leaf) for leaf in range(leaves)], axis=1)
    term = dot_lanes(rows, columns)
    total[...] = near_total[...]

    def add(part, at):
        for i, (p, q) in enumerate([(p, q) for p in (1, -1) for q in (-1, 0, 1)]):
            row = SHIFTS.index((p, q)) * CH
            total[row : row + CH, at] += part[i * CH : (i + 1) * CH, :]

    add(term, slice(0, 3 * CH))
    for z in (-1, 1):
        for leaf in range(leaves):

            @pl.when(listed(near_ref, leaf, z))
            def _():
                plane = end_planes(leaf)
                edge = c_index() == (0 if z > 0 else EDGE - 1)
                edge = jnp.where(edge, roll(plane, -z * (EDGE - 1)), zero)
                add(dot_lanes(far_rows(leaf, z), edge), slice((z + 1) * CH, (z + 2) * CH))

    packed[0:KROWS, :] = total[:, 0:TILE]
    packed[KROWS:, 0:CH] = total[0:SPLIT, TILE:]
    packed[KROWS : 2 * KROWS - SPLIT, CH:] = total[SPLIT:, TILE:]
    packed[2 * KROWS - SPLIT :, CH:] = jnp.zeros((2 * SPLIT - KROWS, CH), F32)
    core = lax.rem(device, 2)
    rows = packed.shape[0] // 2
    keep_ref[...] = packed[pl.ds(pl.multiple_of(core * rows, 8), rows), :]
    send_ref[...] = packed[pl.ds(pl.multiple_of((1 - core) * rows, 8), rows), :]


def grad_far(near, words, dy, cross, chip, total):
    leaves = dy.shape[0]
    rows = KROWS + SPLIT
    shape = jax.ShapeDtypeStruct((rows // 2, TILE), F32)
    return pl.pallas_call(
        grad_far_kernel,
        out_shape=(shape, shape),
        in_specs=[smem_spec()] + [vmem_spec()] * 5,
        out_specs=(vmem_spec(), vmem_spec()),
        scratch_shapes=[
            pltpu.VMEM((leaves + 1, CH, TILE), BF),
            pltpu.VMEM((KROWS, 3 * CH), F32),
            pltpu.VMEM((rows, TILE), F32),
        ],
        cost_estimate=cost(10**8, 2 * 10**6),
        compiler_params=params(),
        name="grad_far",
    )(near, words, dy, cross, chip, total)


def vmem_spec():
    return pl.BlockSpec(memory_space=pltpu.VMEM)


def any_spec():
    return pl.BlockSpec(memory_space=pl.ANY)


def smem_spec():
    return pl.BlockSpec(memory_space=pltpu.SMEM)


def params():
    return pltpu.CompilerParams(vmem_limit_bytes=VMEM_LIMIT)


def cost(flops, bytes_accessed):
    return pl.CostEstimate(flops=flops, bytes_accessed=bytes_accessed, transcendentals=0)


def conv_kernel(
    turned, near_ref, words_ref, x_ref, cross_ref, chip_ref, w_ref, _, out_ref, done_ref, store
):
    leaves = x_ref.shape[0]
    device = lax.axis_index("dom")
    words = words_ref[...]
    occ = [occupancy_tile(words, k) for k in range(4)]
    fill(store, x_ref, occ, (cross_ref, chip_ref), turned)

    def tap(index, r):
        p, q = SHIFTS[index]
        return (p + 1) * 9 + (q + 1) * 3 + r + 1

    if turned:
        taps = jnp.concatenate(
            [
                jnp.concatenate([w_ref[26 - tap(index, r)] for index in range(9)], axis=1)
                for r in (-1, 0, 1)
            ],
            axis=0,
        )
    else:
        taps = jnp.concatenate(
            [
                jnp.concatenate([w_ref[tap(index, r)] for r in (-1, 0, 1)], axis=1)
                for index in range(9)
            ],
            axis=0,
        ).T
    done_ref[...] = jnp.zeros(done_ref.shape, F32)

    def masked(leaf, value):
        return jnp.concatenate(
            [
                value[:, k * TILE : (k + 1) * TILE]
                * jnp.broadcast_to(occ[k][leaf : leaf + 1, :], (CH, TILE))
                for k in range(4)
            ],
            axis=1,
        )

    for leaf in range(leaves):
        near_x = stacked(store, near_ref, leaf, 0, device, leaves)
        wide = jnp.dot(taps, near_x, preferred_element_type=F32)
        total = wide[CH : 2 * CH]
        for r in (-1, 1):
            total = total + shift_c(wide[(r + 1) * CH : (r + 2) * CH], r)
        out_ref[leaf] = masked(leaf, total).astype(BF)

    for leaf in range(leaves):

        @pl.when(listed(near_ref, leaf, -1) | listed(near_ref, leaf, 1))
        def _():
            near_x = stacked(store, near_ref, leaf, 0, device, leaves)
            wide = jnp.dot(taps, near_x, preferred_element_type=F32)
            total = wide[CH : 2 * CH]
            for r in (-1, 1):
                total = total + shift_c(wide[(r + 1) * CH : (r + 2) * CH], r)
            for z in (-1, 1):
                near_z = stacked(store, near_ref, leaf, z, device, leaves)
                part = jnp.dot(
                    taps[(z + 1) * CH : (z + 2) * CH], near_z, preferred_element_type=F32
                )
                total = total + across_c(part, z)
            out_ref[leaf] = masked(leaf, total).astype(BF)


def conv(near, words, x, cross, chip, weight, after, turned):
    leaves = x.shape[0]
    return pl.pallas_call(
        functools.partial(conv_kernel, turned),
        out_shape=(jax.ShapeDtypeStruct(x.shape, BF), jax.ShapeDtypeStruct((8, TILE), F32)),
        in_specs=[smem_spec()] + [vmem_spec()] * 5 + [any_spec()],
        out_specs=(vmem_spec(), vmem_spec()),
        scratch_shapes=[pltpu.VMEM((2 * leaves + 1, CH, 4 * TILE), BF)],
        cost_estimate=cost(2 * 10**9, 2 * 10**6),
        compiler_params=params(),
        name="in_grad_conv" if turned else "out_conv",
    )(near, words, x, cross, chip, weight, after)


def sum_kernel(parts_ref, _, out_ref):
    parts = parts_ref.shape[0]
    total = parts_ref[0]
    for i in range(1, parts):
        total = total + parts_ref[i]
    for i in range(parts):
        out_ref[i] = total


def sum_chunks(parts, after):
    return pl.pallas_call(
        sum_kernel,
        out_shape=jax.ShapeDtypeStruct(parts.shape, F32),
        in_specs=[vmem_spec(), any_spec()],
        out_specs=vmem_spec(),
        cost_estimate=cost(10**5, 5 * 10**5),
        compiler_params=params(),
        name="sum_chunks",
    )(parts, after)


def unpack_kernel(scale, own_ref, other_ref, out_ref, total):
    core = lax.rem(lax.axis_index("dom"), 2)
    rows = own_ref.shape[0]
    total[pl.ds(pl.multiple_of(core * rows, 8), rows), :] = own_ref[...] * scale
    total[pl.ds(pl.multiple_of((1 - core) * rows, 8), rows), :] = other_ref[...] * scale
    for index, (p, q) in enumerate(SHIFTS):
        for r in (-1, 0, 1):
            tap = (p + 1) * 9 + (q + 1) * 3 + r + 1
            row, side = index * CH, r + 1
            if r == 1:
                row, side = (KROWS + row, 0) if row < SPLIT else (KROWS + row - SPLIT, 1)
            out_ref[tap] = total[row : row + CH, side * CH : (side + 1) * CH]


def unpack(own, other, scale):
    return pl.pallas_call(
        functools.partial(unpack_kernel, scale),
        out_shape=jax.ShapeDtypeStruct((27, CH, CH), F32),
        in_specs=[vmem_spec(), vmem_spec()],
        out_specs=vmem_spec(),
        scratch_shapes=[pltpu.VMEM((2 * own.shape[0], TILE), F32)],
        cost_estimate=cost(10**6, 10**6),
        compiler_params=params(),
        name="unpack_grad",
    )(own, other)


def exchange(array, mask, size):
    return lax.ppermute(array, "dom", [(i, i ^ mask) for i in range(size)])


def shards(features, cotangent, weight, mask_words, neighbors):
    leaves, channels, voxels = features.shape
    size = lax.axis_size("dom")
    device = lax.axis_index("dom")
    to_cross, to_chip = edges(mask_words, features, cotangent)
    between = [(i, i + 1) for i in range(1, size - 1, 2)]
    cross = lax.ppermute(to_cross, "dom", between + [(j, i) for i, j in between])
    chip = exchange(to_chip, 1, size)

    total = grad_terms(neighbors, mask_words, features, cotangent)
    keep, send = grad_far(neighbors, mask_words, cotangent, cross, chip, total)
    keep = (keep + exchange(send, 1, size)).reshape(4, -1, TILE)
    line = [
        [b + c + 2 * j for j in range(4)] for b in range(0, size, GROUP) for c in range(2)
    ]
    swap = lambda parts: lax.all_to_all(parts, "dom", 0, 0, axis_index_groups=line)
    got = swap(keep)
    out_features, out_done = conv(
        neighbors, mask_words, features, cross, chip, weight, keep, False
    )
    own = sum_chunks(got, out_done)
    if size > GROUP:
        groups = [[j * GROUP + i for j in range(size // GROUP)] for i in range(GROUP)]
        own = lax.psum(own, "dom", axis_index_groups=groups)
    back = swap(own)
    in_grad, in_done = conv(neighbors, mask_words, cotangent, cross, chip, weight, own, True)
    half = back.reshape(-1, TILE) + in_done[:1]
    other = exchange(half, 1, size)
    scale = float(size * leaves * voxels) ** -0.5
    return (out_features, in_grad, unpack(half, other, scale))


def solution(mesh):
    split = P(("scene", "dom"), None, None)
    flat = P(("scene", "dom"), None)
    return jax.shard_map(
        shards,
        mesh=mesh,
        in_specs=(split, split, P(), flat, flat),
        out_specs=(split, split, P("scene", None, None)),
        check_vma=False,
    )
```

time: 40.4 us -> 42.8 us (1.059)
  waiting for transfers between devices: 3.8 us -> 7.1 us
  starting transfers between devices: 16 us -> 12.9 us
  other arithmetic: 0.03 us -> 0.74 us
  local copies, waits for them, and re-layouts: 0.05 us -> 0.7 us
  Pallas kernels: 19.6 us -> 20.2 us
    ppermute x9 -> x3, starting transfers between devices: 15.4 us -> 4.62 us  [exchange(): return lax.ppermute(array, 'dom', [(i, i ^ mask) for i in range(size)])]
    all_to_all x0 -> x2, starting transfers between devices: none -> 7.6 us  [shards(): lax.all_to_all(parts, 'dom', 0, 0, axis_index_groups=line)]
    all_to_all x0 -> x2, waiting for transfers between devices: none -> 4.17 us  [shards(): lax.all_to_all(parts, 'dom', 0, 0, axis_index_groups=line)]
    pallas_call x4, Pallas kernels: 6.52 us -> 8.47 us  [the longest x1 3.61 us: grad_terms(): pl.pallas_call(grad_kernel, out_shape=jax.ShapeDtypeStruct((KROWS, 3 * CH...]
    pallas_call x2, Pallas kernels: 11.9 us -> 10.6 us  [conv(): pl.pallas_call(functools.partial(conv_kernel, turned), out_shape=(jax.Sha...]
    ppermute x9 -> x3, waiting for transfers between devices: 3.8 us -> 2.92 us  [exchange(): return lax.ppermute(array, 'dom', [(i, i ^ mask) for i in range(size)])]
    add x1 -> x2, other arithmetic: 0.03 us -> 0.74 us  [the longest x1 0.72 us: shards(): keep = (keep + exchange(send, 1, size)).reshape(4, -1, TILE)]
    unnamed x10 -> x12, local copies, waits for them, and re-layouts: 0.02 us -> 0.7 us
  transfers between devices with their start and end apart: 10 -> 6, of which waited for: 3 -> 4; matrix products, arithmetic and copies ran while one was open for 0% -> 0% of each run, Pallas kernels for 30% -> 33%
where the time goes in v3:
time: 42.8 us; the launch traced here: 42.4 us
  Pallas kernels  20.2 us (47%)
  starting transfers between devices  12.9 us (30%)
  waiting for transfers between devices  7.1 us (17%)
  other arithmetic  0.74 us (2%)
  between operations  0.73 us (2%)
  local copies, waits for them, and re-layouts  0.7 us (2%)
    pallas_call x2, Pallas kernels, conv(): pl.pallas_call(functools.partial(conv_kernel, turned), out_shape=(jax.Sha...  10.6 us
    all_to_all x2, starting transfers between devices, shards(): lax.all_to_all(parts, 'dom', 0, 0, axis_index_groups=line)  7.6 us
    ppermute x3, starting transfers between devices, exchange(): return lax.ppermute(array, 'dom', [(i, i ^ mask) for i in range(size)])  4.62 us
    all_to_all x2, waiting for transfers between devices, shards(): lax.all_to_all(parts, 'dom', 0, 0, axis_index_groups=line)  4.17 us
    pallas_call x1, Pallas kernels, grad_terms(): pl.pallas_call(grad_kernel, out_shape=jax.ShapeDtypeStruct((KROWS, 3 * CH...  3.61 us
    ppermute x3, waiting for transfers between devices, exchange(): return lax.ppermute(array, 'dom', [(i, i ^ mask) for i in range(size)])  2.92 us
    pallas_call x1, Pallas kernels, edges(): pl.pallas_call(edges_kernel, out_shape=(shape, shape), in_specs=[pl.Block...  2.19 us
    pallas_call x1, Pallas kernels, grad_far(): pl.pallas_call(grad_far_kernel, out_shape=(shape, shape), in_specs=[smem_...  1.97 us
  transfers between devices with their start and end apart: 6, of which 4 were waited for; matrix products, arithmetic and copies ran while one was open for 0% of the time, Pallas kernels for 33%

profile of v3, /device:TPU:0, one launch (start us, length us, event | category | flops | bytes accessed | tf_op | source)
XLA Modules:
  0.0 42.4 jit_solution(6776049671539370016)
XLA Ops:
  0.6 0.0 copy-start.2
  0.6 0.0 copy-start
  0.7 0.0 copy-start.1
  0.7 2.2 %edges.1 = (bf16[8,64,128]{2,1,0:T(8,128)(2,1)}, bf16[8,64,128]{2,1,0:T(8,128)(2,1)}) custom-call(s32[8,18]{1,0:T(8,128)} %words_ref.7, bf16[8,64,512]{2,1,0:T(8,128)(2,1)} %x_ref.4, bf16[8,64,512]{2,1,0:T(8,128)(2,1)} %x_ref.5), custom_call_target="tpu_custom_call" | custom-call | flops 1000000 | bytes 1000000 | tf_op jit(solution)/shard_map/edges/pallas_call | solution.py:82
  2.9 0.7 %collective-permute-start = (bf16[8,64,128]{2,1,0:T(8,128)(2,1)}, bf16[8,64,128]{2,1,0:T(8,128)(2,1)S(1)}, u32[]{:S(2)}, u32[]{:S(2)}) collective-permute-start(bf16[8,64,128]{2,1,0:T(8,128)(2,1)} %get-tuple-element.11), channel_id=1, source_target_pairs={{1,2},{3,4},{5,6},{2,1},{4,3},{6,5},{9,10},{11,12},{13,14},{10,9},... | collective-permute-start | bytes 393224 | tf_op jit(solution)/shard_map/ppermute | solution.py:505
  3.5 4.4 %collective-permute-start.1 = (bf16[8,64,128]{2,1,0:T(8,128)(2,1)}, bf16[8,64,128]{2,1,0:T(8,128)(2,1)S(1)}, u32[]{:S(2)}, u32[]{:S(2)}) collective-permute-start(bf16[8,64,128]{2,1,0:T(8,128)(2,1)} %get-tuple-element.12), channel_id=1, source_target_pairs={{0,1},{1,0},{2,3},{3,2},{4,5},{5,4},{6,7},{7,6},{8,9},{9,8},{10,11... | collective-permute-start | bytes 393224 | tf_op jit(solution)/shard_map/ppermute | solution.py:496
  8.0 0.0 copy-done.2
  8.0 0.0 copy-done
  8.0 0.0 copy-done.1
  8.0 0.0 copy-start.3
  8.0 0.7 %copy-done.3 = s32[8,26]{1,0:T(8,128)S(1)} copy-done((s32[8,26]{1,0:T(8,128)S(1)}, s32[8,26]{1,0:T(8,128)}, u32[]{:S(2)}) %copy-start.3) | copy-done | bytes 856
  8.7 3.6 %grad_terms.1.near_total = f32[576,192]{1,0:T(8,128)S(1)} custom-call(s32[8,26]{1,0:T(8,128)S(1)} %copy-done.3, s32[8,18]{1,0:T(8,128)S(1)} %copy-done.2, bf16[8,64,512]{2,1,0:T(8,128)(2,1)S(1)} %copy-done.1, bf16[8,64,512]{2,1,0:T(8,128)(2,1)S(1)} %copy-done), custom_call_target="tpu_custom_call" | custom-call | flops 1000000000 | bytes 2000000 | tf_op jit(solution)/shard_map/grad_terms/pallas_call | solution.py:247
  12.3 0.0 collective-permute-done.cross_ref
  12.3 0.0 collective-permute-done.1.chip_ref
  12.3 2.0 %grad_far.1 = (f32[448,128]{1,0:T(8,128)S(1)}, f32[448,128]{1,0:T(8,128)S(1)}) custom-call(s32[8,26]{1,0:T(8,128)S(1)} %copy-done.3, s32[8,18]{1,0:T(8,128)S(1)} %copy-done.2, bf16[8,64,512]{2,1,0:T(8,128)(2,1)S(1)} %copy-done, bf16[8,64,128]{2,1,0:T(8,128)(2,1)S(1)} %collective-permute-done.cross_ref, ...), custom_call_target="tpu_custom_call" | custom-call | flops 100000000 | bytes 2000000 | tf_op jit(solution)/shard_map/grad_far/pallas_call | solution.py:330
  14.3 0.1 collective-permute-start.2
  14.4 1.4 %collective-permute-done.2 = f32[448,128]{1,0:T(8,128)S(1)} collective-permute-done((f32[448,128]{1,0:T(8,128)S(1)}, f32[448,128]{1,0:T(8,128)S(1)}, u32[]{:S(2)}, u32[]{:S(2)}) %collective-permute-start.2) | collective-permute-done | bytes 229408 | tf_op jit(solution)/shard_map/ppermute | solution.py:496
  15.8 0.0 copy-start.5
  15.8 0.7 %add.13 = f32[448,128]{1,0:T(8,128)} add(f32[448,128]{1,0:T(8,128)S(1)} %get-tuple-element.13, f32[448,128]{1,0:T(8,128)S(1)} %collective-permute-done.2) | non-fusion elementwise | flops 57344 | bytes 688128 | tf_op jit(solution)/shard_map/add | solution.py:510
  16.6 0.0 copy-start.4
  16.6 4.0 %all-to-all-start = ((f32[4,112,128]{2,1,0:T(8,128)}), f32[4,112,128]{2,1,0:T(8,128)S(1)}, u32[]{:S(2)}, u32[]{:S(2)}) async-start(f32[4,112,128]{2,1,0:T(8,128)} %bitcast._), calls=%async_computation | async-start | bytes 458752 | tf_op jit(solution)/shard_map/all_to_all | solution.py:514
  20.5 0.0 copy-done.5
  20.6 0.0 copy-done.4
  20.6 5.4 %out_conv.1 = (bf16[8,64,512]{2,1,0:T(8,128)(2,1)}, f32[8,128]{1,0:T(8,128)S(1)}) custom-call(s32[8,26]{1,0:T(8,128)S(1)} %copy-done.4, s32[8,18]{1,0:T(8,128)S(1)} %copy-done.2, bf16[8,64,512]{2,1,0:T(8,128)(2,1)S(1)} %copy-done.1, bf16[8,64,128]{2,1,0:T(8,128)(2,1)S(1)} %collective-permute-done.cross_ref, ...), custom_call_target="tpu_custom_call" | custom-call | flops 2000000000 | bytes 2000000 | tf_op jit(solution)/shard_map/out_conv/pallas_call | solution.py:435
  26.0 3.1 %all-to-all-done.parts_ref = f32[4,112,128]{2,1,0:T(8,128)S(1)} async-done(((f32[4,112,128]{2,1,0:T(8,128)}), f32[4,112,128]{2,1,0:T(8,128)S(1)}, u32[]{:S(2)}, u32[]{:S(2)}) %all-to-all-start) | async-done | bytes 229408 | tf_op jit(solution)/shard_map/all_to_all | solution.py:514
  29.1 0.7 %sum_chunks.1._ = f32[4,112,128]{2,1,0:T(8,128)} custom-call(f32[4,112,128]{2,1,0:T(8,128)S(1)} %all-to-all-done.parts_ref, f32[8,128]{1,0:T(8,128)S(1)} %get-tuple-element.16._), custom_call_target="tpu_custom_call" | custom-call | flops 100000 | bytes 500000 | tf_op jit(solution)/shard_map/sum_chunks/pallas_call | solution.py:457
  29.8 3.6 %all-to-all-start.1 = ((f32[4,112,128]{2,1,0:T(8,128)}), f32[4,112,128]{2,1,0:T(8,128)S(1)}, u32[]{:S(2)}, u32[]{:S(2)}) async-start(f32[4,112,128]{2,1,0:T(8,128)} %sum_chunks.1._), calls=%async_computation.1 | async-start | bytes 458752 | tf_op jit(solution)/shard_map/all_to_all | solution.py:514
  33.4 5.2 %in_grad_conv.1 = (bf16[8,64,512]{2,1,0:T(8,128)(2,1)}, f32[8,128]{1,0:T(8,128)S(1)}) custom-call(s32[8,26]{1,0:T(8,128)S(1)} %copy-done.4, s32[8,18]{1,0:T(8,128)S(1)} %copy-done.2, bf16[8,64,512]{2,1,0:T(8,128)(2,1)S(1)} %copy-done, bf16[8,64,128]{2,1,0:T(8,128)(2,1)S(1)} %collective-permute-done.cross_ref, ...), custom_call_target="tpu_custom_call" | custom-call | flops 2000000000 | bytes 2000000 | tf_op jit(solution)/shard_map/in_grad_conv/pallas_call | solution.py:435
  38.6 1.1 %all-to-all-done.1 = f32[4,112,128]{2,1,0:T(8,128)S(1)} async-done(((f32[4,112,128]{2,1,0:T(8,128)}), f32[4,112,128]{2,1,0:T(8,128)S(1)}, u32[]{:S(2)}, u32[]{:S(2)}) %all-to-all-start.1) | async-done | bytes 229408 | tf_op jit(solution)/shard_map/all_to_all | solution.py:514
  39.7 0.1 collective-permute-start.3
  39.7 1.5 %collective-permute-done.3.other_ref = f32[448,128]{1,0:T(8,128)S(1)} collective-permute-done((f32[448,128]{1,0:T(8,128)S(1)}, f32[448,128]{1,0:T(8,128)S(1)}, u32[]{:S(2)}, u32[]{:S(2)}) %collective-permute-start.3) | collective-permute-done | bytes 229408 | tf_op jit(solution)/shard_map/ppermute | solution.py:496
  41.2 1.2 %unpack_grad.1 = f32[27,64,64]{2,1,0:T(8,128)} custom-call(f32[448,128]{1,0:T(8,128)S(1)} %bitcast_add_fusion.own_ref, f32[448,128]{1,0:T(8,128)S(1)} %collective-permute-done.3.other_ref), custom_call_target="tpu_custom_call" | custom-call | flops 1000000 | bytes 1000000 | tf_op jit(solution)/shard_map/unpack_grad/pallas_call | solution.py:483
  (2 shorter events, 0.0 us)
Async XLA Ops:
  0.6 7.3 %copy-start.2 = (s32[8,18]{1,0:T(8,128)S(1)}, s32[8,18]{1,0:T(8,128)}, u32[]{:S(2)}) copy-start(s32[8,18]{1,0:T(8,128)} %words_ref.7) | copy-start | bytes 1732
  0.6 7.3 %copy-start = (bf16[8,64,512]{2,1,0:T(8,128)(2,1)S(1)}, bf16[8,64,512]{2,1,0:T(8,128)(2,1)}, u32[]{:S(2)}) copy-start(bf16[8,64,512]{2,1,0:T(8,128)(2,1)} %x_ref.5) | copy-start | bytes 1572868
  0.7 7.3 %copy-start.1 = (bf16[8,64,512]{2,1,0:T(8,128)(2,1)S(1)}, bf16[8,64,512]{2,1,0:T(8,128)(2,1)}, u32[]{:S(2)}) copy-start(bf16[8,64,512]{2,1,0:T(8,128)(2,1)} %x_ref.4) | copy-start | bytes 1572868
  2.9 9.4 %collective-permute-start = (bf16[8,64,128]{2,1,0:T(8,128)(2,1)}, bf16[8,64,128]{2,1,0:T(8,128)(2,1)S(1)}, u32[]{:S(2)}, u32[]{:S(2)}) collective-permute-start(bf16[8,64,128]{2,1,0:T(8,128)(2,1)} %get-tuple-element.11), channel_id=1, source_target_pairs={{1,2},{3,4},{5,6},{2,1},{4,3},{6,5},{9,10},{11,12},{13,14},{10,9},... | collective-permute-start | bytes 393224 | tf_op jit(solution)/shard_map/ppermute | solution.py:505
  3.5 8.8 %collective-permute-start.1 = (bf16[8,64,128]{2,1,0:T(8,128)(2,1)}, bf16[8,64,128]{2,1,0:T(8,128)(2,1)S(1)}, u32[]{:S(2)}, u32[]{:S(2)}) collective-permute-start(bf16[8,64,128]{2,1,0:T(8,128)(2,1)} %get-tuple-element.12), channel_id=1, source_target_pairs={{0,1},{1,0},{2,3},{3,2},{4,5},{5,4},{6,7},{7,6},{8,9},{9,8},{10,11... | collective-permute-start | bytes 393224 | tf_op jit(solution)/shard_map/ppermute | solution.py:496
  8.0 0.7 %copy-start.3 = (s32[8,26]{1,0:T(8,128)S(1)}, s32[8,26]{1,0:T(8,128)}, u32[]{:S(2)}) copy-start(s32[8,26]{1,0:T(8,128)} %near_ref.7) | copy-start | bytes 2500
  14.3 1.6 %collective-permute-start.2 = (f32[448,128]{1,0:T(8,128)S(1)}, f32[448,128]{1,0:T(8,128)S(1)}, u32[]{:S(2)}, u32[]{:S(2)}) collective-permute-start(f32[448,128]{1,0:T(8,128)S(1)} %get-tuple-element.14), channel_id=1, source_target_pairs={{0,1},{1,0},{2,3},{3,2},{4,5},{5,4},{6,7},{7,6},{8,9},{9,8},{10,11... | collective-permute-start | bytes 688136 | tf_op jit(solution)/shard_map/ppermute | solution.py:496
  15.8 4.7 %copy-start.5 = (bf16[27,64,64]{2,1,0:T(8,128)(2,1)S(1)}, bf16[27,64,64]{2,1,0:T(8,128)(2,1)}, u32[]{:S(2)}) copy-start(bf16[27,64,64]{2,1,0:T(8,128)(2,1)} %w_ref.3) | copy-start | bytes 663556
  16.6 4.0 %copy-start.4 = (s32[8,26]{1,0:T(8,128)S(1)}, s32[8,26]{1,0:T(8,128)}, u32[]{:S(2)}) copy-start(s32[8,26]{1,0:T(8,128)} %near_ref.7) | copy-start | bytes 2500
  16.6 12.5 %all-to-all-start = ((f32[4,112,128]{2,1,0:T(8,128)}), f32[4,112,128]{2,1,0:T(8,128)S(1)}, u32[]{:S(2)}, u32[]{:S(2)}) async-start(f32[4,112,128]{2,1,0:T(8,128)} %bitcast._), calls=%async_computation | async-start | bytes 458752 | tf_op jit(solution)/shard_map/all_to_all | solution.py:514
  29.8 9.9 %all-to-all-start.1 = ((f32[4,112,128]{2,1,0:T(8,128)}), f32[4,112,128]{2,1,0:T(8,128)S(1)}, u32[]{:S(2)}, u32[]{:S(2)}) async-start(f32[4,112,128]{2,1,0:T(8,128)} %sum_chunks.1._), calls=%async_computation.1 | async-start | bytes 458752 | tf_op jit(solution)/shard_map/all_to_all | solution.py:514
  39.7 1.6 %collective-permute-start.3 = (f32[448,128]{1,0:T(8,128)S(1)}, f32[448,128]{1,0:T(8,128)S(1)}, u32[]{:S(2)}, u32[]{:S(2)}) collective-permute-start(f32[448,128]{1,0:T(8,128)S(1)} %bitcast_add_fusion.own_ref), channel_id=1, source_target_pairs={{0,1},{1,0},{2,3},{3,2},{4,5},{5,4},{6,7},{7,6},{8,9},{9,8},{10,11... | collective-permute-start | bytes 688136 | tf_op jit(solution)/shard_map/ppermute | solution.py:496

commit v4 on v3

--- a/solution.py
+++ b/solution.py
@@ -216,7 +216,7 @@
     return lax.dot_general(a, b, CONTRACT_LANES, preferred_element_type=F32)
 
 
-def grad_kernel(near_ref, words_ref, x_ref, d_ref, total, store):
+def grad_kernel(near_ref, words_ref, x_ref, d_ref, total, stack_ref, store):
     leaves = x_ref.shape[0]
     device = lax.axis_index("dom")
     words = words_ref[...]
@@ -224,6 +224,7 @@
     fill(store, x_ref, occ, None, False)
     for leaf in range(leaves):
         near_x = stacked(store, near_ref, leaf, 0, device, leaves, "near")
+        stack_ref[leaf] = near_x
         center = masked_field(d_ref, occ, leaf)
         wide = jnp.concatenate([shift_c(center, -r) for r in (-1, 0, 1)], axis=0)
         term = dot_lanes(near_x, wide)
@@ -246,9 +247,12 @@
     leaves = x.shape[0]
     return pl.pallas_call(
         grad_kernel,
-        out_shape=jax.ShapeDtypeStruct((KROWS, 3 * CH), F32),
+        out_shape=(
+            jax.ShapeDtypeStruct((KROWS, 3 * CH), F32),
+            jax.ShapeDtypeStruct((leaves, KROWS, 4 * TILE), BF),
+        ),
         in_specs=[smem_spec()] + [vmem_spec()] * 3,
-        out_specs=vmem_spec(),
+        out_specs=(vmem_spec(), vmem_spec()),
         scratch_shapes=[pltpu.VMEM((leaves + 1, CH, 4 * TILE), BF)],
         cost_estimate=cost(10**9, 2 * 10**6),
         compiler_params=params(),
@@ -256,67 +260,91 @@
     )(near, words, x, dy)
 
 
+def split_far(cross_ref, chip_ref, leaf):
+    first_core = lax.rem(lax.axis_index("dom"), 2) == 0
+    low = jnp.where(first_core, chip_ref[leaf], cross_ref[leaf])
+    high = jnp.where(first_core, cross_ref[leaf], chip_ref[leaf])
+    return low, high
+
+
 def grad_far_kernel(
-    near_ref, words_ref, d_ref, cross_ref, chip_ref, near_total, keep_ref, send_ref, store, total, packed
+    near_ref, words_ref, d_ref, cross_ref, chip_ref, near_total, keep_ref, send_ref, store, packed
 ):
     leaves = d_ref.shape[0]
     device = lax.axis_index("dom")
-    first_core = lax.rem(device, 2) == 0
     words = words_ref[...]
     occ_lo, occ_hi = occupancy_tile(words, 0), occupancy_tile(words, 3)
     left = lane_ids(CH) < FACE
     zero = jnp.zeros((CH, TILE), BF)
     for leaf in range(leaves):
-        low = jnp.where(first_core, chip_ref[leaf], cross_ref[leaf])
-        high = jnp.where(first_core, cross_ref[leaf], chip_ref[leaf])
-        store[leaf] = jnp.where(left, low, high)
-    store[leaves] = zero
-
-    def far_rows(leaf, z):
-        where = lambda p, q: place(near_ref, leaf, p, q, z, device, leaves, "far")
-        tiles = {q: [jnp.where(left, store[where(1, q)], store[where(-1, q)])] for q in (-1, 0, 1)}
+        low, high = split_far(cross_ref, chip_ref, leaf)
+        store[0, leaf], store[1, leaf] = low, high
+        store[2, leaf], store[3, leaf] = roll(low, FACE), roll(high, FACE)
+    for i in range(4):
+        store[i, leaves] = zero
+
+    def far_rows(p, one, two, z):
+        at = lambda leaf, q: place(near_ref, leaf, p, q, z, device, leaves, "far")
+        first, second = (0, 2) if p > 0 else (3, 1)
+        tiles = {
+            q: [jnp.where(left, store[first, at(one, q)], store[second, at(two, q)])]
+            for q in (-1, 0, 1)
+        }
         moved = moved_tiles(tiles)
-        after = [jnp.where(left, moved[q][0], zero) for q in (-1, 0, 1)]
-        before = [jnp.where(left, zero, moved[q][0]) for q in (-1, 0, 1)]
-        return jnp.concatenate(after + before, axis=0)
-
-    def end_planes(leaf):
-        low = d_ref[leaf, :, 0:TILE] * spread(occ_lo, leaf)
-        high = d_ref[leaf, :, 3 * TILE : 4 * TILE] * spread(occ_hi, leaf)
-        return roll(jnp.where(left, low, high), FACE)
-
-    def wide(leaf):
-        plane = end_planes(leaf)
+        return jnp.concatenate([moved[q][0] for q in (-1, 0, 1)], axis=0)
+
+    def end_plane(p, one, two):
+        if p > 0:
+            a, b = [d_ref[l, :, 3 * TILE :] * spread(occ_hi, l) for l in (one, two)]
+            return jnp.where(left, roll(a, FACE), b)
+        a, b = [d_ref[l, :, 0:TILE] * spread(occ_lo, l) for l in (one, two)]
+        return jnp.where(left, a, roll(b, FACE))
+
+    def wide(plane):
         cell = c_index()
         last = jnp.where(cell == EDGE - 1, zero, roll(plane, -1))
         first = jnp.where(cell == 0, zero, roll(plane, 1))
         return jnp.concatenate([last, plane, first], axis=0)
 
-    rows = jnp.concatenate([far_rows(leaf, 0) for leaf in range(leaves)], axis=1)
-    columns = jnp.concatenate([wide(leaf) for leaf in range(leaves)], axis=1)
-    term = dot_lanes(rows, columns)
-    total[...] = near_total[...]
-
-    def add(part, at):
-        for i, (p, q) in enumerate([(p, q) for p in (1, -1) for q in (-1, 0, 1)]):
+    pairs = [(leaf, leaf + 1) for leaf in range(0, leaves, 2)]
+    for index, (p, q) in enumerate(SHIFTS):
+        if p == 0:
+            row = index * CH
+            packed[row : row + CH, :] = near_total[row : row + CH, 0:TILE]
+            far, side = (KROWS + row, 0) if row < SPLIT else (KROWS + row - SPLIT, 1)
+            packed[far : far + CH, side * CH : (side + 1) * CH] = near_total[row : row + CH, TILE:]
+    for p in (-1, 1):
+        rows = jnp.concatenate([far_rows(p, a, b, 0) for a, b in pairs], axis=1)
+        columns = jnp.concatenate([wide(end_plane(p, a, b)) for a, b in pairs], axis=1)
+        term = dot_lanes(rows, columns)
+        for q in (-1, 0, 1):
             row = SHIFTS.index((p, q)) * CH
-            total[row : row + CH, at] += part[i * CH : (i + 1) * CH, :]
-
-    add(term, slice(0, 3 * CH))
+            block = near_total[row : row + CH, :] + term[(q + 1) * CH : (q + 2) * CH, :]
+            packed[row : row + CH, :] = block[:, 0:TILE]
+            far, side = (KROWS + row, 0) if row < SPLIT else (KROWS + row - SPLIT, 1)
+            packed[far : far + CH, side * CH : (side + 1) * CH] = block[:, TILE:]
+    packed[2 * KROWS - SPLIT :, CH:] = jnp.zeros((2 * SPLIT - KROWS, CH), F32)
+
     for z in (-1, 1):
         for leaf in range(leaves):
 
             @pl.when(listed(near_ref, leaf, z))
             def _():
-                plane = end_planes(leaf)
                 edge = c_index() == (0 if z > 0 else EDGE - 1)
-                edge = jnp.where(edge, roll(plane, -z * (EDGE - 1)), zero)
-                add(dot_lanes(far_rows(leaf, z), edge), slice((z + 1) * CH, (z + 2) * CH))
-
-    packed[0:KROWS, :] = total[:, 0:TILE]
-    packed[KROWS:, 0:CH] = total[0:SPLIT, TILE:]
-    packed[KROWS : 2 * KROWS - SPLIT, CH:] = total[SPLIT:, TILE:]
-    packed[2 * KROWS - SPLIT :, CH:] = jnp.zeros((2 * SPLIT - KROWS, CH), F32)
+                for p in (-1, 1):
+                    plane = jnp.where(left, end_plane(p, leaf, leaf), zero)
+                    plane = jnp.where(edge, roll(plane, -z * (EDGE - 1)), zero)
+                    term = dot_lanes(far_rows(p, leaf, leaf, z), plane)
+                    for q in (-1, 0, 1):
+                        row, side = SHIFTS.index((p, q)) * CH, 0
+                        if z > 0:
+                            row, side = (
+                                (KROWS + row, 0) if row < SPLIT else (KROWS + row - SPLIT, 1)
+                            )
+                        packed[row : row + CH, side * CH : (side + 1) * CH] += term[
+                            (q + 1) * CH : (q + 2) * CH, :
+                        ]
+
     core = lax.rem(device, 2)
     rows = packed.shape[0] // 2
     keep_ref[...] = packed[pl.ds(pl.multiple_of(core * rows, 8), rows), :]
@@ -333,8 +361,7 @@
         in_specs=[smem_spec()] + [vmem_spec()] * 5,
         out_specs=(vmem_spec(), vmem_spec()),
         scratch_shapes=[
-            pltpu.VMEM((leaves + 1, CH, TILE), BF),
-            pltpu.VMEM((KROWS, 3 * CH), F32),
+            pltpu.VMEM((4, leaves + 1, CH, TILE), BF),
             pltpu.VMEM((rows, TILE), F32),
         ],
         cost_estimate=cost(10**8, 2 * 10**6),
@@ -363,106 +390,201 @@
     return pl.CostEstimate(flops=flops, bytes_accessed=bytes_accessed, transcendentals=0)
 
 
-def conv_kernel(
-    turned, near_ref, words_ref, x_ref, cross_ref, chip_ref, w_ref, _, out_ref, done_ref, store
-):
-    leaves = x_ref.shape[0]
-    device = lax.axis_index("dom")
-    words = words_ref[...]
-    occ = [occupancy_tile(words, k) for k in range(4)]
-    fill(store, x_ref, occ, (cross_ref, chip_ref), turned)
-
+def ordered_taps(w_ref, turned):
     def tap(index, r):
         p, q = SHIFTS[index]
         return (p + 1) * 9 + (q + 1) * 3 + r + 1
 
     if turned:
-        taps = jnp.concatenate(
+        return jnp.concatenate(
             [
                 jnp.concatenate([w_ref[26 - tap(index, r)] for index in range(9)], axis=1)
                 for r in (-1, 0, 1)
             ],
             axis=0,
         )
-    else:
-        taps = jnp.concatenate(
-            [
-                jnp.concatenate([w_ref[tap(index, r)] for r in (-1, 0, 1)], axis=1)
-                for index in range(9)
-            ],
-            axis=0,
-        ).T
-    done_ref[...] = jnp.zeros(done_ref.shape, F32)
-
-    def masked(leaf, value):
-        return jnp.concatenate(
-            [
-                value[:, k * TILE : (k + 1) * TILE]
-                * jnp.broadcast_to(occ[k][leaf : leaf + 1, :], (CH, TILE))
-                for k in range(4)
-            ],
-            axis=1,
-        )
-
-    for leaf in range(leaves):
-        near_x = stacked(store, near_ref, leaf, 0, device, leaves)
-        wide = jnp.dot(taps, near_x, preferred_element_type=F32)
-        total = wide[CH : 2 * CH]
-        for r in (-1, 1):
-            total = total + shift_c(wide[(r + 1) * CH : (r + 2) * CH], r)
-        out_ref[leaf] = masked(leaf, total).astype(BF)
-
-    for leaf in range(leaves):
-
-        @pl.when(listed(near_ref, leaf, -1) | listed(near_ref, leaf, 1))
-        def _():
+    return jnp.concatenate(
+        [
+            jnp.concatenate([w_ref[tap(index, r)] for r in (-1, 0, 1)], axis=1)
+            for index in range(9)
+        ],
+        axis=0,
+    ).T
+
+
+def masked_sum(occ, leaf, value):
+    return jnp.concatenate(
+        [
+            value[:, k * TILE : (k + 1) * TILE]
+            * jnp.broadcast_to(occ[k][leaf : leaf + 1, :], (CH, TILE))
+            for k in range(4)
+        ],
+        axis=1,
+    ).astype(BF)
+
+
+def leaf_sum(taps, near_x):
+    wide = jnp.dot(taps, near_x, preferred_element_type=F32)
+    total = wide[CH : 2 * CH]
+    for r in (-1, 1):
+        total = total + shift_c(wide[(r + 1) * CH : (r + 2) * CH], r)
+    return total
+
+
+def third_dimension(near_ref, taps, occ, x_ref, cross_ref, chip_ref, turned, out_ref, store):
+    leaves = x_ref.shape[0]
+    device = lax.axis_index("dom")
+    found = [listed(near_ref, leaf, -1) | listed(near_ref, leaf, 1) for leaf in range(leaves)]
+
+    @pl.when(functools.reduce(jnp.logical_or, found))
+    def _():
+        fill(store, x_ref, occ, (cross_ref, chip_ref), turned)
+
+        def one(leaf, carry):
             near_x = stacked(store, near_ref, leaf, 0, device, leaves)
-            wide = jnp.dot(taps, near_x, preferred_element_type=F32)
-            total = wide[CH : 2 * CH]
-            for r in (-1, 1):
-                total = total + shift_c(wide[(r + 1) * CH : (r + 2) * CH], r)
+            total = leaf_sum(taps, near_x)
             for z in (-1, 1):
                 near_z = stacked(store, near_ref, leaf, z, device, leaves)
                 part = jnp.dot(
                     taps[(z + 1) * CH : (z + 2) * CH], near_z, preferred_element_type=F32
                 )
                 total = total + across_c(part, z)
-            out_ref[leaf] = masked(leaf, total).astype(BF)
-
-
-def conv(near, words, x, cross, chip, weight, after, turned):
+            out_ref[leaf] = masked_sum(occ, leaf, total)
+            return carry
+
+        for leaf in range(leaves):
+            one(leaf, 0)
+
+
+def out_kernel(
+    near_ref, words_ref, x_ref, d_ref, cross_ref, chip_ref, w_ref, stack_ref, _,
+    out_ref, stack_dy_ref, done_ref, store, far,
+):
+    leaves = x_ref.shape[0]
+    device = lax.axis_index("dom")
+    words = words_ref[...]
+    occ = [occupancy_tile(words, k) for k in range(4)]
+    done_ref[...] = jnp.zeros(done_ref.shape, F32)
+    left = lane_ids(CH) < FACE
+    zero = jnp.zeros((CH, TILE), BF)
+    taps = ordered_taps(w_ref, False)
+    fill(store, d_ref, occ, (cross_ref, chip_ref), True)
+    for leaf in range(leaves):
+        low, high = split_far(cross_ref, chip_ref, leaf)
+        far[leaf] = jnp.where(left, low, high)
+    far[leaves] = zero
+
+    def far_planes(leaf):
+        at = lambda p, q: place(near_ref, leaf, p, q, 0, device, leaves, "far")
+        tiles = {q: [jnp.where(left, far[at(1, q)], far[at(-1, q)])] for q in (-1, 0, 1)}
+        moved = moved_tiles(tiles)
+        return {q: roll(moved[q][0], FACE) for q in (-1, 0, 1)}
+
+    for leaf in range(leaves):
+        stack_dy_ref[leaf] = stacked(store, near_ref, leaf, 0, device, leaves)
+        planes = far_planes(leaf)
+        pieces = []
+        for index, (p, q) in enumerate(SHIFTS):
+            piece = stack_ref[leaf, index * CH : (index + 1) * CH, :]
+            parts = [piece[:, k * TILE : (k + 1) * TILE] for k in range(4)]
+            if p > 0:
+                parts[3] = parts[3] + jnp.where(left, zero, planes[q])
+            elif p < 0:
+                parts[0] = parts[0] + jnp.where(left, planes[q], zero)
+            pieces.append(jnp.concatenate(parts, axis=1))
+        total = leaf_sum(taps, jnp.concatenate(pieces, axis=0))
+        out_ref[leaf] = masked_sum(occ, leaf, total)
+    third_dimension(near_ref, taps, occ, x_ref, cross_ref, chip_ref, False, out_ref, store)
+
+
+def out_conv(near, words, x, dy, cross, chip, weight, stack, after):
     leaves = x.shape[0]
     return pl.pallas_call(
-        functools.partial(conv_kernel, turned),
-        out_shape=(jax.ShapeDtypeStruct(x.shape, BF), jax.ShapeDtypeStruct((8, TILE), F32)),
-        in_specs=[smem_spec()] + [vmem_spec()] * 5 + [any_spec()],
-        out_specs=(vmem_spec(), vmem_spec()),
+        out_kernel,
+        out_shape=(
+            jax.ShapeDtypeStruct(x.shape, BF),
+            jax.ShapeDtypeStruct(stack.shape, BF),
+            jax.ShapeDtypeStruct((8, TILE), F32),
+        ),
+        in_specs=[smem_spec()] + [vmem_spec()] * 7 + [any_spec()],
+        out_specs=(vmem_spec(),) * 3,
+        scratch_shapes=[
+            pltpu.VMEM((2 * leaves + 1, CH, 4 * TILE), BF),
+            pltpu.VMEM((leaves + 1, CH, TILE), BF),
+        ],
+        cost_estimate=cost(10**9, 2 * 10**6),
+        compiler_params=params(),
+        name="out_conv",
+    )(near, words, x, dy, cross, chip, weight, stack, after)
+
+
+def in_grad_kernel(
+    near_ref, words_ref, d_ref, cross_ref, chip_ref, w_ref, stack_ref, _, out_ref, done_ref, store
+):
+    leaves = d_ref.shape[0]
+    words = words_ref[...]
+    occ = [occupancy_tile(words, k) for k in range(4)]
+    done_ref[...] = jnp.zeros(done_ref.shape, F32)
+    taps = ordered_taps(w_ref, True)
+    for leaf in range(leaves):
+        out_ref[leaf] = masked_sum(occ, leaf, leaf_sum(taps, stack_ref[leaf]))
+    third_dimension(near_ref, taps, occ, d_ref, cross_ref, chip_ref, True, out_ref, store)
+
+
+def in_grad_conv(near, words, dy, cross, chip, weight, stack, after):
+    leaves = dy.shape[0]
+    return pl.pallas_call(
+        in_grad_kernel,
+        out_shape=(jax.ShapeDtypeStruct(dy.shape, BF), jax.ShapeDtypeStruct((8, TILE), F32)),
+        in_specs=[smem_spec()] + [vmem_spec()] * 6 + [any_spec()],
+        out_specs=(vmem_spec(),) * 2,
         scratch_shapes=[pltpu.VMEM((2 * leaves + 1, CH, 4 * TILE), BF)],
-        cost_estimate=cost(2 * 10**9, 2 * 10**6),
+        cost_estimate=cost(10**9, 2 * 10**6),
         compiler_params=params(),
-        name="in_grad_conv" if turned else "out_conv",
-    )(near, words, x, cross, chip, weight, after)
-
-
-def sum_kernel(parts_ref, _, out_ref):
-    parts = parts_ref.shape[0]
-    total = parts_ref[0]
-    for i in range(1, parts):
-        total = total + parts_ref[i]
-    for i in range(parts):
-        out_ref[i] = total
-
-
-def sum_chunks(parts, after):
+        name="in_grad_conv",
+    )(near, words, dy, cross, chip, weight, stack, after)
+
+
+def sum_kernel(own_ref, *refs):
+    *got_refs, _, out_ref = refs
+    total = own_ref[...]
+    for got_ref in got_refs:
+        total = total + got_ref[...]
+    out_ref[...] = total
+
+
+def sum_chunks(own, got, after):
     return pl.pallas_call(
         sum_kernel,
-        out_shape=jax.ShapeDtypeStruct(parts.shape, F32),
-        in_specs=[vmem_spec(), any_spec()],
+        out_shape=jax.ShapeDtypeStruct(own.shape, F32),
+        in_specs=[vmem_spec()] * (1 + len(got)) + [any_spec()],
+        out_specs=vmem_spec(),
+        cost_estimate=cost(10**5, 3 * 10**5),
+        compiler_params=params(),
+        name="sum_chunks",
+    )(own, *got, after)
+
+
+def join_kernel(*refs):
+    *parts, _, out_ref = refs
+    lane = lax.rem(lax.axis_index("dom") // 2, 4)
+    rows = parts[0].shape[0]
+    for mask, part in enumerate(parts):
+        at = pl.multiple_of(jnp.bitwise_xor(lane, mask) * rows, 8)
+        out_ref[pl.ds(at, rows), :] = part[...]
+
+
+def join_chunks(parts, after):
+    rows = parts[0].shape[0]
+    return pl.pallas_call(
+        join_kernel,
+        out_shape=jax.ShapeDtypeStruct((len(parts) * rows, TILE), F32),
+        in_specs=[vmem_spec()] * len(parts) + [any_spec()],
         out_specs=vmem_spec(),
         cost_estimate=cost(10**5, 5 * 10**5),
         compiler_params=params(),
-        name="sum_chunks",
-    )(parts, after)
+        name="join_chunks",
+    )(*parts, after)
 
 
 def unpack_kernel(scale, own_ref, other_ref, out_ref, total):
@@ -505,24 +627,27 @@
     cross = lax.ppermute(to_cross, "dom", between + [(j, i) for i, j in between])
     chip = exchange(to_chip, 1, size)
 
-    total = grad_terms(neighbors, mask_words, features, cotangent)
+    total, stack = grad_terms(neighbors, mask_words, features, cotangent)
     keep, send = grad_far(neighbors, mask_words, cotangent, cross, chip, total)
-    keep = (keep + exchange(send, 1, size)).reshape(4, -1, TILE)
-    line = [
-        [b + c + 2 * j for j in range(4)] for b in range(0, size, GROUP) for c in range(2)
-    ]
-    swap = lambda parts: lax.all_to_all(parts, "dom", 0, 0, axis_index_groups=line)
-    got = swap(keep)
-    out_features, out_done = conv(
-        neighbors, mask_words, features, cross, chip, weight, keep, False
+    keep = keep + exchange(send, 1, size)
+    rows = keep.shape[0] // 4
+    lane = (device // 2) % 4
+    chunk = lambda index: lax.dynamic_slice_in_dim(keep, index * rows, rows, axis=0)
+    to_send = [chunk(lane ^ m) for m in (1, 2, 3)]
+    own = chunk(lane)
+    got = [exchange(part, 2 * m, size) for m, part in zip((1, 2, 3), to_send)]
+    out_features, stack_dy, out_done = out_conv(
+        neighbors, mask_words, features, cotangent, cross, chip, weight, stack, to_send[2]
     )
-    own = sum_chunks(got, out_done)
+    own = sum_chunks(own, got, out_done)
     if size > GROUP:
         groups = [[j * GROUP + i for j in range(size // GROUP)] for i in range(GROUP)]
         own = lax.psum(own, "dom", axis_index_groups=groups)
-    back = swap(own)
-    in_grad, in_done = conv(neighbors, mask_words, cotangent, cross, chip, weight, own, True)
-    half = back.reshape(-1, TILE) + in_done[:1]
+    back = [exchange(own, 2 * m, size) for m in (1, 2, 3)]
+    in_grad, in_done = in_grad_conv(
+        neighbors, mask_words, cotangent, cross, chip, weight, stack_dy, own
+    )
+    half = join_chunks([own] + back, in_done)
     other = exchange(half, 1, size)
     scale = float(size * leaves * voxels) ** -0.5
     return (out_features, in_grad, unpack(half, other, scale))

time: 42.8 us -> 46.4 us (1.084)
  local copies, waits for them, and re-layouts: 0.7 us -> 8.65 us
  waiting for transfers between devices: 7.1 us -> 4.01 us
  Pallas kernels: 20.2 us -> 18.4 us
  starting transfers between devices: 12.9 us -> 14.2 us
  other arithmetic: 0.74 us -> 0.03 us
    ppermute x3 -> x9, starting transfers between devices: 4.62 us -> 13.5 us  [exchange(): return lax.ppermute(array, 'dom', [(i, i ^ mask) for i in range(size)])]
    unnamed x12 -> x24, local copies, waits for them, and re-layouts: 0.7 us -> 8.62 us
    all_to_all x2 -> x0, starting transfers between devices: 7.6 us -> none  [shards(): lax.all_to_all(parts, 'dom', 0, 0, axis_index_groups=line)]
    all_to_all x2 -> x0, waiting for transfers between devices: 4.17 us -> none  [shards(): lax.all_to_all(parts, 'dom', 0, 0, axis_index_groups=line)]
    pallas_call x4 -> x5, Pallas kernels: 14.9 us -> 13.1 us  [the longest x1 6.3 us: out_conv(): pl.pallas_call(out_kernel, out_shape=(jax.ShapeDtypeStruct(x.shape, BF),...]
    ppermute x3 -> x9, waiting for transfers between devices: 2.92 us -> 4.01 us  [exchange(): return lax.ppermute(array, 'dom', [(i, i ^ mask) for i in range(size)])]
    add x2 -> x1, other arithmetic: 0.74 us -> 0.03 us  [shards(): keep = keep + exchange(send, 1, size)]
  transfers between devices with their start and end apart: 6 -> 10, of which waited for: 4 -> 3; matrix products, arithmetic and copies ran while one was open for 0% -> 0% of each run, Pallas kernels for 33% -> 28%
where the time goes in v4:
time: 46.4 us; the launch traced here: 46.1 us
  Pallas kernels  18.4 us (40%)
  starting transfers between devices  14.2 us (31%)
  local copies, waits for them, and re-layouts  8.65 us (19%)
  waiting for transfers between devices  4.01 us (9%)
  between operations  0.81 us (2%)
    ppermute x9, starting transfers between devices, exchange(): return lax.ppermute(array, 'dom', [(i, i ^ mask) for i in range(size)])  13.5 us
    unnamed x24, local copies, waits for them, and re-layouts  8.62 us
    pallas_call x1, Pallas kernels, out_conv(): pl.pallas_call(out_kernel, out_shape=(jax.ShapeDtypeStruct(x.shape, BF),...  6.3 us
    ppermute x9, waiting for transfers between devices, exchange(): return lax.ppermute(array, 'dom', [(i, i ^ mask) for i in range(size)])  4.01 us
    pallas_call x1, Pallas kernels, grad_terms(): pl.pallas_call(grad_kernel, out_shape=(jax.ShapeDtypeStruct((KROWS, 3 * C...  3.64 us
    pallas_call x1, Pallas kernels, in_grad_conv(): pl.pallas_call(in_grad_kernel, out_shape=(jax.ShapeDtypeStruct(dy.shape,...  3.16 us
    pallas_call x1, Pallas kernels, edges(): pl.pallas_call(edges_kernel, out_shape=(shape, shape), in_specs=[pl.Block...  2.18 us
    pallas_call x1, Pallas kernels, grad_far(): pl.pallas_call(grad_far_kernel, out_shape=(shape, shape), in_specs=[smem_...  1.89 us
  transfers between devices with their start and end apart: 10, of which 3 were waited for; matrix products, arithmetic and copies ran while one was open for 0% of the time, Pallas kernels for 28%

profile of v4, /device:TPU:0, one launch (start us, length us, event | category | flops | bytes accessed | tf_op | source)
XLA Modules:
  0.0 46.1 jit_solution(6097333923017139996)
XLA Ops:
  0.6 0.0 copy-start.5
  0.6 0.0 copy-start.1
  0.7 0.0 copy-start.8
  0.7 2.2 %edges.1 = (bf16[8,64,128]{2,1,0:T(8,128)(2,1)}, bf16[8,64,128]{2,1,0:T(8,128)(2,1)}) custom-call(s32[8,18]{1,0:T(8,128)} %words_ref.7, bf16[8,64,512]{2,1,0:T(8,128)(2,1)} %x_ref.3, bf16[8,64,512]{2,1,0:T(8,128)(2,1)} %d_ref.7), custom_call_target="tpu_custom_call" | custom-call | flops 1000000 | bytes 1000000 | tf_op jit(solution)/shard_map/edges/pallas_call | solution.py:82
  2.9 0.7 %collective-permute-start = (bf16[8,64,128]{2,1,0:T(8,128)(2,1)}, bf16[8,64,128]{2,1,0:T(8,128)(2,1)S(1)}, u32[]{:S(2)}, u32[]{:S(2)}) collective-permute-start(bf16[8,64,128]{2,1,0:T(8,128)(2,1)} %get-tuple-element.14), channel_id=1, source_target_pairs={{1,2},{3,4},{5,6},{2,1},{4,3},{6,5},{9,10},{11,12},{13,14},{10,9},... | collective-permute-start | bytes 393224 | tf_op jit(solution)/shard_map/ppermute | solution.py:627
  3.5 4.4 %collective-permute-start.1 = (bf16[8,64,128]{2,1,0:T(8,128)(2,1)}, bf16[8,64,128]{2,1,0:T(8,128)(2,1)S(1)}, u32[]{:S(2)}, u32[]{:S(2)}) collective-permute-start(bf16[8,64,128]{2,1,0:T(8,128)(2,1)} %get-tuple-element.15), channel_id=1, source_target_pairs={{0,1},{1,0},{2,3},{3,2},{4,5},{5,4},{6,7},{7,6},{8,9},{9,8},{10,11... | collective-permute-start | bytes 393224 | tf_op jit(solution)/shard_map/ppermute | solution.py:618
  8.0 0.0 copy-start
  8.0 1.0 %copy-done = bf16[8,64,512]{2,1,0:T(8,128)(2,1)S(1)} copy-done((bf16[8,64,512]{2,1,0:T(8,128)(2,1)S(1)}, bf16[8,64,512]{2,1,0:T(8,128)(2,1)}, u32[]{:S(2)}) %copy-start) | copy-done | bytes 524312
  9.0 0.0 copy-start.4
  9.0 1.0 %copy-done.4 = bf16[8,64,512]{2,1,0:T(8,128)(2,1)S(1)} copy-done((bf16[8,64,512]{2,1,0:T(8,128)(2,1)S(1)}, bf16[8,64,512]{2,1,0:T(8,128)(2,1)}, u32[]{:S(2)}) %copy-start.4) | copy-done | bytes 524312
  10.1 0.0 copy-start.7
  10.1 0.7 %copy-done.7 = s32[8,18]{1,0:T(8,128)S(1)} copy-done((s32[8,18]{1,0:T(8,128)S(1)}, s32[8,18]{1,0:T(8,128)}, u32[]{:S(2)}) %copy-start.7) | copy-done | bytes 600
  10.7 0.0 copy-start.9
  10.8 0.7 %copy-done.9 = s32[8,26]{1,0:T(8,128)S(1)} copy-done((s32[8,26]{1,0:T(8,128)S(1)}, s32[8,26]{1,0:T(8,128)}, u32[]{:S(2)}) %copy-start.9) | copy-done | bytes 856
  11.4 0.0 copy-start.6
  11.4 0.0 copy-start.11
  11.4 3.6 %grad_terms.1 = (f32[576,192]{1,0:T(8,128)S(1)}, bf16[8,576,512]{2,1,0:T(8,128)(2,1)S(1)}) custom-call(s32[8,26]{1,0:T(8,128)S(1)} %copy-done.9, s32[8,18]{1,0:T(8,128)S(1)} %copy-done.7, bf16[8,64,512]{2,1,0:T(8,128)(2,1)S(1)} %copy-done.4, bf16[8,64,512]{2,1,0:T(8,128)(2,1)S(1)} %copy-done), custom_call_target="tpu_custom_call" | custom-call | flops 1000000000 | bytes 2000000 | tf_op jit(solution)/shard_map/grad_terms/pallas_call | solution.py:248
  15.1 0.0 copy-start.2
  15.1 2.1 %copy-done.2 = bf16[8,576,512]{2,1,0:T(8,128)(2,1)} copy-done((bf16[8,576,512]{2,1,0:T(8,128)(2,1)}, bf16[8,576,512]{2,1,0:T(8,128)(2,1)S(1)}, u32[]{:S(2)}) %copy-start.2) | copy-done | bytes 4718616
  17.2 0.0 collective-permute-done.cross_ref
  17.2 0.0 collective-permute-done.1.chip_ref
  17.2 0.0 copy-done.1
  17.2 0.0 copy-start.10
  17.3 0.7 %copy-done.10 = s32[8,26]{1,0:T(8,128)S(1)} copy-done((s32[8,26]{1,0:T(8,128)S(1)}, s32[8,26]{1,0:T(8,128)}, u32[]{:S(2)}) %copy-start.10) | copy-done | bytes 856
  17.9 1.9 %grad_far.1 = (f32[448,128]{1,0:T(8,128)S(1)}, f32[448,128]{1,0:T(8,128)S(1)}) custom-call(s32[8,26]{1,0:T(8,128)S(1)} %copy-done.10, s32[8,18]{1,0:T(8,128)S(1)} %copy-done.7, bf16[8,64,512]{2,1,0:T(8,128)(2,1)S(1)} %copy-done.1, bf16[8,64,128]{2,1,0:T(8,128)(2,1)S(1)} %collective-permute-done.cross_ref, ...), custom_call_target="tpu_custom_call" | custom-call | flops 100000000 | bytes 2000000 | tf_op jit(solution)/shard_map/grad_far/pallas_call | solution.py:358
  19.8 0.1 collective-permute-start.2
  20.0 1.4 %collective-permute-done.2 = f32[448,128]{1,0:T(8,128)S(1)} collective-permute-done((f32[448,128]{1,0:T(8,128)S(1)}, f32[448,128]{1,0:T(8,128)S(1)}, u32[]{:S(2)}, u32[]{:S(2)}) %collective-permute-start.2) | collective-permute-done | bytes 229408 | tf_op jit(solution)/shard_map/ppermute | solution.py:618
  21.5 1.6 %collective-permute-start.3 = (f32[112,128]{1,0:T(8,128)S(1)}, f32[112,128]{1,0:T(8,128)S(1)}, u32[]{:S(2)}, u32[]{:S(2)}) collective-permute-start(f32[112,128]{1,0:T(8,128)S(1)} %get-tuple-element.26), channel_id=1, source_target_pairs={{0,2},{1,3},{2,0},{3,1},{4,6},{5,7},{6,4},{7,5},{8,10},{9,11},{10,... | collective-permute-start | bytes 172040 | tf_op jit(solution)/shard_map/ppermute | solution.py:618
  23.1 1.1 %collective-permute-start.4 = (f32[112,128]{1,0:T(8,128)S(1)}, f32[112,128]{1,0:T(8,128)S(1)}, u32[]{:S(2)}, u32[]{:S(2)}) collective-permute-start(f32[112,128]{1,0:T(8,128)S(1)} %get-tuple-element.25), channel_id=1, source_target_pairs={{0,4},{1,5},{2,6},{3,7},{4,0},{5,1},{6,2},{7,3},{8,12},{9,13},{10,... | collective-permute-start | bytes 172040 | tf_op jit(solution)/shard_map/ppermute | solution.py:618
  24.2 1.7 %collective-permute-start.5 = (f32[112,128]{1,0:T(8,128)S(1)}, f32[112,128]{1,0:T(8,128)S(1)}, u32[]{:S(2)}, u32[]{:S(2)}) collective-permute-start(f32[112,128]{1,0:T(8,128)S(1)} %get-tuple-element.28._), channel_id=1, source_target_pairs={{0,6},{1,7},{2,4},{3,5},{4,2},{5,3},{6,0},{7,1},{8,14},{9,15},{10,... | collective-permute-start | bytes 172040 | tf_op jit(solution)/shard_map/ppermute | solution.py:618
  25.9 0.0 copy-done.5
  25.9 0.0 copy-done.8
  25.9 0.0 copy-done.6
  25.9 0.0 copy-done.11
  25.9 0.0 copy-start.3
  25.9 2.3 %copy-done.3 = bf16[8,576,512]{2,1,0:T(8,128)(2,1)S(1)} copy-done((bf16[8,576,512]{2,1,0:T(8,128)(2,1)S(1)}, bf16[8,576,512]{2,1,0:T(8,128)(2,1)}, u32[]{:S(2)}) %copy-start.3) | copy-done | bytes 4718616
  28.3 6.3 %out_conv.1 = (bf16[8,64,512]{2,1,0:T(8,128)(2,1)}, bf16[8,576,512]{2,1,0:T(8,128)(2,1)S(1)}, f32[8,128]{1,0:T(8,128)S(1)}) custom-call(s32[8,26]{1,0:T(8,128)S(1)} %copy-done.11, s32[8,18]{1,0:T(8,128)S(1)} %copy-done.8, bf16[8,64,512]{2,1,0:T(8,128)(2,1)S(1)} %copy-done.5, bf16[8,64,512]{2,1,0:T(8,128)(2,1)S(1)} %copy-done.1, ...), custom_call_target="tpu_custom_call" | custom-call | flops 1000000000 | bytes 2000000 | tf_op jit(solution)/shard_map/out_conv/pallas_call | solution.py:502
  34.6 0.0 collective-permute-done.3.refs_0_
  34.6 0.0 collective-permute-done.4.refs_1_
  34.6 0.0 collective-permute-done.5.refs_2_
  34.6 0.7 %collective-permute-start.6 = (f32[112,128]{1,0:T(8,128)S(1)}, f32[112,128]{1,0:T(8,128)S(1)}, u32[]{:S(2)}, u32[]{:S(2)}) collective-permute-start(f32[112,128]{1,0:T(8,128)S(1)} %sum_chunks.1._.refs_0_), channel_id=1, source_target_pairs={{0,2},{1,3},{2,0},{3,1},{4,6},{5,7},{6,4},{7,5},{8,10},{9,11},{10,... | collective-permute-start | bytes 172040 | tf_op jit(solution)/shard_map/ppermute | solution.py:618
  35.3 2.0 %collective-permute-start.7 = (f32[112,128]{1,0:T(8,128)S(1)}, f32[112,128]{1,0:T(8,128)S(1)}, u32[]{:S(2)}, u32[]{:S(2)}) collective-permute-start(f32[112,128]{1,0:T(8,128)S(1)} %sum_chunks.1._.refs_0_), channel_id=1, source_target_pairs={{0,4},{1,5},{2,6},{3,7},{4,0},{5,1},{6,2},{7,3},{8,12},{9,13},{10,... | collective-permute-start | bytes 172040 | tf_op jit(solution)/shard_map/ppermute | solution.py:618
  37.3 1.7 %collective-permute-start.8 = (f32[112,128]{1,0:T(8,128)S(1)}, f32[112,128]{1,0:T(8,128)S(1)}, u32[]{:S(2)}, u32[]{:S(2)}) collective-permute-start(f32[112,128]{1,0:T(8,128)S(1)} %sum_chunks.1._.refs_0_), channel_id=1, source_target_pairs={{0,6},{1,7},{2,4},{3,5},{4,2},{5,3},{6,0},{7,1},{8,14},{9,15},{10,... | collective-permute-start | bytes 172040 | tf_op jit(solution)/shard_map/ppermute | solution.py:618
  39.0 3.2 %in_grad_conv.1 = (bf16[8,64,512]{2,1,0:T(8,128)(2,1)}, f32[8,128]{1,0:T(8,128)S(1)}) custom-call(s32[8,26]{1,0:T(8,128)S(1)} %copy-done.11, s32[8,18]{1,0:T(8,128)S(1)} %copy-done.8, bf16[8,64,512]{2,1,0:T(8,128)(2,1)S(1)} %copy-done.1, bf16[8,64,128]{2,1,0:T(8,128)(2,1)S(1)} %collective-permute-done.cross_ref, ...), custom_call_target="tpu_custom_call" | custom-call | flops 1000000000 | bytes 2000000 | tf_op jit(solution)/shard_map/in_grad_conv/pallas_call | solution.py:536
  42.2 0.0 collective-permute-done.6.refs_1_
  42.2 0.0 collective-permute-done.7.refs_2_
  42.2 1.1 %collective-permute-done.8.refs_3_ = f32[112,128]{1,0:T(8,128)S(1)} collective-permute-done((f32[112,128]{1,0:T(8,128)S(1)}, f32[112,128]{1,0:T(8,128)S(1)}, u32[]{:S(2)}, u32[]{:S(2)}) %collective-permute-start.8) | collective-permute-done | bytes 57376 | tf_op jit(solution)/shard_map/ppermute | solution.py:618
  43.3 0.1 collective-permute-start.9
  43.4 1.5 %collective-permute-done.9.other_ref = f32[448,128]{1,0:T(8,128)S(1)} collective-permute-done((f32[448,128]{1,0:T(8,128)S(1)}, f32[448,128]{1,0:T(8,128)S(1)}, u32[]{:S(2)}, u32[]{:S(2)}) %collective-permute-start.9) | collective-permute-done | bytes 229408 | tf_op jit(solution)/shard_map/ppermute | solution.py:618
  44.9 1.2 %unpack_grad.1 = f32[27,64,64]{2,1,0:T(8,128)} custom-call(f32[448,128]{1,0:T(8,128)S(1)} %join_chunks.1.own_ref, f32[448,128]{1,0:T(8,128)S(1)} %collective-permute-done.9.other_ref), custom_call_target="tpu_custom_call" | custom-call | flops 1000000 | bytes 1000000 | tf_op jit(solution)/shard_map/unpack_grad/pallas_call | solution.py:605
  (4 shorter events, 0.1 us)
Async XLA Ops:
  0.6 25.3 %copy-start.5 = (bf16[8,64,512]{2,1,0:T(8,128)(2,1)S(1)}, bf16[8,64,512]{2,1,0:T(8,128)(2,1)}, u32[]{:S(2)}) copy-start(bf16[8,64,512]{2,1,0:T(8,128)(2,1)} %x_ref.3) | copy-start | bytes 1572868
  0.6 16.6 %copy-start.1 = (bf16[8,64,512]{2,1,0:T(8,128)(2,1)S(1)}, bf16[8,64,512]{2,1,0:T(8,128)(2,1)}, u32[]{:S(2)}) copy-start(bf16[8,64,512]{2,1,0:T(8,128)(2,1)} %d_ref.7) | copy-start | bytes 1572868
  0.7 25.3 %copy-start.8 = (s32[8,18]{1,0:T(8,128)S(1)}, s32[8,18]{1,0:T(8,128)}, u32[]{:S(2)}) copy-start(s32[8,18]{1,0:T(8,128)} %words_ref.7) | copy-start | bytes 1732
  2.9 14.4 %collective-permute-start = (bf16[8,64,128]{2,1,0:T(8,128)(2,1)}, bf16[8,64,128]{2,1,0:T(8,128)(2,1)S(1)}, u32[]{:S(2)}, u32[]{:S(2)}) collective-permute-start(bf16[8,64,128]{2,1,0:T(8,128)(2,1)} %get-tuple-element.14), channel_id=1, source_target_pairs={{1,2},{3,4},{5,6},{2,1},{4,3},{6,5},{9,10},{11,12},{13,14},{10,9},... | collective-permute-start | bytes 393224 | tf_op jit(solution)/shard_map/ppermute | solution.py:627
  3.5 13.7 %collective-permute-start.1 = (bf16[8,64,128]{2,1,0:T(8,128)(2,1)}, bf16[8,64,128]{2,1,0:T(8,128)(2,1)S(1)}, u32[]{:S(2)}, u32[]{:S(2)}) collective-permute-start(bf16[8,64,128]{2,1,0:T(8,128)(2,1)} %get-tuple-element.15), channel_id=1, source_target_pairs={{0,1},{1,0},{2,3},{3,2},{4,5},{5,4},{6,7},{7,6},{8,9},{9,8},{10,11... | collective-permute-start | bytes 393224 | tf_op jit(solution)/shard_map/ppermute | solution.py:618
  8.0 1.0 %copy-start = (bf16[8,64,512]{2,1,0:T(8,128)(2,1)S(1)}, bf16[8,64,512]{2,1,0:T(8,128)(2,1)}, u32[]{:S(2)}) copy-start(bf16[8,64,512]{2,1,0:T(8,128)(2,1)} %d_ref.7) | copy-start | bytes 1572868
  9.0 1.0 %copy-start.4 = (bf16[8,64,512]{2,1,0:T(8,128)(2,1)S(1)}, bf16[8,64,512]{2,1,0:T(8,128)(2,1)}, u32[]{:S(2)}) copy-start(bf16[8,64,512]{2,1,0:T(8,128)(2,1)} %x_ref.3) | copy-start | bytes 1572868
  10.1 0.7 %copy-start.7 = (s32[8,18]{1,0:T(8,128)S(1)}, s32[8,18]{1,0:T(8,128)}, u32[]{:S(2)}) copy-start(s32[8,18]{1,0:T(8,128)} %words_ref.7) | copy-start | bytes 1732
  10.7 0.7 %copy-start.9 = (s32[8,26]{1,0:T(8,128)S(1)}, s32[8,26]{1,0:T(8,128)}, u32[]{:S(2)}) copy-start(s32[8,26]{1,0:T(8,128)} %near_ref.7) | copy-start | bytes 2500
  11.4 14.5 %copy-start.6 = (bf16[27,64,64]{2,1,0:T(8,128)(2,1)S(1)}, bf16[27,64,64]{2,1,0:T(8,128)(2,1)}, u32[]{:S(2)}) copy-start(bf16[27,64,64]{2,1,0:T(8,128)(2,1)} %w_ref.3) | copy-start | bytes 663556
  11.4 14.5 %copy-start.11 = (s32[8,26]{1,0:T(8,128)S(1)}, s32[8,26]{1,0:T(8,128)}, u32[]{:S(2)}) copy-start(s32[8,26]{1,0:T(8,128)} %near_ref.7) | copy-start | bytes 2500
  15.1 2.1 %copy-start.2 = (bf16[8,576,512]{2,1,0:T(8,128)(2,1)}, bf16[8,576,512]{2,1,0:T(8,128)(2,1)S(1)}, u32[]{:S(2)}) copy-start(bf16[8,576,512]{2,1,0:T(8,128)(2,1)S(1)} %get-tuple-element.16.stack_ref) | copy-start | bytes 14155780
  17.2 0.7 %copy-start.10 = (s32[8,26]{1,0:T(8,128)S(1)}, s32[8,26]{1,0:T(8,128)}, u32[]{:S(2)}) copy-start(s32[8,26]{1,0:T(8,128)} %near_ref.7) | copy-start | bytes 2500
  19.8 1.6 %collective-permute-start.2 = (f32[448,128]{1,0:T(8,128)S(1)}, f32[448,128]{1,0:T(8,128)S(1)}, u32[]{:S(2)}, u32[]{:S(2)}) collective-permute-start(f32[448,128]{1,0:T(8,128)S(1)} %get-tuple-element.19), channel_id=1, source_target_pairs={{0,1},{1,0},{2,3},{3,2},{4,5},{5,4},{6,7},{7,6},{8,9},{9,8},{10,11... | collective-permute-start | bytes 688136 | tf_op jit(solution)/shard_map/ppermute | solution.py:618
  21.5 13.1 %collective-permute-start.3 = (f32[112,128]{1,0:T(8,128)S(1)}, f32[112,128]{1,0:T(8,128)S(1)}, u32[]{:S(2)}, u32[]{:S(2)}) collective-permute-start(f32[112,128]{1,0:T(8,128)S(1)} %get-tuple-element.26), channel_id=1, source_target_pairs={{0,2},{1,3},{2,0},{3,1},{4,6},{5,7},{6,4},{7,5},{8,10},{9,11},{10,... | collective-permute-start | bytes 172040 | tf_op jit(solution)/shard_map/ppermute | solution.py:618
  23.1 11.5 %collective-permute-start.4 = (f32[112,128]{1,0:T(8,128)S(1)}, f32[112,128]{1,0:T(8,128)S(1)}, u32[]{:S(2)}, u32[]{:S(2)}) collective-permute-start(f32[112,128]{1,0:T(8,128)S(1)} %get-tuple-element.25), channel_id=1, source_target_pairs={{0,4},{1,5},{2,6},{3,7},{4,0},{5,1},{6,2},{7,3},{8,12},{9,13},{10,... | collective-permute-start | bytes 172040 | tf_op jit(solution)/shard_map/ppermute | solution.py:618
  24.2 10.4 %collective-permute-start.5 = (f32[112,128]{1,0:T(8,128)S(1)}, f32[112,128]{1,0:T(8,128)S(1)}, u32[]{:S(2)}, u32[]{:S(2)}) collective-permute-start(f32[112,128]{1,0:T(8,128)S(1)} %get-tuple-element.28._), channel_id=1, source_target_pairs={{0,6},{1,7},{2,4},{3,5},{4,2},{5,3},{6,0},{7,1},{8,14},{9,15},{10,... | collective-permute-start | bytes 172040 | tf_op jit(solution)/shard_map/ppermute | solution.py:618
  25.9 2.3 %copy-start.3 = (bf16[8,576,512]{2,1,0:T(8,128)(2,1)S(1)}, bf16[8,576,512]{2,1,0:T(8,128)(2,1)}, u32[]{:S(2)}) copy-start(bf16[8,576,512]{2,1,0:T(8,128)(2,1)} %copy-done.2) | copy-start | bytes 14155780
  34.6 7.6 %collective-permute-start.6 = (f32[112,128]{1,0:T(8,128)S(1)}, f32[112,128]{1,0:T(8,128)S(1)}, u32[]{:S(2)}, u32[]{:S(2)}) collective-permute-start(f32[112,128]{1,0:T(8,128)S(1)} %sum_chunks.1._.refs_0_), channel_id=1, source_target_pairs={{0,2},{1,3},{2,0},{3,1},{4,6},{5,7},{6,4},{7,5},{8,10},{9,11},{10,... | collective-permute-start | bytes 172040 | tf_op jit(solution)/shard_map/ppermute | solution.py:618
  35.3 6.9 %collective-permute-start.7 = (f32[112,128]{1,0:T(8,128)S(1)}, f32[112,128]{1,0:T(8,128)S(1)}, u32[]{:S(2)}, u32[]{:S(2)}) collective-permute-start(f32[112,128]{1,0:T(8,128)S(1)} %sum_chunks.1._.refs_0_), channel_id=1, source_target_pairs={{0,4},{1,5},{2,6},{3,7},{4,0},{5,1},{6,2},{7,3},{8,12},{9,13},{10,... | collective-permute-start | bytes 172040 | tf_op jit(solution)/shard_map/ppermute | solution.py:618
  37.3 6.0 %collective-permute-start.8 = (f32[112,128]{1,0:T(8,128)S(1)}, f32[112,128]{1,0:T(8,128)S(1)}, u32[]{:S(2)}, u32[]{:S(2)}) collective-permute-start(f32[112,128]{1,0:T(8,128)S(1)} %sum_chunks.1._.refs_0_), channel_id=1, source_target_pairs={{0,6},{1,7},{2,4},{3,5},{4,2},{5,3},{6,0},{7,1},{8,14},{9,15},{10,... | collective-permute-start | bytes 172040 | tf_op jit(solution)/shard_map/ppermute | solution.py:618
  43.3 1.6 %collective-permute-start.9 = (f32[448,128]{1,0:T(8,128)S(1)}, f32[448,128]{1,0:T(8,128)S(1)}, u32[]{:S(2)}, u32[]{:S(2)}) collective-permute-start(f32[448,128]{1,0:T(8,128)S(1)} %join_chunks.1.own_ref), channel_id=1, source_target_pairs={{0,1},{1,0},{2,3},{3,2},{4,5},{5,4},{6,7},{7,6},{8,9},{9,8},{10,11... | collective-permute-start | bytes 688136 | tf_op jit(solution)/shard_map/ppermute | solution.py:618

commit v5 on v4

v5 whole, which is shorter than its diff:
```python
import functools

import jax
import jax.numpy as jnp
from jax import lax
from jax.experimental import pallas as pl
from jax.experimental.pallas import tpu as pltpu
from jax.sharding import PartitionSpec as P

BITS = 30
WORDS = 18
EDGE = 8
FACE = EDGE * EDGE
TILE = 128
CH = 64
GROUP = 8
KROWS = 9 * CH
SPLIT = 5 * CH
STACK = (3 * CH, 6 * TILE)
VMEM_LIMIT = 16 * 1024 * 1024
BF = jnp.bfloat16
F32 = jnp.float32

SHIFTS = [(p, q) for p in (-1, 0, 1) for q in (-1, 0, 1)]


def column_of(p, q, r):
    tap = (p + 1) * 9 + (q + 1) * 3 + r + 1
    return tap if tap < 13 else tap - 1


def lane_ids(rows):
    return lax.broadcasted_iota(jnp.int32, (rows, TILE), 1)


def pick(test, a, b):
    rows = 16 if a.dtype == BF else 8
    mask = test(lane_ids(rows))
    return jnp.concatenate(
        [
            jnp.where(mask, a[i : i + rows], b[i : i + rows])
            for i in range(0, a.shape[0], rows)
        ],
        axis=0,
    )


def left(lane):
    return lane < FACE


def row_first(lane):
    return (lane // EDGE) % EDGE == 0


def row_last(lane):
    return (lane // EDGE) % EDGE == EDGE - 1


def cell_first(lane):
    return lane % EDGE == 0


def cell_last(lane):
    return lane % EDGE == EDGE - 1


def roll(value, amount):
    return pltpu.roll(value, amount % TILE, 1)


def swap(value):
    return roll(value, FACE)


def tile_of(value, k):
    return value[:, k * TILE : (k + 1) * TILE]


def occupancy_tile(words, tile):
    lane = lane_ids(words.shape[0]) + tile * TILE
    first, last = (tile * TILE) // BITS, (tile * TILE + TILE - 1) // BITS
    word = jnp.broadcast_to(words[:, first : first + 1], lane.shape)
    place = lane - first * BITS
    for w in range(first + 1, last + 1):
        past = lane >= w * BITS
        word = jnp.where(past, jnp.broadcast_to(words[:, w : w + 1], lane.shape), word)
        place = jnp.where(past, lane - w * BITS, place)
    return (jnp.right_shift(word, place) & 1).astype(F32)


def spread(occ, leaf):
    part = jnp.broadcast_to(occ[leaf : leaf + 1, :], (16, TILE)).astype(BF)
    return jnp.concatenate([part] * (CH // 16), axis=0)


def masked_tiles(field_ref, occ, leaf):
    return [
        field_ref[leaf, :, k * TILE : (k + 1) * TILE] * spread(occ[k], leaf) for k in range(4)
    ]


def reorder(tiles):
    n0, n1, n2, n3 = tiles
    r0, r1, r2, r3 = [swap(t) for t in tiles]
    order = [pick(left, n0, r2), pick(left, r0, n2), pick(left, n1, r3), pick(left, r1, n3)]
    flipped = [pick(left, n2, r0), pick(left, r2, n0), pick(left, n3, r1), pick(left, r3, n1)]
    return order, flipped


def restore(t0, t1, t2, t3):
    return [
        pick(left, t0, swap(t1)),
        pick(left, t2, swap(t3)),
        pick(left, swap(t0), t1),
        pick(left, swap(t2), t3),
    ]


def shift_q(center, flipped, q):
    test = row_last if q < 0 else row_first
    return [roll(pick(test, m, c), -q * EDGE) for m, c in zip(flipped, center)]


def edges_kernel(meta_ref, x_ref, d_ref, cross_ref, chip_ref):
    words = meta_ref[:, 0:WORDS]
    occ_lo = occupancy_tile(words, 0)
    occ_hi = occupancy_tile(words, 3)
    first_core = lax.rem(lax.axis_index("dom"), 2) == 0
    for leaf in range(x_ref.shape[0]):
        low, high = spread(occ_lo, leaf), spread(occ_hi, leaf)
        x_lo, x_hi = x_ref[leaf, :, 0:TILE] * low, x_ref[leaf, :, 3 * TILE :] * high
        d_lo, d_hi = d_ref[leaf, :, 0:TILE] * low, d_ref[leaf, :, 3 * TILE :] * high
        up = pick(left, swap(d_hi), x_hi)
        down = pick(left, x_lo, swap(d_lo))
        cross_ref[leaf] = jnp.where(first_core, down, up)
        chip_ref[leaf] = jnp.where(first_core, up, down)


def edges(meta, x, dy):
    shape = jax.ShapeDtypeStruct((x.shape[0], CH, TILE), BF)
    return pl.pallas_call(
        edges_kernel,
        out_shape=(shape, shape),
        in_specs=[vmem_spec()] * 3,
        out_specs=(vmem_spec(), vmem_spec()),
        cost_estimate=cost(10**6, 10**6),
        compiler_params=params(),
        name="edges",
    )(meta, x, dy)


def split_far(cross_ref, chip_ref, leaf):
    first_core = lax.rem(lax.axis_index("dom"), 2) == 0
    low = jnp.where(first_core, chip_ref[leaf], cross_ref[leaf])
    high = jnp.where(first_core, cross_ref[leaf], chip_ref[leaf])
    return low, high


def fill(store, flip, field_ref, occ, halo, turned):
    leaves = field_ref.shape[0]
    for leaf in range(leaves):
        order, flipped = reorder(masked_tiles(field_ref, occ, leaf))
        store[leaf] = jnp.concatenate(order, axis=1)
        flip[leaf] = jnp.concatenate(flipped, axis=1)
    if halo:
        for leaf in range(leaves):
            low, high = split_far(*halo, leaf)
            store[leaves + leaf, :, 0:TILE] = swap(low) if turned else low
            store[leaves + leaf, :, 3 * TILE :] = swap(high) if turned else high
    store[store.shape[0] - 1] = jnp.zeros(store.shape[1:], BF)
    flip[leaves] = jnp.zeros(flip.shape[1:], BF)


def place(near_ref, leaf, p, q, z, device, leaves, which):
    if (p, q, z) == (0, 0, 0):
        return leaf
    ident = near_ref[leaf, WORDS + column_of(p, q, z)]
    owner = ident // leaves
    slot = ident - owner * leaves
    absent = ident < 0
    if which == "all":
        slot = jnp.where(owner == device, slot, slot + leaves)
        return jnp.where(absent, 2 * leaves, slot)
    here = owner == device
    if which == "far":
        here = jnp.logical_not(here)
    return jnp.where(jnp.logical_and(here, jnp.logical_not(absent)), slot, leaves)


def stacked(store, flip, near_ref, leaf, z, device, leaves, which="all"):
    rows = {}
    center = None
    for q in (0, -1, 1):
        mid = place(near_ref, leaf, 0, q, z, device, leaves, which)
        after = place(near_ref, leaf, 1, q, z, device, leaves, which)
        before = place(near_ref, leaf, -1, q, z, device, leaves, which)
        mine = store[mid]
        past = pick(left, store[after, :, 0:TILE], tile_of(mine, 0))
        ahead = pick(left, tile_of(mine, 3), store[before, :, 3 * TILE :])
        if q == 0:
            center = [swap(ahead)] + [tile_of(mine, k) for k in range(4)] + [swap(past)]
            rows[q] = center
        else:
            other = flip[jnp.minimum(mid, leaves)]
            flipped = [ahead] + [tile_of(other, k) for k in range(4)] + [past]
            rows[q] = shift_q(center, flipped, q)
    return jnp.concatenate([jnp.concatenate(rows[q], axis=1) for q in (-1, 0, 1)], axis=0)


def unstack(stack):
    return jnp.concatenate([stack[:, i * TILE : (i + 4) * TILE] for i in range(3)], axis=0)


def shift_c(value, r):
    if r == 0:
        return value
    test = cell_last if r > 0 else cell_first
    tiles = [tile_of(value, k) for k in range(value.shape[1] // TILE)]
    return jnp.concatenate([pick(test, jnp.zeros_like(t), roll(t, -r)) for t in tiles], axis=1)


def across_c(value, z):
    test = cell_last if z > 0 else cell_first
    tiles = [tile_of(value, k) for k in range(value.shape[1] // TILE)]
    return jnp.concatenate(
        [pick(test, roll(t, z * (EDGE - 1)), jnp.zeros_like(t)) for t in tiles], axis=1
    )


def listed(near_ref, leaf, z):
    found = jnp.int32(-1)
    for p in (-1, 0, 1):
        for q in (-1, 0, 1):
            found = jnp.maximum(found, near_ref[leaf, WORDS + column_of(p, q, z)])
    return found >= 0


CONTRACT_LANES = (((1,), (1,)), ((), ()))


def dot_lanes(a, b):
    return lax.dot_general(a, b, CONTRACT_LANES, preferred_element_type=F32)


def grad_kernel(near_ref, meta_ref, x_ref, d_ref, total, stack_ref, store, flip):
    leaves = x_ref.shape[0]
    device = lax.axis_index("dom")
    words = meta_ref[:, 0:WORDS]
    occ = [occupancy_tile(words, k) for k in range(4)]
    fill(store, flip, x_ref, occ, None, False)

    def ordered_dy(leaf):
        return jnp.concatenate(reorder(masked_tiles(d_ref, occ, leaf))[0], axis=1)

    for leaf in range(leaves):
        stack = stacked(store, flip, near_ref, leaf, 0, device, leaves, "near")
        stack_ref[leaf] = stack
        center = ordered_dy(leaf)
        wide = jnp.concatenate([shift_c(center, -r) for r in (-1, 0, 1)], axis=0)
        term = dot_lanes(unstack(stack), wide)
        if leaf == 0:
            total[...] = term
        else:
            total[...] += term

    for z in (-1, 1):
        for leaf in range(leaves):

            @pl.when(listed(near_ref, leaf, z))
            def _():
                stack = stacked(store, flip, near_ref, leaf, z, device, leaves, "near")
                edge = across_c(ordered_dy(leaf), -z)
                total[:, (z + 1) * CH : (z + 2) * CH] += dot_lanes(unstack(stack), edge)


def grad_terms(meta, x, dy):
    leaves = x.shape[0]
    return pl.pallas_call(
        grad_kernel,
        out_shape=(
            jax.ShapeDtypeStruct((KROWS, 3 * CH), F32),
            jax.ShapeDtypeStruct((leaves,) + STACK, BF),
        ),
        in_specs=[smem_spec()] + [vmem_spec()] * 3,
        out_specs=(vmem_spec(), vmem_spec()),
        scratch_shapes=[pltpu.VMEM((leaves + 1, CH, 4 * TILE), BF)] * 2,
        cost_estimate=cost(10**9, 2 * 10**6),
        compiler_params=params(),
        name="grad_terms",
    )(meta, meta, x, dy)


def third_part(row):
    return (KROWS + row, 0) if row < SPLIT else (KROWS + row - SPLIT, 1)


def grad_far_kernel(
    near_ref, meta_ref, d_ref, cross_ref, chip_ref, near_total, keep_ref, send_ref, store, packed
):
    leaves = d_ref.shape[0]
    device = lax.axis_index("dom")
    words = meta_ref[:, 0:WORDS]
    occ_lo, occ_hi = occupancy_tile(words, 0), occupancy_tile(words, 3)
    for leaf in range(leaves):
        low, high = split_far(cross_ref, chip_ref, leaf)
        store[0, leaf], store[1, leaf] = low, high
        store[2, leaf], store[3, leaf] = swap(low), swap(high)
    for i in range(4):
        store[i, leaves] = jnp.zeros((CH, TILE), BF)

    def far_rows(p, one, two, z):
        at = lambda leaf, q: place(near_ref, leaf, p, q, z, device, leaves, "far")
        first, second = (0, 2) if p > 0 else (3, 1)
        pair = lambda a, b, q: pick(left, store[first, at(a, q)], store[second, at(b, q)])
        center = pair(one, two, 0)
        sides = [shift_q([center], [pair(two, one, q)], q)[0] for q in (-1, 1)]
        return jnp.concatenate([sides[0], center, sides[1]], axis=0)

    def end_plane(p, one, two):
        if p > 0:
            a, b = [d_ref[l, :, 3 * TILE :] * spread(occ_hi, l) for l in (one, two)]
            return pick(left, swap(a), b)
        a, b = [d_ref[l, :, 0:TILE] * spread(occ_lo, l) for l in (one, two)]
        return pick(left, a, swap(b))

    pairs = [(leaf, leaf + 1) for leaf in range(0, leaves, 2)]
    for p in (-1, 0, 1):
        term = None
        if p != 0:
            rows = jnp.concatenate([far_rows(p, a, b, 0) for a, b in pairs], axis=1)
            planes = jnp.concatenate([end_plane(p, a, b) for a, b in pairs], axis=1)
            wide = jnp.concatenate([shift_c(planes, -r) for r in (-1, 0, 1)], axis=0)
            term = dot_lanes(rows, wide)
        for q in (-1, 0, 1):
            row = SHIFTS.index((p, q)) * CH
            block = near_total[row : row + CH, :]
            if p != 0:
                block = block + term[(q + 1) * CH : (q + 2) * CH, :]
            packed[row : row + CH, :] = block[:, 0:TILE]
            low, side = third_part(row)
            packed[low : low + CH, side * CH : (side + 1) * CH] = block[:, TILE:]
    packed[2 * KROWS - SPLIT :, CH:] = jnp.zeros((2 * SPLIT - KROWS, CH), F32)

    for z in (-1, 1):
        for leaf in range(leaves):

            @pl.when(listed(near_ref, leaf, z))
            def _():
                for p in (-1, 1):
                    plane = end_plane(p, leaf, leaf)
                    plane = across_c(pick(left, plane, jnp.zeros_like(plane)), -z)
                    term = dot_lanes(far_rows(p, leaf, leaf, z), plane)
                    for q in (-1, 0, 1):
                        row, side = SHIFTS.index((p, q)) * CH, 0
                        if z > 0:
                            row, side = third_part(row)
                        packed[row : row + CH, side * CH : (side + 1) * CH] += term[
                            (q + 1) * CH : (q + 2) * CH, :
                        ]

    core = lax.rem(device, 2)
    rows = packed.shape[0] // 2
    keep_ref[...] = packed[pl.ds(pl.multiple_of(core * rows, 8), rows), :]
    send_ref[...] = packed[pl.ds(pl.multiple_of((1 - core) * rows, 8), rows), :]


def grad_far(meta, dy, cross, chip, total):
    leaves = dy.shape[0]
    rows = KROWS + SPLIT
    shape = jax.ShapeDtypeStruct((rows // 2, TILE), F32)
    return pl.pallas_call(
        grad_far_kernel,
        out_shape=(shape, shape),
        in_specs=[smem_spec()] + [vmem_spec()] * 5,
        out_specs=(vmem_spec(), vmem_spec()),
        scratch_shapes=[
            pltpu.VMEM((4, leaves + 1, CH, TILE), BF),
            pltpu.VMEM((rows, TILE), F32),
        ],
        cost_estimate=cost(10**8, 2 * 10**6),
        compiler_params=params(),
        name="grad_far",
    )(meta, meta, dy, cross, chip, total)


def vmem_spec():
    return pl.BlockSpec(memory_space=pltpu.VMEM)


def any_spec():
    return pl.BlockSpec(memory_space=pl.ANY)


def smem_spec():
    return pl.BlockSpec(memory_space=pltpu.SMEM)


def params():
    return pltpu.CompilerParams(vmem_limit_bytes=VMEM_LIMIT)


def cost(flops, bytes_accessed):
    return pl.CostEstimate(flops=flops, bytes_accessed=bytes_accessed, transcendentals=0)


def ordered_taps(w_ref, turned):
    def tap(index, r):
        p, q = SHIFTS[index]
        return (p + 1) * 9 + (q + 1) * 3 + r + 1

    if turned:
        return jnp.concatenate(
            [
                jnp.concatenate([w_ref[26 - tap(index, r)] for index in range(9)], axis=1)
                for r in (-1, 0, 1)
            ],
            axis=0,
        )
    return jnp.concatenate(
        [
            jnp.concatenate([w_ref[tap(index, r)] for r in (-1, 0, 1)], axis=1)
            for index in range(9)
        ],
        axis=0,
    ).T


def finish(occ, leaf, total):
    rounded = total.astype(BF)
    tiles = restore(*[tile_of(rounded, k) for k in range(4)])
    return jnp.concatenate([t * spread(occ[k], leaf) for k, t in enumerate(tiles)], axis=1)


def leaf_sum(taps, near_x):
    wide = jnp.dot(taps, near_x, preferred_element_type=F32)
    total = wide[CH : 2 * CH]
    for r in (-1, 1):
        total = total + shift_c(wide[(r + 1) * CH : (r + 2) * CH], r)
    return total


def third_dimension(near_ref, taps, occ, x_ref, cross_ref, chip_ref, turned, out_ref, store, flip):
    leaves = x_ref.shape[0]
    device = lax.axis_index("dom")
    found = [listed(near_ref, leaf, -1) | listed(near_ref, leaf, 1) for leaf in range(leaves)]

    @pl.when(functools.reduce(jnp.logical_or, found))
    def _():
        fill(store, flip, x_ref, occ, (cross_ref, chip_ref), turned)
        for leaf in range(leaves):
            stack = stacked(store, flip, near_ref, leaf, 0, device, leaves)
            total = leaf_sum(taps, unstack(stack))
            for z in (-1, 1):
                stack = stacked(store, flip, near_ref, leaf, z, device, leaves)
                part = jnp.dot(
                    taps[(z + 1) * CH : (z + 2) * CH], unstack(stack), preferred_element_type=F32
                )
                total = total + across_c(part, z)
            out_ref[leaf] = finish(occ, leaf, total)


def out_kernel(
    near_ref, meta_ref, x_ref, d_ref, cross_ref, chip_ref, w_ref, stack_ref, _,
    out_ref, stack_dy_ref, done_ref, store, flip, far,
):
    leaves = x_ref.shape[0]
    device = lax.axis_index("dom")
    words = meta_ref[:, 0:WORDS]
    occ = [occupancy_tile(words, k) for k in range(4)]
    done_ref[...] = jnp.zeros(done_ref.shape, F32)
    taps = ordered_taps(w_ref, False)
    fill(store, flip, d_ref, occ, (cross_ref, chip_ref), True)
    for leaf in range(leaves):
        low, high = split_far(cross_ref, chip_ref, leaf)
        both = pick(left, low, high)
        far[0, leaf], far[1, leaf] = both, swap(both)
    far[0, leaves] = far[1, leaves] = jnp.zeros((CH, TILE), BF)

    def far_tiles(leaf):
        at = lambda p, q: place(near_ref, leaf, p, q, 0, device, leaves, "far")
        center = pick(left, far[1, at(-1, 0)], far[1, at(1, 0)])
        flipped = {q: pick(left, far[0, at(1, q)], far[0, at(-1, q)]) for q in (-1, 1)}
        sides = [shift_q([center], [flipped[q]], q)[0] for q in (-1, 1)]
        return jnp.concatenate([sides[0], center, sides[1]], axis=0)

    for leaf in range(leaves):
        stack_dy_ref[leaf] = stacked(store, flip, near_ref, leaf, 0, device, leaves)
        planes = far_tiles(leaf)
        zero = jnp.zeros_like(planes)
        stack = stack_ref[leaf]
        stack = jnp.concatenate(
            [
                tile_of(stack, 0) + pick(left, planes, zero),
                stack[:, TILE : 5 * TILE],
                tile_of(stack, 5) + pick(left, zero, planes),
            ],
            axis=1,
        )
        out_ref[leaf] = finish(occ, leaf, leaf_sum(taps, unstack(stack)))
    third_dimension(
        near_ref, taps, occ, x_ref, cross_ref, chip_ref, False, out_ref, store, flip
    )


def out_conv(meta, x, dy, cross, chip, weight, stack, after):
    leaves = x.shape[0]
    return pl.pallas_call(
        out_kernel,
        out_shape=(
            jax.ShapeDtypeStruct(x.shape, BF),
            jax.ShapeDtypeStruct(stack.shape, BF),
            jax.ShapeDtypeStruct((8, TILE), F32),
        ),
        in_specs=[smem_spec()] + [vmem_spec()] * 7 + [any_spec()],
        out_specs=(vmem_spec(),) * 3,
        scratch_shapes=[
            pltpu.VMEM((2 * leaves + 1, CH, 4 * TILE), BF),
            pltpu.VMEM((leaves + 1, CH, 4 * TILE), BF),
            pltpu.VMEM((2, leaves + 1, CH, TILE), BF),
        ],
        cost_estimate=cost(10**9, 2 * 10**6),
        compiler_params=params(),
        name="out_conv",
    )(meta, meta, x, dy, cross, chip, weight, stack, after)


def in_grad_kernel(
    near_ref, meta_ref, d_ref, cross_ref, chip_ref, w_ref, stack_ref, _,
    out_ref, done_ref, store, flip,
):
    leaves = d_ref.shape[0]
    words = meta_ref[:, 0:WORDS]
    occ = [occupancy_tile(words, k) for k in range(4)]
    done_ref[...] = jnp.zeros(done_ref.shape, F32)
    taps = ordered_taps(w_ref, True)
    for leaf in range(leaves):
        out_ref[leaf] = finish(occ, leaf, leaf_sum(taps, unstack(stack_ref[leaf])))
    third_dimension(near_ref, taps, occ, d_ref, cross_ref, chip_ref, True, out_ref, store, flip)


def in_grad_conv(meta, dy, cross, chip, weight, stack, after):
    leaves = dy.shape[0]
    return pl.pallas_call(
        in_grad_kernel,
        out_shape=(jax.ShapeDtypeStruct(dy.shape, BF), jax.ShapeDtypeStruct((8, TILE), F32)),
        in_specs=[smem_spec()] + [vmem_spec()] * 6 + [any_spec()],
        out_specs=(vmem_spec(),) * 2,
        scratch_shapes=[
            pltpu.VMEM((2 * leaves + 1, CH, 4 * TILE), BF),
            pltpu.VMEM((leaves + 1, CH, 4 * TILE), BF),
        ],
        cost_estimate=cost(10**9, 2 * 10**6),
        compiler_params=params(),
        name="in_grad_conv",
    )(meta, meta, dy, cross, chip, weight, stack, after)


def sum_kernel(own_ref, *refs):
    *got_refs, _, out_ref = refs
    total = own_ref[...]
    for got_ref in got_refs:
        total = total + got_ref[...]
    out_ref[...] = total


def sum_chunks(own, got, after):
    return pl.pallas_call(
        sum_kernel,
        out_shape=jax.ShapeDtypeStruct(own.shape, F32),
        in_specs=[vmem_spec()] * (1 + len(got)) + [any_spec()],
        out_specs=vmem_spec(),
        cost_estimate=cost(10**5, 3 * 10**5),
        compiler_params=params(),
        name="sum_chunks",
    )(own, *got, after)


def join_kernel(*refs):
    *parts, _, out_ref = refs
    lane = lax.rem(lax.axis_index("dom") // 2, 4)
    rows = parts[0].shape[0]
    for mask, part in enumerate(parts):
        at = pl.multiple_of(jnp.bitwise_xor(lane, mask) * rows, 8)
        out_ref[pl.ds(at, rows), :] = part[...]


def join_chunks(parts, after):
    rows = parts[0].shape[0]
    return pl.pallas_call(
        join_kernel,
        out_shape=jax.ShapeDtypeStruct((len(parts) * rows, TILE), F32),
        in_specs=[vmem_spec()] * len(parts) + [any_spec()],
        out_specs=vmem_spec(),
        cost_estimate=cost(10**5, 5 * 10**5),
        compiler_params=params(),
        name="join_chunks",
    )(*parts, after)


def unpack_kernel(scale, own_ref, other_ref, out_ref, total):
    core = lax.rem(lax.axis_index("dom"), 2)
    rows = own_ref.shape[0]
    total[pl.ds(pl.multiple_of(core * rows, 8), rows), :] = own_ref[...] * scale
    total[pl.ds(pl.multiple_of((1 - core) * rows, 8), rows), :] = other_ref[...] * scale
    for index, (p, q) in enumerate(SHIFTS):
        for r in (-1, 0, 1):
            tap = (p + 1) * 9 + (q + 1) * 3 + r + 1
            row, side = index * CH, r + 1
            if r == 1:
                row, side = third_part(row)
            out_ref[tap] = total[row : row + CH, side * CH : (side + 1) * CH]


def unpack(own, other, scale):
    return pl.pallas_call(
        functools.partial(unpack_kernel, scale),
        out_shape=jax.ShapeDtypeStruct((27, CH, CH), F32),
        in_specs=[vmem_spec(), vmem_spec()],
        out_specs=vmem_spec(),
        scratch_shapes=[pltpu.VMEM((2 * own.shape[0], TILE), F32)],
        cost_estimate=cost(10**6, 10**6),
        compiler_params=params(),
        name="unpack_grad",
    )(own, other)


def exchange(array, mask, size):
    return lax.ppermute(array, "dom", [(i, i ^ mask) for i in range(size)])


def shards(features, cotangent, weight, mask_words, neighbors):
    leaves, channels, voxels = features.shape
    size = lax.axis_size("dom")
    device = lax.axis_index("dom")
    meta = jnp.concatenate([mask_words, neighbors], axis=1)
    to_cross, to_chip = edges(meta, features, cotangent)
    between = [(i, i + 1) for i in range(1, size - 1, 2)]
    cross = lax.ppermute(to_cross, "dom", between + [(j, i) for i, j in between])
    chip = exchange(to_chip, 1, size)

    total, stack = grad_terms(meta, features, cotangent)
    keep, send = grad_far(meta, cotangent, cross, chip, total)
    keep = keep + exchange(send, 1, size)
    rows = keep.shape[0] // 4
    lane = (device // 2) % 4
    chunk = lambda index: lax.dynamic_slice_in_dim(keep, index * rows, rows, axis=0)
    to_send = [chunk(lane ^ m) for m in (1, 2, 3)]
    own = chunk(lane)
    got = [exchange(part, 2 * m, size) for m, part in zip((1, 2, 3), to_send)]
    out_features, stack_dy, out_done = out_conv(
        meta, features, cotangent, cross, chip, weight, stack, to_send[2]
    )
    own = sum_chunks(own, got, out_done)
    if size > GROUP:
        groups = [[j * GROUP + i for j in range(size // GROUP)] for i in range(GROUP)]
        own = lax.psum(own, "dom", axis_index_groups=groups)
    back = [exchange(own, 2 * m, size) for m in (1, 2, 3)]
    in_grad, in_done = in_grad_conv(meta, cotangent, cross, chip, weight, stack_dy, own)
    half = join_chunks([own] + back, in_done)
    other = exchange(half, 1, size)
    scale = float(size * leaves * voxels) ** -0.5
    return (out_features, in_grad, unpack(half, other, scale))


def solution(mesh):
    split = P(("scene", "dom"), None, None)
    flat = P(("scene", "dom"), None)
    return jax.shard_map(
        shards,
        mesh=mesh,
        in_specs=(split, split, P(), flat, flat),
        out_specs=(split, split, P("scene", None, None)),
        check_vma=False,
    )
```

time: 46.4 us -> 42 us (0.905)
  local copies, waits for them, and re-layouts: 8.65 us -> 4.74 us
  Pallas kernels: 18.4 us -> 14.9 us
  other arithmetic: 0.03 us -> 1.85 us
  waiting for transfers between devices: 4.01 us -> 5.29 us
    unnamed x24 -> x18, local copies, waits for them, and re-layouts: 8.62 us -> 4.71 us
    pallas_call x1, Pallas kernels: 2.18 us -> 0.23 us  [edges(): pl.pallas_call(edges_kernel, out_shape=(shape, shape), in_specs=[vmem_spe...]
    pallas_call x1, Pallas kernels: 6.3 us -> 4.62 us  [out_conv(): pl.pallas_call(out_kernel, out_shape=(jax.ShapeDtypeStruct(x.shape, BF),...]
    ppermute x9, waiting for transfers between devices: 4.01 us -> 5.28 us  [exchange(): return lax.ppermute(array, 'dom', [(i, i ^ mask) for i in range(size)])]
    add x1, other arithmetic: 0.03 us -> 1.07 us  [shards(): keep = keep + exchange(send, 1, size)]
    concatenate x0 -> x1, other arithmetic: none -> 0.78 us  [shards(): meta = jnp.concatenate([mask_words, neighbors], axis=1)]
    pallas_call x1, Pallas kernels: 1.89 us -> 2.54 us  [grad_far(): pl.pallas_call(grad_far_kernel, out_shape=(shape, shape), in_specs=[smem_...]
    pallas_call x1, Pallas kernels: 3.64 us -> 3.09 us  [grad_terms(): pl.pallas_call(grad_kernel, out_shape=(jax.ShapeDtypeStruct((KROWS, 3 * C...]
  transfers between devices with their start and end apart: 10 -> 10, of which waited for: 3 -> 3; matrix products, arithmetic and copies ran while one was open for 0% -> 0% of each run, Pallas kernels for 28% -> 26%
where the time goes in v5:
time: 42 us; the launch traced here: 41.7 us
  Pallas kernels  14.9 us (35%)
  starting transfers between devices  14.1 us (34%)
  waiting for transfers between devices  5.29 us (13%)
  local copies, waits for them, and re-layouts  4.74 us (11%)
  other arithmetic  1.85 us (4%)
  between operations  0.75 us (2%)
    ppermute x9, starting transfers between devices, exchange(): return lax.ppermute(array, 'dom', [(i, i ^ mask) for i in range(size)])  13.4 us
    ppermute x9, waiting for transfers between devices, exchange(): return lax.ppermute(array, 'dom', [(i, i ^ mask) for i in range(size)])  5.28 us
    unnamed x18, local copies, waits for them, and re-layouts  4.71 us
    pallas_call x1, Pallas kernels, out_conv(): pl.pallas_call(out_kernel, out_shape=(jax.ShapeDtypeStruct(x.shape, BF),...  4.62 us
    pallas_call x1, Pallas kernels, in_grad_conv(): pl.pallas_call(in_grad_kernel, out_shape=(jax.ShapeDtypeStruct(dy.shape,...  3.24 us
    pallas_call x1, Pallas kernels, grad_terms(): pl.pallas_call(grad_kernel, out_shape=(jax.ShapeDtypeStruct((KROWS, 3 * C...  3.09 us
    pallas_call x1, Pallas kernels, grad_far(): pl.pallas_call(grad_far_kernel, out_shape=(shape, shape), in_specs=[smem_...  2.54 us
    pallas_call x1, Pallas kernels, unpack(): pl.pallas_call(functools.partial(unpack_kernel, scale), out_shape=jax.Sha...  1.16 us
  transfers between devices with their start and end apart: 10, of which 3 were waited for; matrix products, arithmetic and copies ran while one was open for 0% of the time, Pallas kernels for 26%

profile of v5, /device:TPU:0, one launch (start us, length us, event | category | flops | bytes accessed | tf_op | source)
XLA Modules:
  0.0 41.7 jit_solution(9824544131473435198)
XLA Ops:
  0.6 0.8 %pad_add_fusion.meta_ref.near_ref = s32[8,44]{1,0:T(8,128)S(1)} fusion(s32[8,26]{1,0:T(8,128)} %param.9, s32[8,18]{1,0:T(8,128)} %param.8), kind=kLoop, calls=%fused_computation | loop fusion | flops 352 | bytes 2816 | tf_op jit(solution)/shard_map/concatenate | solution.py:636
  1.4 0.0 copy-start
  1.4 1.0 %copy-done = bf16[8,64,512]{2,1,0:T(8,128)(2,1)S(1)} copy-done((bf16[8,64,512]{2,1,0:T(8,128)(2,1)S(1)}, bf16[8,64,512]{2,1,0:T(8,128)(2,1)}, u32[]{:S(2)}) %copy-start) | copy-done | bytes 524312
  2.5 0.0 copy-start.2
  2.5 1.0 %copy-done.2 = bf16[8,64,512]{2,1,0:T(8,128)(2,1)S(1)} copy-done((bf16[8,64,512]{2,1,0:T(8,128)(2,1)S(1)}, bf16[8,64,512]{2,1,0:T(8,128)(2,1)}, u32[]{:S(2)}) %copy-start.2) | copy-done | bytes 524312
  3.5 0.0 copy-start.1
  3.5 0.2 edges.1
  3.7 0.7 %collective-permute-start = (bf16[8,64,128]{2,1,0:T(8,128)(2,1)S(1)}, bf16[8,64,128]{2,1,0:T(8,128)(2,1)S(1)}, u32[]{:S(2)}, u32[]{:S(2)}) collective-permute-start(bf16[8,64,128]{2,1,0:T(8,128)(2,1)S(1)} %get-tuple-element.14), channel_id=1, source_target_pairs={{1,2},{3,4},{5,6},{2,1},{4,3},{6,5},{9,10},{11,12},{13,14},{10,9},... | collective-permute-start | bytes 393224 | tf_op jit(solution)/shard_map/ppermute | solution.py:639
  4.4 0.0 copy-start.3
  4.4 4.4 %collective-permute-start.1 = (bf16[8,64,128]{2,1,0:T(8,128)(2,1)S(1)}, bf16[8,64,128]{2,1,0:T(8,128)(2,1)S(1)}, u32[]{:S(2)}, u32[]{:S(2)}) collective-permute-start(bf16[8,64,128]{2,1,0:T(8,128)(2,1)S(1)} %get-tuple-element.15), channel_id=1, source_target_pairs={{0,1},{1,0},{2,3},{3,2},{4,5},{5,4},{6,7},{7,6},{8,9},{9,8},{10,11... | collective-permute-start | bytes 393224 | tf_op jit(solution)/shard_map/ppermute | solution.py:629
  8.9 3.1 %grad_terms.1 = (f32[576,192]{1,0:T(8,128)S(1)}, bf16[8,192,768]{2,1,0:T(8,128)(2,1)S(1)}) custom-call(s32[8,44]{1,0:T(8,128)S(1)} %pad_add_fusion.meta_ref.near_ref, s32[8,44]{1,0:T(8,128)S(1)} %pad_add_fusion.meta_ref.near_ref, bf16[8,64,512]{2,1,0:T(8,128)(2,1)S(1)} %copy-done.2, bf16[8,64,512]{2,1,0:T(8,128)(2,1)S(1)} %copy-done), custom_call_target="tpu_custom_call" | custom-call | flops 1000000000 | bytes 2000000 | tf_op jit(solution)/shard_map/grad_terms/pallas_call | solution.py:279
  12.0 0.0 collective-permute-done.cross_ref
  12.0 0.0 collective-permute-done.1.chip_ref
  12.0 0.0 copy-start.4
  12.0 0.0 copy-done.1
  12.0 2.5 %grad_far.1 = (f32[448,128]{1,0:T(8,128)S(1)}, f32[448,128]{1,0:T(8,128)}) custom-call(s32[8,44]{1,0:T(8,128)S(1)} %pad_add_fusion.meta_ref.near_ref, s32[8,44]{1,0:T(8,128)S(1)} %pad_add_fusion.meta_ref.near_ref, bf16[8,64,512]{2,1,0:T(8,128)(2,1)S(1)} %copy-done.1, bf16[8,64,128]{2,1,0:T(8,128)(2,1)S(1)} %collective-permute-done.cross_ref, ...), custom_call_target="tpu_custom_call" | custom-call | flops 100000000 | bytes 2000000 | tf_op jit(solution)/shard_map/grad_far/pallas_call | solution.py:372
  14.5 0.0 copy-done.4
  14.6 0.0 copy-start.8
  14.6 0.7 %copy-done.8 = f32[448,128]{1,0:T(8,128)} copy-done((f32[448,128]{1,0:T(8,128)}, f32[448,128]{1,0:T(8,128)S(1)}, u32[]{:S(2)}) %copy-start.8) | copy-done | bytes 229400
  15.2 0.0 collective-permute-start.2
  15.3 1.8 %collective-permute-done.2 = f32[448,128]{1,0:T(8,128)} collective-permute-done((f32[448,128]{1,0:T(8,128)}, f32[448,128]{1,0:T(8,128)}, u32[]{:S(2)}, u32[]{:S(2)}) %collective-permute-start.2) | collective-permute-done | bytes 229408 | tf_op jit(solution)/shard_map/ppermute | solution.py:629
  17.1 1.1 %add.20 = f32[448,128]{1,0:T(8,128)S(1)} add(f32[448,128]{1,0:T(8,128)} %copy-done.8, f32[448,128]{1,0:T(8,128)} %collective-permute-done.2) | non-fusion elementwise | flops 57344 | bytes 688128 | tf_op jit(solution)/shard_map/add | solution.py:644
  18.1 0.0 copy-start.6
  18.2 1.6 %collective-permute-start.3 = (f32[112,128]{1,0:T(8,128)S(1)}, f32[112,128]{1,0:T(8,128)S(1)}, u32[]{:S(2)}, u32[]{:S(2)}) collective-permute-start(f32[112,128]{1,0:T(8,128)S(1)} %get-tuple-element.26), channel_id=1, source_target_pairs={{0,2},{1,3},{2,0},{3,1},{4,6},{5,7},{6,4},{7,5},{8,10},{9,11},{10,... | collective-permute-start | bytes 172040 | tf_op jit(solution)/shard_map/ppermute | solution.py:629
  19.8 2.1 %collective-permute-start.4 = (f32[112,128]{1,0:T(8,128)S(1)}, f32[112,128]{1,0:T(8,128)S(1)}, u32[]{:S(2)}, u32[]{:S(2)}) collective-permute-start(f32[112,128]{1,0:T(8,128)S(1)} %get-tuple-element.25), channel_id=1, source_target_pairs={{0,4},{1,5},{2,6},{3,7},{4,0},{5,1},{6,2},{7,3},{8,12},{9,13},{10,... | collective-permute-start | bytes 172040 | tf_op jit(solution)/shard_map/ppermute | solution.py:629
  21.9 0.7 %collective-permute-start.5 = (f32[112,128]{1,0:T(8,128)S(1)}, f32[112,128]{1,0:T(8,128)S(1)}, u32[]{:S(2)}, u32[]{:S(2)}) collective-permute-start(f32[112,128]{1,0:T(8,128)S(1)} %get-tuple-element.28._), channel_id=1, source_target_pairs={{0,6},{1,7},{2,4},{3,5},{4,2},{5,3},{6,0},{7,1},{8,14},{9,15},{10,... | collective-permute-start | bytes 172040 | tf_op jit(solution)/shard_map/ppermute | solution.py:629
  22.7 0.0 copy-done.3
  22.7 0.0 copy-start.5
  22.7 0.9 %copy-done.5 = bf16[8,64,128]{2,1,0:T(8,128)(2,1)S(1)} copy-done((bf16[8,64,128]{2,1,0:T(8,128)(2,1)S(1)}, bf16[8,64,128]{2,1,0:T(8,128)(2,1)}, u32[]{:S(2)}) %copy-start.5) | copy-done | bytes 131096
  23.6 0.0 copy-start.7
  23.6 1.0 %copy-done.7 = bf16[27,64,64]{2,1,0:T(8,128)(2,1)S(1)} copy-done((bf16[27,64,64]{2,1,0:T(8,128)(2,1)S(1)}, bf16[27,64,64]{2,1,0:T(8,128)(2,1)}, u32[]{:S(2)}) %copy-start.7) | copy-done | bytes 221208
  24.6 4.6 %out_conv.1 = (bf16[8,64,512]{2,1,0:T(8,128)(2,1)}, bf16[8,192,768]{2,1,0:T(8,128)(2,1)S(1)}, f32[8,128]{1,0:T(8,128)S(1)}) custom-call(s32[8,44]{1,0:T(8,128)S(1)} %pad_add_fusion.meta_ref.near_ref, s32[8,44]{1,0:T(8,128)S(1)} %pad_add_fusion.meta_ref.near_ref, bf16[8,64,512]{2,1,0:T(8,128)(2,1)S(1)} %copy-done.3, bf16[8,64,512]{2,1,0:T(8,128)(2,1)S(1)} %copy-done.1, ...), custom_call_target="tpu_custom_call" | custom-call | flops 1000000000 | bytes 2000000 | tf_op jit(solution)/shard_map/out_conv/pallas_call | solution.py:508
  29.2 0.0 collective-permute-done.3.refs_0_
  29.2 0.0 collective-permute-done.4.refs_1_
  29.2 0.0 collective-permute-done.5.refs_2_
  29.2 0.7 %collective-permute-start.6 = (f32[112,128]{1,0:T(8,128)S(1)}, f32[112,128]{1,0:T(8,128)S(1)}, u32[]{:S(2)}, u32[]{:S(2)}) collective-permute-start(f32[112,128]{1,0:T(8,128)S(1)} %sum_chunks.1._.refs_0_), channel_id=1, source_target_pairs={{0,2},{1,3},{2,0},{3,1},{4,6},{5,7},{6,4},{7,5},{8,10},{9,11},{10,... | collective-permute-start | bytes 172040 | tf_op jit(solution)/shard_map/ppermute | solution.py:629
  30.0 3.0 %collective-permute-start.7 = (f32[112,128]{1,0:T(8,128)S(1)}, f32[112,128]{1,0:T(8,128)S(1)}, u32[]{:S(2)}, u32[]{:S(2)}) collective-permute-start(f32[112,128]{1,0:T(8,128)S(1)} %sum_chunks.1._.refs_0_), channel_id=1, source_target_pairs={{0,4},{1,5},{2,6},{3,7},{4,0},{5,1},{6,2},{7,3},{8,12},{9,13},{10,... | collective-permute-start | bytes 172040 | tf_op jit(solution)/shard_map/ppermute | solution.py:629
  32.9 0.7 %collective-permute-start.8 = (f32[112,128]{1,0:T(8,128)S(1)}, f32[112,128]{1,0:T(8,128)S(1)}, u32[]{:S(2)}, u32[]{:S(2)}) collective-permute-start(f32[112,128]{1,0:T(8,128)S(1)} %sum_chunks.1._.refs_0_), channel_id=1, source_target_pairs={{0,6},{1,7},{2,4},{3,5},{4,2},{5,3},{6,0},{7,1},{8,14},{9,15},{10,... | collective-permute-start | bytes 172040 | tf_op jit(solution)/shard_map/ppermute | solution.py:629
  33.7 0.0 copy-done.6
  33.7 3.2 %in_grad_conv.1 = (bf16[8,64,512]{2,1,0:T(8,128)(2,1)}, f32[8,128]{1,0:T(8,128)S(1)}) custom-call(s32[8,44]{1,0:T(8,128)S(1)} %pad_add_fusion.meta_ref.near_ref, s32[8,44]{1,0:T(8,128)S(1)} %pad_add_fusion.meta_ref.near_ref, bf16[8,64,512]{2,1,0:T(8,128)(2,1)S(1)} %copy-done.1, bf16[8,64,128]{2,1,0:T(8,128)(2,1)S(1)} %collective-permute-done.cross_ref, ...), custom_call_target="tpu_custom_call" | custom-call | flops 1000000000 | bytes 2000000 | tf_op jit(solution)/shard_map/in_grad_conv/pallas_call | solution.py:544
  36.9 0.0 collective-permute-done.6.refs_1_
  36.9 0.0 collective-permute-done.7.refs_2_
  36.9 2.0 %collective-permute-done.8.refs_3_ = f32[112,128]{1,0:T(8,128)S(1)} collective-permute-done((f32[112,128]{1,0:T(8,128)S(1)}, f32[112,128]{1,0:T(8,128)S(1)}, u32[]{:S(2)}, u32[]{:S(2)}) %collective-permute-start.8) | collective-permute-done | bytes 57376 | tf_op jit(solution)/shard_map/ppermute | solution.py:629
  38.9 0.1 collective-permute-start.9
  39.0 1.5 %collective-permute-done.9.other_ref = f32[448,128]{1,0:T(8,128)S(1)} collective-permute-done((f32[448,128]{1,0:T(8,128)S(1)}, f32[448,128]{1,0:T(8,128)S(1)}, u32[]{:S(2)}, u32[]{:S(2)}) %collective-permute-start.9) | collective-permute-done | bytes 229408 | tf_op jit(solution)/shard_map/ppermute | solution.py:629
  40.5 1.2 %unpack_grad.1 = f32[27,64,64]{2,1,0:T(8,128)} custom-call(f32[448,128]{1,0:T(8,128)S(1)} %join_chunks.1.own_ref, f32[448,128]{1,0:T(8,128)S(1)} %collective-permute-done.9.other_ref), custom_call_target="tpu_custom_call" | custom-call | flops 1000000 | bytes 1000000 | tf_op jit(solution)/shard_map/unpack_grad/pallas_call | solution.py:616
  (3 shorter events, 0.1 us)
Async XLA Ops:
  1.4 1.0 %copy-start = (bf16[8,64,512]{2,1,0:T(8,128)(2,1)S(1)}, bf16[8,64,512]{2,1,0:T(8,128)(2,1)}, u32[]{:S(2)}) copy-start(bf16[8,64,512]{2,1,0:T(8,128)(2,1)} %d_ref.9) | copy-start | bytes 1572868
  2.5 1.0 %copy-start.2 = (bf16[8,64,512]{2,1,0:T(8,128)(2,1)S(1)}, bf16[8,64,512]{2,1,0:T(8,128)(2,1)}, u32[]{:S(2)}) copy-start(bf16[8,64,512]{2,1,0:T(8,128)(2,1)} %x_ref.5) | copy-start | bytes 1572868
  3.5 8.5 %copy-start.1 = (bf16[8,64,512]{2,1,0:T(8,128)(2,1)S(1)}, bf16[8,64,512]{2,1,0:T(8,128)(2,1)}, u32[]{:S(2)}) copy-start(bf16[8,64,512]{2,1,0:T(8,128)(2,1)} %d_ref.9) | copy-start | bytes 1572868
  3.7 8.2 %collective-permute-start = (bf16[8,64,128]{2,1,0:T(8,128)(2,1)S(1)}, bf16[8,64,128]{2,1,0:T(8,128)(2,1)S(1)}, u32[]{:S(2)}, u32[]{:S(2)}) collective-permute-start(bf16[8,64,128]{2,1,0:T(8,128)(2,1)S(1)} %get-tuple-element.14), channel_id=1, source_target_pairs={{1,2},{3,4},{5,6},{2,1},{4,3},{6,5},{9,10},{11,12},{13,14},{10,9},... | collective-permute-start | bytes 393224 | tf_op jit(solution)/shard_map/ppermute | solution.py:639
  4.4 18.2 %copy-start.3 = (bf16[8,64,512]{2,1,0:T(8,128)(2,1)S(1)}, bf16[8,64,512]{2,1,0:T(8,128)(2,1)}, u32[]{:S(2)}) copy-start(bf16[8,64,512]{2,1,0:T(8,128)(2,1)} %x_ref.5) | copy-start | bytes 1572868
  4.4 7.6 %collective-permute-start.1 = (bf16[8,64,128]{2,1,0:T(8,128)(2,1)S(1)}, bf16[8,64,128]{2,1,0:T(8,128)(2,1)S(1)}, u32[]{:S(2)}, u32[]{:S(2)}) collective-permute-start(bf16[8,64,128]{2,1,0:T(8,128)(2,1)S(1)} %get-tuple-element.15), channel_id=1, source_target_pairs={{0,1},{1,0},{2,3},{3,2},{4,5},{5,4},{6,7},{7,6},{8,9},{9,8},{10,11... | collective-permute-start | bytes 393224 | tf_op jit(solution)/shard_map/ppermute | solution.py:629
  12.0 2.6 %copy-start.4 = (bf16[8,64,128]{2,1,0:T(8,128)(2,1)}, bf16[8,64,128]{2,1,0:T(8,128)(2,1)S(1)}, u32[]{:S(2)}) copy-start(bf16[8,64,128]{2,1,0:T(8,128)(2,1)S(1)} %collective-permute-done.1.chip_ref) | copy-start | bytes 393220
  14.6 0.7 %copy-start.8 = (f32[448,128]{1,0:T(8,128)}, f32[448,128]{1,0:T(8,128)S(1)}, u32[]{:S(2)}) copy-start(f32[448,128]{1,0:T(8,128)S(1)} %get-tuple-element.18) | copy-start | bytes 688132
  15.2 1.8 %collective-permute-start.2 = (f32[448,128]{1,0:T(8,128)}, f32[448,128]{1,0:T(8,128)}, u32[]{:S(2)}, u32[]{:S(2)}) collective-permute-start(f32[448,128]{1,0:T(8,128)} %get-tuple-element.19), channel_id=1, source_target_pairs={{0,1},{1,0},{2,3},{3,2},{4,5},{5,4},{6,7},{7,6},{8,9},{9,8},{10,11... | collective-permute-start | bytes 688136 | tf_op jit(solution)/shard_map/ppermute | solution.py:629
  18.1 15.5 %copy-start.6 = (bf16[8,64,128]{2,1,0:T(8,128)(2,1)S(1)}, bf16[8,64,128]{2,1,0:T(8,128)(2,1)}, u32[]{:S(2)}) copy-start(bf16[8,64,128]{2,1,0:T(8,128)(2,1)} %copy-done.4) | copy-start | bytes 393220
  18.2 11.0 %collective-permute-start.3 = (f32[112,128]{1,0:T(8,128)S(1)}, f32[112,128]{1,0:T(8,128)S(1)}, u32[]{:S(2)}, u32[]{:S(2)}) collective-permute-start(f32[112,128]{1,0:T(8,128)S(1)} %get-tuple-element.26), channel_id=1, source_target_pairs={{0,2},{1,3},{2,0},{3,1},{4,6},{5,7},{6,4},{7,5},{8,10},{9,11},{10,... | collective-permute-start | bytes 172040 | tf_op jit(solution)/shard_map/ppermute | solution.py:629
  19.8 9.4 %collective-permute-start.4 = (f32[112,128]{1,0:T(8,128)S(1)}, f32[112,128]{1,0:T(8,128)S(1)}, u32[]{:S(2)}, u32[]{:S(2)}) collective-permute-start(f32[112,128]{1,0:T(8,128)S(1)} %get-tuple-element.25), channel_id=1, source_target_pairs={{0,4},{1,5},{2,6},{3,7},{4,0},{5,1},{6,2},{7,3},{8,12},{9,13},{10,... | collective-permute-start | bytes 172040 | tf_op jit(solution)/shard_map/ppermute | solution.py:629
  21.9 7.3 %collective-permute-start.5 = (f32[112,128]{1,0:T(8,128)S(1)}, f32[112,128]{1,0:T(8,128)S(1)}, u32[]{:S(2)}, u32[]{:S(2)}) collective-permute-start(f32[112,128]{1,0:T(8,128)S(1)} %get-tuple-element.28._), channel_id=1, source_target_pairs={{0,6},{1,7},{2,4},{3,5},{4,2},{5,3},{6,0},{7,1},{8,14},{9,15},{10,... | collective-permute-start | bytes 172040 | tf_op jit(solution)/shard_map/ppermute | solution.py:629
  22.7 0.9 %copy-start.5 = (bf16[8,64,128]{2,1,0:T(8,128)(2,1)S(1)}, bf16[8,64,128]{2,1,0:T(8,128)(2,1)}, u32[]{:S(2)}) copy-start(bf16[8,64,128]{2,1,0:T(8,128)(2,1)} %copy-done.4) | copy-start | bytes 393220
  23.6 1.0 %copy-start.7 = (bf16[27,64,64]{2,1,0:T(8,128)(2,1)S(1)}, bf16[27,64,64]{2,1,0:T(8,128)(2,1)}, u32[]{:S(2)}) copy-start(bf16[27,64,64]{2,1,0:T(8,128)(2,1)} %w_ref.3) | copy-start | bytes 663556
  29.2 7.7 %collective-permute-start.6 = (f32[112,128]{1,0:T(8,128)S(1)}, f32[112,128]{1,0:T(8,128)S(1)}, u32[]{:S(2)}, u32[]{:S(2)}) collective-permute-start(f32[112,128]{1,0:T(8,128)S(1)} %sum_chunks.1._.refs_0_), channel_id=1, source_target_pairs={{0,2},{1,3},{2,0},{3,1},{4,6},{5,7},{6,4},{7,5},{8,10},{9,11},{10,... | collective-permute-start | bytes 172040 | tf_op jit(solution)/shard_map/ppermute | solution.py:629
  30.0 7.0 %collective-permute-start.7 = (f32[112,128]{1,0:T(8,128)S(1)}, f32[112,128]{1,0:T(8,128)S(1)}, u32[]{:S(2)}, u32[]{:S(2)}) collective-permute-start(f32[112,128]{1,0:T(8,128)S(1)} %sum_chunks.1._.refs_0_), channel_id=1, source_target_pairs={{0,4},{1,5},{2,6},{3,7},{4,0},{5,1},{6,2},{7,3},{8,12},{9,13},{10,... | collective-permute-start | bytes 172040 | tf_op jit(solution)/shard_map/ppermute | solution.py:629
  32.9 6.0 %collective-permute-start.8 = (f32[112,128]{1,0:T(8,128)S(1)}, f32[112,128]{1,0:T(8,128)S(1)}, u32[]{:S(2)}, u32[]{:S(2)}) collective-permute-start(f32[112,128]{1,0:T(8,128)S(1)} %sum_chunks.1._.refs_0_), channel_id=1, source_target_pairs={{0,6},{1,7},{2,4},{3,5},{4,2},{5,3},{6,0},{7,1},{8,14},{9,15},{10,... | collective-permute-start | bytes 172040 | tf_op jit(solution)/shard_map/ppermute | solution.py:629
  38.9 1.6 %collective-permute-start.9 = (f32[448,128]{1,0:T(8,128)S(1)}, f32[448,128]{1,0:T(8,128)S(1)}, u32[]{:S(2)}, u32[]{:S(2)}) collective-permute-start(f32[448,128]{1,0:T(8,128)S(1)} %join_chunks.1.own_ref), channel_id=1, source_target_pairs={{0,1},{1,0},{2,3},{3,2},{4,5},{5,4},{6,7},{7,6},{8,9},{9,8},{10,11... | collective-permute-start | bytes 688136 | tf_op jit(solution)/shard_map/ppermute | solution.py:629

commit v6 on v5

v6 whole, which is shorter than its diff:
```python
import functools

import jax
import jax.numpy as jnp
from jax import lax
from jax.experimental import pallas as pl
from jax.experimental.pallas import tpu as pltpu
from jax.sharding import PartitionSpec as P

BITS = 30
NEAR = 26
EDGE = 8
FACE = EDGE * EDGE
TILE = 128
CH = 64
GROUP = 8
KROWS = 9 * CH
SPLIT = 5 * CH
STACK = (3 * CH, 6 * TILE)
VMEM_LIMIT = 16 * 1024 * 1024
BF = jnp.bfloat16
F32 = jnp.float32

SHIFTS = [(p, q) for p in (-1, 0, 1) for q in (-1, 0, 1)]


def column_of(p, q, r):
    tap = (p + 1) * 9 + (q + 1) * 3 + r + 1
    return tap if tap < 13 else tap - 1


def lane_ids(rows):
    return lax.broadcasted_iota(jnp.int32, (rows, TILE), 1)


def pick(test, a, b):
    rows = 16 if a.dtype == BF else 8
    mask = test(lane_ids(rows))
    return jnp.concatenate(
        [
            jnp.where(mask, a[i : i + rows], b[i : i + rows])
            for i in range(0, a.shape[0], rows)
        ],
        axis=0,
    )


def left(lane):
    return lane < FACE


def row_first(lane):
    return (lane // EDGE) % EDGE == 0


def row_last(lane):
    return (lane // EDGE) % EDGE == EDGE - 1


def cell_first(lane):
    return lane % EDGE == 0


def cell_last(lane):
    return lane % EDGE == EDGE - 1


def roll(value, amount):
    return pltpu.roll(value, amount % TILE, 1)


def swap(value):
    return roll(value, FACE)


def tile_of(value, k):
    return value[:, k * TILE : (k + 1) * TILE]


def occupancy_tile(words, tile):
    lane = lane_ids(words.shape[0]) + tile * TILE
    first, last = (tile * TILE) // BITS, (tile * TILE + TILE - 1) // BITS
    word = jnp.broadcast_to(words[:, first : first + 1], lane.shape)
    place = lane - first * BITS
    for w in range(first + 1, last + 1):
        past = lane >= w * BITS
        word = jnp.where(past, jnp.broadcast_to(words[:, w : w + 1], lane.shape), word)
        place = jnp.where(past, lane - w * BITS, place)
    return (jnp.right_shift(word, place) & 1).astype(F32)


def spread(occ, leaf):
    part = jnp.broadcast_to(occ[leaf : leaf + 1, :], (16, TILE)).astype(BF)
    return jnp.concatenate([part] * (CH // 16), axis=0)


def masked_tiles(field_ref, occ, leaf):
    return [
        field_ref[leaf, :, k * TILE : (k + 1) * TILE] * spread(occ[k], leaf) for k in range(4)
    ]


def reorder(tiles):
    n0, n1, n2, n3 = tiles
    r0, r1, r2, r3 = [swap(t) for t in tiles]
    order = [pick(left, n0, r2), pick(left, r0, n2), pick(left, n1, r3), pick(left, r1, n3)]
    flipped = [pick(left, n2, r0), pick(left, r2, n0), pick(left, n3, r1), pick(left, r3, n1)]
    return order, flipped


def restore(t0, t1, t2, t3):
    return [
        pick(left, t0, swap(t1)),
        pick(left, t2, swap(t3)),
        pick(left, swap(t0), t1),
        pick(left, swap(t2), t3),
    ]


def shift_q(center, flipped, q):
    test = row_last if q < 0 else row_first
    return [roll(pick(test, m, c), -q * EDGE) for m, c in zip(flipped, center)]


def write_tables(near, all_ref, own_ref, far_ref, flags_ref):
    leaves = near.shape[0]
    first = lax.axis_index("dom") * leaves
    slot = near - first
    absent = near < 0
    here = (slot >= 0) & (slot < leaves) & jnp.logical_not(absent)
    other = jnp.where(slot < 0, slot + leaves, slot - leaves)
    own_ref[...] = jnp.where(here, slot, leaves)
    far_ref[...] = jnp.where(here | absent, leaves, other)
    all_ref[...] = jnp.where(absent, 2 * leaves, jnp.where(here, slot, other + leaves))
    column = lax.broadcasted_iota(jnp.int32, near.shape, 1)
    cell = lax.rem(jnp.where(column < 13, column, column + 1), 3)
    flags = [
        jnp.max(jnp.where(present, 1, 0).astype(F32), axis=1, keepdims=True)
        for present in (
            jnp.logical_not(absent) & (cell == 0),
            jnp.logical_not(absent) & (cell == 2),
        )
    ]
    some = jnp.max(jnp.maximum(*flags), axis=0, keepdims=True)
    lane = lane_ids(leaves)
    table = jnp.where(lane == 0, flags[0], jnp.where(lane == 1, flags[1], some))
    flags_ref[...] = table.astype(jnp.int32)


def prepare_kernel(
    meta_ref, x_ref, d_ref, cross_ref, chip_ref, store, flip, store_dy, flip_dy, occ_ref,
    all_ref, own_ref, far_ref, flags_ref,
):
    leaves = x_ref.shape[0]
    words = meta_ref[:, NEAR:]
    occ = [occupancy_tile(words, k) for k in range(4)]
    occ_ref[...] = jnp.concatenate(occ, axis=1)
    write_tables(meta_ref[:, 0:NEAR], all_ref, own_ref, far_ref, flags_ref)
    first_core = lax.rem(lax.axis_index("dom"), 2) == 0
    for leaf in range(leaves):
        x_tiles, d_tiles = masked_tiles(x_ref, occ, leaf), masked_tiles(d_ref, occ, leaf)
        up = pick(left, swap(d_tiles[3]), x_tiles[3])
        down = pick(left, x_tiles[0], swap(d_tiles[0]))
        cross_ref[leaf] = jnp.where(first_core, down, up)
        chip_ref[leaf] = jnp.where(first_core, up, down)
        for tiles, order_ref, flip_ref in ((x_tiles, store, flip), (d_tiles, store_dy, flip_dy)):
            order, flipped = reorder(tiles)
            order_ref[leaf] = jnp.concatenate(order, axis=1)
            flip_ref[leaf] = jnp.concatenate(flipped, axis=1)
    for ref in (store, flip, store_dy, flip_dy):
        ref[leaves] = jnp.zeros(ref.shape[1:], BF)


def prepare(meta, x, dy):
    leaves = x.shape[0]
    planes = jax.ShapeDtypeStruct((leaves, CH, TILE), BF)
    store = jax.ShapeDtypeStruct((leaves + 1,) + x.shape[1:], BF)
    table = jax.ShapeDtypeStruct((leaves, NEAR), jnp.int32)
    return pl.pallas_call(
        prepare_kernel,
        out_shape=(planes,) * 2
        + (store,) * 4
        + (jax.ShapeDtypeStruct((leaves, 4 * TILE), F32),)
        + (table,) * 3
        + (jax.ShapeDtypeStruct((leaves, TILE), jnp.int32),),
        in_specs=[vmem_spec()] * 3,
        out_specs=(vmem_spec(),) * 11,
        cost_estimate=cost(10**6, 4 * 10**6),
        compiler_params=params(),
        name="prepare",
    )(meta, x, dy)


def split_far(cross_ref, chip_ref, leaf):
    first_core = lax.rem(lax.axis_index("dom"), 2) == 0
    low = jnp.where(first_core, chip_ref[leaf], cross_ref[leaf])
    high = jnp.where(first_core, cross_ref[leaf], chip_ref[leaf])
    return low, high


def with_far(store, own, cross_ref, chip_ref, turned):
    leaves = own.shape[0] - 1
    for leaf in range(leaves):
        store[leaf] = own[leaf]
        low, high = split_far(cross_ref, chip_ref, leaf)
        store[leaves + leaf, :, 0:TILE] = swap(low) if turned else low
        store[leaves + leaf, :, 3 * TILE :] = swap(high) if turned else high
    store[2 * leaves] = own[leaves]


def place(table_ref, leaf, p, q, z):
    if (p, q, z) == (0, 0, 0):
        return leaf
    return table_ref[leaf, column_of(p, q, z)]


def third(flags_ref, leaf, z):
    return flags_ref[leaf, 0 if z < 0 else 1] > 0


def any_third(flags_ref):
    return flags_ref[0, 2] > 0


def stacked(store, flip, table_ref, leaf, z):
    rows = {}
    center = None
    for q in (0, -1, 1):
        mid = place(table_ref, leaf, 0, q, z)
        after = place(table_ref, leaf, 1, q, z)
        before = place(table_ref, leaf, -1, q, z)
        mine = store[mid]
        past = pick(left, store[after, :, 0:TILE], tile_of(mine, 0))
        ahead = pick(left, tile_of(mine, 3), store[before, :, 3 * TILE :])
        if q == 0:
            center = [swap(ahead)] + [tile_of(mine, k) for k in range(4)] + [swap(past)]
            rows[q] = center
        else:
            other = flip[jnp.minimum(mid, flip.shape[0] - 1)]
            flipped = [ahead] + [tile_of(other, k) for k in range(4)] + [past]
            rows[q] = shift_q(center, flipped, q)
    return jnp.concatenate([jnp.concatenate(rows[q], axis=1) for q in (-1, 0, 1)], axis=0)


def unstack(stack):
    return jnp.concatenate([stack[:, i * TILE : (i + 4) * TILE] for i in range(3)], axis=0)


def shift_c(value, r):
    if r == 0:
        return value
    test = cell_last if r > 0 else cell_first
    tiles = [tile_of(value, k) for k in range(value.shape[1] // TILE)]
    return jnp.concatenate([pick(test, jnp.zeros_like(t), roll(t, -r)) for t in tiles], axis=1)


def across_c(value, z):
    test = cell_last if z > 0 else cell_first
    tiles = [tile_of(value, k) for k in range(value.shape[1] // TILE)]
    return jnp.concatenate(
        [pick(test, roll(t, z * (EDGE - 1)), jnp.zeros_like(t)) for t in tiles], axis=1
    )


CONTRACT_LANES = (((1,), (1,)), ((), ()))


def dot_lanes(a, b):
    return lax.dot_general(a, b, CONTRACT_LANES, preferred_element_type=F32)


def grad_kernel(
    table_ref, flags_ref, store, flip, store_dy, flip_dy, total, stack_ref, stack_dy_ref
):
    leaves = stack_ref.shape[0]
    for leaf in range(leaves):
        stack = stacked(store, flip, table_ref, leaf, 0)
        stack_ref[leaf] = stack
        stack_dy_ref[leaf] = stacked(store_dy, flip_dy, table_ref, leaf, 0)
        wide = jnp.concatenate([shift_c(store_dy[leaf], -r) for r in (-1, 0, 1)], axis=0)
        term = dot_lanes(unstack(stack), wide)
        if leaf == 0:
            total[...] = term
        else:
            total[...] += term

    @pl.when(any_third(flags_ref))
    def _():
        for z in (-1, 1):
            for leaf in range(leaves):

                @pl.when(third(flags_ref, leaf, z))
                def _():
                    stack = stacked(store, flip, table_ref, leaf, z)
                    edge = across_c(store_dy[leaf], -z)
                    total[:, (z + 1) * CH : (z + 2) * CH] += dot_lanes(unstack(stack), edge)


def grad_terms(table, flags, store, flip, store_dy, flip_dy):
    leaves = store.shape[0] - 1
    stack = jax.ShapeDtypeStruct((leaves,) + STACK, BF)
    return pl.pallas_call(
        grad_kernel,
        out_shape=(jax.ShapeDtypeStruct((KROWS, 3 * CH), F32), stack, stack),
        in_specs=[smem_spec()] * 2 + [vmem_spec()] * 4,
        out_specs=(vmem_spec(),) * 3,
        cost_estimate=cost(10**9, 2 * 10**6),
        compiler_params=params(),
        name="grad_terms",
    )(table, flags, store, flip, store_dy, flip_dy)


def third_part(row):
    return (KROWS + row, 0) if row < SPLIT else (KROWS + row - SPLIT, 1)


def grad_far_kernel(
    table_ref, flags_ref, store_dy, cross_ref, chip_ref, near_total, keep_ref, send_ref,
    store, packed,
):
    leaves = store_dy.shape[0] - 1
    for leaf in range(leaves):
        low, high = split_far(cross_ref, chip_ref, leaf)
        store[0, leaf], store[1, leaf] = low, high
        store[2, leaf], store[3, leaf] = swap(low), swap(high)
    for i in range(4):
        store[i, leaves] = jnp.zeros((CH, TILE), BF)

    def far_rows(p, one, two, z):
        at = lambda leaf, q: place(table_ref, leaf, p, q, z)
        first, second = (0, 2) if p > 0 else (3, 1)
        pair = lambda a, b, q: pick(left, store[first, at(a, q)], store[second, at(b, q)])
        center = pair(one, two, 0)
        sides = [shift_q([center], [pair(two, one, q)], q)[0] for q in (-1, 1)]
        return jnp.concatenate([sides[0], center, sides[1]], axis=0)

    def end_plane(p, one, two):
        if p > 0:
            return pick(left, swap(store_dy[one, :, 3 * TILE :]), store_dy[two, :, 3 * TILE :])
        return pick(left, store_dy[one, :, 0:TILE], swap(store_dy[two, :, 0:TILE]))

    pairs = [(leaf, leaf + 1) for leaf in range(0, leaves, 2)]
    for p in (-1, 0, 1):
        term = None
        if p != 0:
            rows = jnp.concatenate([far_rows(p, a, b, 0) for a, b in pairs], axis=1)
            planes = jnp.concatenate([end_plane(p, a, b) for a, b in pairs], axis=1)
            wide = jnp.concatenate([shift_c(planes, -r) for r in (-1, 0, 1)], axis=0)
            term = dot_lanes(rows, wide)
        for q in (-1, 0, 1):
            row = SHIFTS.index((p, q)) * CH
            block = near_total[row : row + CH, :]
            if p != 0:
                block = block + term[(q + 1) * CH : (q + 2) * CH, :]
            packed[row : row + CH, :] = block[:, 0:TILE]
            low, side = third_part(row)
            packed[low : low + CH, side * CH : (side + 1) * CH] = block[:, TILE:]
    packed[2 * KROWS - SPLIT :, CH:] = jnp.zeros((2 * SPLIT - KROWS, CH), F32)

    @pl.when(any_third(flags_ref))
    def _():
        for z in (-1, 1):
            for leaf in range(leaves):

                @pl.when(third(flags_ref, leaf, z))
                def _():
                    for p in (-1, 1):
                        plane = end_plane(p, leaf, leaf)
                        plane = across_c(pick(left, plane, jnp.zeros_like(plane)), -z)
                        term = dot_lanes(far_rows(p, leaf, leaf, z), plane)
                        for q in (-1, 0, 1):
                            row, side = SHIFTS.index((p, q)) * CH, 0
                            if z > 0:
                                row, side = third_part(row)
                            packed[row : row + CH, side * CH : (side + 1) * CH] += term[
                                (q + 1) * CH : (q + 2) * CH, :
                            ]

    core = lax.rem(lax.axis_index("dom"), 2)
    rows = packed.shape[0] // 2
    keep_ref[...] = packed[pl.ds(pl.multiple_of(core * rows, 8), rows), :]
    send_ref[...] = packed[pl.ds(pl.multiple_of((1 - core) * rows, 8), rows), :]


def grad_far(table, flags, store_dy, cross, chip, total):
    leaves = store_dy.shape[0] - 1
    rows = KROWS + SPLIT
    shape = jax.ShapeDtypeStruct((rows // 2, TILE), F32)
    return pl.pallas_call(
        grad_far_kernel,
        out_shape=(shape, shape),
        in_specs=[smem_spec()] * 2 + [vmem_spec()] * 4,
        out_specs=(vmem_spec(), vmem_spec()),
        scratch_shapes=[
            pltpu.VMEM((4, leaves + 1, CH, TILE), BF),
            pltpu.VMEM((rows, TILE), F32),
        ],
        cost_estimate=cost(10**8, 2 * 10**6),
        compiler_params=params(),
        name="grad_far",
    )(table, flags, store_dy, cross, chip, total)


def vmem_spec():
    return pl.BlockSpec(memory_space=pltpu.VMEM)


def any_spec():
    return pl.BlockSpec(memory_space=pl.ANY)


def smem_spec():
    return pl.BlockSpec(memory_space=pltpu.SMEM)


def params():
    return pltpu.CompilerParams(vmem_limit_bytes=VMEM_LIMIT)


def cost(flops, bytes_accessed):
    return pl.CostEstimate(flops=flops, bytes_accessed=bytes_accessed, transcendentals=0)


def ordered_taps(w_ref, turned):
    def tap(index, r):
        p, q = SHIFTS[index]
        return (p + 1) * 9 + (q + 1) * 3 + r + 1

    if turned:
        return jnp.concatenate(
            [
                jnp.concatenate([w_ref[26 - tap(index, r)] for index in range(9)], axis=1)
                for r in (-1, 0, 1)
            ],
            axis=0,
        )
    return jnp.concatenate(
        [
            jnp.concatenate([w_ref[tap(index, r)] for r in (-1, 0, 1)], axis=1)
            for index in range(9)
        ],
        axis=0,
    ).T


def finish(occ, leaf, total):
    rounded = total.astype(BF)
    tiles = restore(*[tile_of(rounded, k) for k in range(4)])
    return jnp.concatenate([t * spread(occ[k], leaf) for k, t in enumerate(tiles)], axis=1)


def leaf_sum(taps, near_x):
    wide = jnp.dot(taps, near_x, preferred_element_type=F32)
    total = wide[CH : 2 * CH]
    for r in (-1, 1):
        total = total + shift_c(wide[(r + 1) * CH : (r + 2) * CH], r)
    return total


def far_tiles(far, table_ref, leaf):
    at = lambda p, q: place(table_ref, leaf, p, q, 0)
    center = pick(left, far[1, at(-1, 0)], far[1, at(1, 0)])
    flipped = {q: pick(left, far[0, at(1, q)], far[0, at(-1, q)]) for q in (-1, 1)}
    sides = [shift_q([center], [flipped[q]], q)[0] for q in (-1, 1)]
    return jnp.concatenate([sides[0], center, sides[1]], axis=0)


def conv_kernel(
    turned, far_table_ref, all_table_ref, flags_ref, occ_ref, own, flip, cross_ref, chip_ref, w_ref,
    stack_ref, _, out_ref, done_ref, far, store,
):
    leaves = out_ref.shape[0]
    occ = [tile_of(occ_ref[...], k) for k in range(4)]
    done_ref[...] = jnp.zeros(done_ref.shape, F32)
    taps = ordered_taps(w_ref, turned)
    for leaf in range(leaves):
        low, high = split_far(cross_ref, chip_ref, leaf)
        both = pick(left, high, low) if turned else pick(left, low, high)
        far[0, leaf], far[1, leaf] = (swap(both), both) if turned else (both, swap(both))
    far[0, leaves] = far[1, leaves] = jnp.zeros((CH, TILE), BF)
    for leaf in range(leaves):
        planes = far_tiles(far, far_table_ref, leaf)
        zero = jnp.zeros_like(planes)
        stack = stack_ref[leaf]
        stack = jnp.concatenate(
            [
                tile_of(stack, 0) + pick(left, planes, zero),
                stack[:, TILE : 5 * TILE],
                tile_of(stack, 5) + pick(left, zero, planes),
            ],
            axis=1,
        )
        out_ref[leaf] = finish(occ, leaf, leaf_sum(taps, unstack(stack)))

    @pl.when(any_third(flags_ref))
    def _():
        with_far(store, own, cross_ref, chip_ref, turned)
        for leaf in range(leaves):
            total = leaf_sum(taps, unstack(stacked(store, flip, all_table_ref, leaf, 0)))
            for z in (-1, 1):
                near_z = unstack(stacked(store, flip, all_table_ref, leaf, z))
                part = jnp.dot(
                    taps[(z + 1) * CH : (z + 2) * CH], near_z, preferred_element_type=F32
                )
                total = total + across_c(part, z)
            out_ref[leaf] = finish(occ, leaf, total)


def conv(far_table, all_table, flags, occ, own, flip, cross, chip, weight, stack, after, turned):
    leaves = stack.shape[0]
    return pl.pallas_call(
        functools.partial(conv_kernel, turned),
        out_shape=(
            jax.ShapeDtypeStruct((leaves, CH, 4 * TILE), BF),
            jax.ShapeDtypeStruct((8, TILE), F32),
        ),
        in_specs=[smem_spec()] * 3 + [vmem_spec()] * 7 + [any_spec()],
        out_specs=(vmem_spec(),) * 2,
        scratch_shapes=[
            pltpu.VMEM((2, leaves + 1, CH, TILE), BF),
            pltpu.VMEM((2 * leaves + 1, CH, 4 * TILE), BF),
        ],
        cost_estimate=cost(10**9, 2 * 10**6),
        compiler_params=params(),
        name="in_grad_conv" if turned else "out_conv",
    )(far_table, all_table, flags, occ, own, flip, cross, chip, weight, stack, after)


def split_kernel(keep_ref, got_ref, *refs):
    *out_refs, total = refs
    total[...] = keep_ref[...] + got_ref[...]
    lane = lax.rem(lax.axis_index("dom") // 2, 4)
    rows = out_refs[0].shape[0]
    for mask, out_ref in enumerate(out_refs):
        at = pl.multiple_of(jnp.bitwise_xor(lane, mask) * rows, 8)
        out_ref[...] = total[pl.ds(at, rows), :]


def split_chunks(keep, got):
    chunk = jax.ShapeDtypeStruct((keep.shape[0] // 4, TILE), F32)
    return pl.pallas_call(
        split_kernel,
        out_shape=(chunk,) * 4,
        in_specs=[vmem_spec()] * 2,
        out_specs=(vmem_spec(),) * 4,
        scratch_shapes=[pltpu.VMEM(keep.shape, F32)],
        cost_estimate=cost(10**5, 10**6),
        compiler_params=params(),
        name="split_chunks",
    )(keep, got)


def sum_kernel(own_ref, *refs):
    *got_refs, _, out_ref = refs
    total = own_ref[...]
    for got_ref in got_refs:
        total = total + got_ref[...]
    out_ref[...] = total


def sum_chunks(own, got, after):
    return pl.pallas_call(
        sum_kernel,
        out_shape=jax.ShapeDtypeStruct(own.shape, F32),
        in_specs=[vmem_spec()] * (1 + len(got)) + [any_spec()],
        out_specs=vmem_spec(),
        cost_estimate=cost(10**5, 3 * 10**5),
        compiler_params=params(),
        name="sum_chunks",
    )(own, *got, after)


def join_kernel(*refs):
    *parts, _, out_ref = refs
    lane = lax.rem(lax.axis_index("dom") // 2, 4)
    rows = parts[0].shape[0]
    for mask, part in enumerate(parts):
        at = pl.multiple_of(jnp.bitwise_xor(lane, mask) * rows, 8)
        out_ref[pl.ds(at, rows), :] = part[...]


def join_chunks(parts, after):
    rows = parts[0].shape[0]
    return pl.pallas_call(
        join_kernel,
        out_shape=jax.ShapeDtypeStruct((len(parts) * rows, TILE), F32),
        in_specs=[vmem_spec()] * len(parts) + [any_spec()],
        out_specs=vmem_spec(),
        cost_estimate=cost(10**5, 5 * 10**5),
        compiler_params=params(),
        name="join_chunks",
    )(*parts, after)


def unpack_kernel(scale, own_ref, other_ref, out_ref, total):
    core = lax.rem(lax.axis_index("dom"), 2)
    rows = own_ref.shape[0]
    total[pl.ds(pl.multiple_of(core * rows, 8), rows), :] = own_ref[...] * scale
    total[pl.ds(pl.multiple_of((1 - core) * rows, 8), rows), :] = other_ref[...] * scale
    for index, (p, q) in enumerate(SHIFTS):
        for r in (-1, 0, 1):
            tap = (p + 1) * 9 + (q + 1) * 3 + r + 1
            row, side = index * CH, r + 1
            if r == 1:
                row, side = third_part(row)
            out_ref[tap] = total[row : row + CH, side * CH : (side + 1) * CH]


def unpack(own, other, scale):
    return pl.pallas_call(
        functools.partial(unpack_kernel, scale),
        out_shape=jax.ShapeDtypeStruct((27, CH, CH), F32),
        in_specs=[vmem_spec(), vmem_spec()],
        out_specs=vmem_spec(),
        scratch_shapes=[pltpu.VMEM((2 * own.shape[0], TILE), F32)],
        cost_estimate=cost(10**6, 10**6),
        compiler_params=params(),
        name="unpack_grad",
    )(own, other)


def exchange(array, mask, size):
    return lax.ppermute(array, "dom", [(i, i ^ mask) for i in range(size)])


def shards(features, cotangent, weight, mask_words, neighbors):
    leaves, channels, voxels = features.shape
    size = lax.axis_size("dom")
    meta = jnp.concatenate([neighbors, mask_words], axis=1)
    to_cross, to_chip, *fields, occ, all_table, own_table, far_table, flags = prepare(
        meta, features, cotangent
    )
    store, flip, store_dy, flip_dy = fields
    between = [(i, i + 1) for i in range(1, size - 1, 2)]
    cross = lax.ppermute(to_cross, "dom", between + [(j, i) for i, j in between])
    chip = exchange(to_chip, 1, size)

    total, stack, stack_dy = grad_terms(own_table, flags, *fields)
    keep, send = grad_far(far_table, flags, store_dy, cross, chip, total)
    own, *to_send = split_chunks(keep, exchange(send, 1, size))
    got = [exchange(part, 2 * m, size) for m, part in zip((1, 2, 3), to_send)]
    out_features, out_done = conv(
        far_table, all_table, flags, occ, store, flip, cross, chip, weight, stack,
        to_send[2], False,
    )
    own = sum_chunks(own, got, out_done)
    if size > GROUP:
        groups = [[j * GROUP + i for j in range(size // GROUP)] for i in range(GROUP)]
        own = lax.psum(own, "dom", axis_index_groups=groups)
    back = [exchange(own, 2 * m, size) for m in (1, 2, 3)]
    in_grad, in_done = conv(
        far_table, all_table, flags, occ, store_dy, flip_dy, cross, chip, weight, stack_dy,
        own, True,
    )
    half = join_chunks([own] + back, in_done)
    other = exchange(half, 1, size)
    scale = float(size * leaves * voxels) ** -0.5
    return (out_features, in_grad, unpack(half, other, scale))


def solution(mesh):
    split = P(("scene", "dom"), None, None)
    flat = P(("scene", "dom"), None)
    return jax.shard_map(
        shards,
        mesh=mesh,
        in_specs=(split, split, P(), flat, flat),
        out_specs=(split, split, P("scene", None, None)),
        check_vma=False,
    )
```

time: 42 us -> 36.3 us (0.86)
  local copies, waits for them, and re-layouts: 4.74 us -> 2.09 us
  Pallas kernels: 14.9 us -> 13.4 us
  other arithmetic: 1.85 us -> 0.78 us
    unnamed x18 -> x6, local copies, waits for them, and re-layouts: 4.71 us -> 2.09 us
    pallas_call x1, Pallas kernels: 2.54 us -> 1.45 us  [grad_far(): pl.pallas_call(grad_far_kernel, out_shape=(shape, shape), in_specs=[smem_...]
    add x1 -> x0, other arithmetic: 1.07 us -> none  [shards(): keep = keep + exchange(send, 1, size)]
    pallas_call x3 -> x4, Pallas kernels: 8.08 us -> 7.71 us  [the longest x2 7.04 us: conv(): pl.pallas_call(functools.partial(conv_kernel, turned), out_shape=(jax.Sha...]
  transfers between devices with their start and end apart: 10 -> 10, of which waited for: 3 -> 4; matrix products, arithmetic and copies ran while one was open for 0% -> 0% of each run, Pallas kernels for 26% -> 28%
where the time goes in v6:
time: 36.3 us; the launch traced here: 36.1 us
  starting transfers between devices  14.2 us (39%)
  Pallas kernels  13.4 us (37%)
  waiting for transfers between devices  4.89 us (13%)
  local copies, waits for them, and re-layouts  2.09 us (6%)
  other arithmetic  0.78 us (2%)
  between operations  0.71 us (2%)
    ppermute x9, starting transfers between devices, exchange(): return lax.ppermute(array, 'dom', [(i, i ^ mask) for i in range(size)])  13.5 us
    pallas_call x2, Pallas kernels, conv(): pl.pallas_call(functools.partial(conv_kernel, turned), out_shape=(jax.Sha...  7.04 us
    ppermute x9, waiting for transfers between devices, exchange(): return lax.ppermute(array, 'dom', [(i, i ^ mask) for i in range(size)])  4.89 us
    pallas_call x1, Pallas kernels, grad_terms(): pl.pallas_call(grad_kernel, out_shape=(jax.ShapeDtypeStruct((KROWS, 3 * C...  3.05 us
    unnamed x6, local copies, waits for them, and re-layouts  2.09 us
    pallas_call x1, Pallas kernels, grad_far(): pl.pallas_call(grad_far_kernel, out_shape=(shape, shape), in_specs=[smem_...  1.45 us
    pallas_call x1, Pallas kernels, unpack(): pl.pallas_call(functools.partial(unpack_kernel, scale), out_shape=jax.Sha...  1.16 us
    concatenate x1, other arithmetic, shards(): meta = jnp.concatenate([neighbors, mask_words], axis=1)  0.78 us
  transfers between devices with their start and end apart: 10, of which 4 were waited for; matrix products, arithmetic and copies ran while one was open for 0% of the time, Pallas kernels for 28%

profile of v6, /device:TPU:0, one launch (start us, length us, event | category | flops | bytes accessed | tf_op | source)
XLA Modules:
  0.0 36.1 jit_solution(15919068795309742681)
XLA Ops:
  0.6 0.8 %pad_add_fusion.meta_ref = s32[8,44]{1,0:T(8,128)S(1)} fusion(s32[8,18]{1,0:T(8,128)} %param.8, s32[8,26]{1,0:T(8,128)} %param.9), kind=kLoop, calls=%fused_computation | loop fusion | flops 352 | bytes 2816 | tf_op jit(solution)/shard_map/concatenate | solution.py:629
  1.4 0.0 copy-start.1
  1.4 1.0 %copy-done.1 = bf16[8,64,512]{2,1,0:T(8,128)(2,1)S(1)} copy-done((bf16[8,64,512]{2,1,0:T(8,128)(2,1)S(1)}, bf16[8,64,512]{2,1,0:T(8,128)(2,1)}, u32[]{:S(2)}) %copy-start.1) | copy-done | bytes 524312
  2.5 0.0 copy-start.2
  2.5 1.0 %copy-done.2 = bf16[8,64,512]{2,1,0:T(8,128)(2,1)S(1)} copy-done((bf16[8,64,512]{2,1,0:T(8,128)(2,1)S(1)}, bf16[8,64,512]{2,1,0:T(8,128)(2,1)}, u32[]{:S(2)}) %copy-start.2) | copy-done | bytes 524312
  3.5 0.6 %prepare.1 = (bf16[8,64,128]{2,1,0:T(8,128)(2,1)S(1)}, bf16[8,64,128]{2,1,0:T(8,128)(2,1)S(1)}, bf16[9,64,512]{2,1,0:T(8,128)(2,1)S(1)}, bf16[9,64,512]{2,1,0:T(...) custom-call(s32[8,44]{1,0:T(8,128)S(1)} %pad_add_fusion.meta_ref, ...), custom_call_target="tpu_custom_call" | custom-call | flops 1000000 | bytes 4000000 | tf_op jit(solution)/shard_map/prepare/pallas_call | solution.py:179
  4.1 0.7 %collective-permute-start = (bf16[8,64,128]{2,1,0:T(8,128)(2,1)S(1)}, bf16[8,64,128]{2,1,0:T(8,128)(2,1)S(1)}, u32[]{:S(2)}, u32[]{:S(2)}) collective-permute-start(bf16[8,64,128]{2,1,0:T(8,128)(2,1)S(1)} %get-tuple-element.33), channel_id=1, source_target_pairs={{1,2},{3,4},{5,6},{2,1},{4,3},{6,5},{9,10},{11,12},{13,14},{10,9},... | collective-permute-start | bytes 393224 | tf_op jit(solution)/shard_map/ppermute | solution.py:635
  4.8 4.4 %collective-permute-start.1 = (bf16[8,64,128]{2,1,0:T(8,128)(2,1)S(1)}, bf16[8,64,128]{2,1,0:T(8,128)(2,1)S(1)}, u32[]{:S(2)}, u32[]{:S(2)}) collective-permute-start(bf16[8,64,128]{2,1,0:T(8,128)(2,1)S(1)} %get-tuple-element.34), channel_id=1, source_target_pairs={{0,1},{1,0},{2,3},{3,2},{4,5},{5,4},{6,7},{7,6},{8,9},{9,8},{10,11... | collective-permute-start | bytes 393224 | tf_op jit(solution)/shard_map/ppermute | solution.py:623
  9.2 0.0 copy-start
  9.2 3.1 %grad_terms.1 = (f32[576,192]{1,0:T(8,128)S(1)}, bf16[8,192,768]{2,1,0:T(8,128)(2,1)S(1)}, bf16[8,192,768]{2,1,0:T(8,128)(2,1)S(1)}) custom-call(s32[8,26]{1,0:T(8,128)S(1)} %get-tuple-element.35.table_ref, s32[8,128]{1,0:T(8,128)S(1)} %get-tuple-element.29.flags_ref, bf16[9,64,512]{2,1,0:T(8,128)(2,1)S(1)} %get-tuple-element.31.store.own, ...), custom_call_target="tpu_custom_call" | custom-call | flops 1000000000 | bytes 2000000 | tf_op jit(solution)/shard_map/grad_terms/pallas_call | solution.py:302
  12.3 0.0 collective-permute-done.cross_ref
  12.3 0.0 collective-permute-done.1.chip_ref
  12.3 1.5 %grad_far.1 = (f32[448,128]{1,0:T(8,128)S(1)}, f32[448,128]{1,0:T(8,128)S(1)}) custom-call(s32[8,26]{1,0:T(8,128)S(1)} %get-tuple-element.27.table_ref.far_table_ref, s32[8,128]{1,0:T(8,128)S(1)} %get-tuple-element.29.flags_ref, bf16[9,64,512]{2,1,0:T(8,128)(2,1)S(1)} %get-tuple-element.36.store_dy.own, ...), custom_call_target="tpu_custom_call" | custom-call | flops 100000000 | bytes 2000000 | tf_op jit(solution)/shard_map/grad_far/pallas_call | solution.py:389
  13.8 0.1 collective-permute-start.2
  13.9 1.5 %collective-permute-done.2.got_ref = f32[448,128]{1,0:T(8,128)S(1)} collective-permute-done((f32[448,128]{1,0:T(8,128)S(1)}, f32[448,128]{1,0:T(8,128)S(1)}, u32[]{:S(2)}, u32[]{:S(2)}) %collective-permute-start.2) | collective-permute-done | bytes 229408 | tf_op jit(solution)/shard_map/ppermute | solution.py:623
  15.4 1.6 %collective-permute-start.3 = (f32[112,128]{1,0:T(8,128)S(1)}, f32[112,128]{1,0:T(8,128)S(1)}, u32[]{:S(2)}, u32[]{:S(2)}) collective-permute-start(f32[112,128]{1,0:T(8,128)S(1)} %get-tuple-element.46), channel_id=1, source_target_pairs={{0,2},{1,3},{2,0},{3,1},{4,6},{5,7},{6,4},{7,5},{8,10},{9,11},{10,... | collective-permute-start | bytes 172040 | tf_op jit(solution)/shard_map/ppermute | solution.py:623
  17.0 2.1 %collective-permute-start.4 = (f32[112,128]{1,0:T(8,128)S(1)}, f32[112,128]{1,0:T(8,128)S(1)}, u32[]{:S(2)}, u32[]{:S(2)}) collective-permute-start(f32[112,128]{1,0:T(8,128)S(1)} %get-tuple-element.47), channel_id=1, source_target_pairs={{0,4},{1,5},{2,6},{3,7},{4,0},{5,1},{6,2},{7,3},{8,12},{9,13},{10,... | collective-permute-start | bytes 172040 | tf_op jit(solution)/shard_map/ppermute | solution.py:623
  19.2 0.7 %collective-permute-start.5 = (f32[112,128]{1,0:T(8,128)S(1)}, f32[112,128]{1,0:T(8,128)S(1)}, u32[]{:S(2)}, u32[]{:S(2)}) collective-permute-start(f32[112,128]{1,0:T(8,128)S(1)} %get-tuple-element.42._), channel_id=1, source_target_pairs={{0,6},{1,7},{2,4},{3,5},{4,2},{5,3},{6,0},{7,1},{8,14},{9,15},{10,... | collective-permute-start | bytes 172040 | tf_op jit(solution)/shard_map/ppermute | solution.py:623
  19.9 0.0 copy-done
  19.9 3.4 %out_conv.1 = (bf16[8,64,512]{2,1,0:T(8,128)(2,1)}, f32[8,128]{1,0:T(8,128)S(1)}) custom-call(s32[8,26]{1,0:T(8,128)S(1)} %get-tuple-element.27.table_ref.far_table_ref, s32[8,26]{1,0:T(8,128)S(1)} %get-tuple-element.28.all_table_ref, s32[8,128]{1,0:T(8,128)S(1)} %get-tuple-element.29.flags_ref, f32[8,512]{1,0:T(8,128)S(1)} %get-tuple-element.30.occ_ref, ...), custom_call_target="tpu_custom_call" | custom-call | flops 1000000000 | bytes 2000000 | tf_op jit(solution)/shard_map/out_conv/pallas_call | solution.py:511
  23.3 0.0 collective-permute-done.3.refs_0_
  23.3 0.8 %collective-permute-done.4.refs_1_ = f32[112,128]{1,0:T(8,128)S(1)} collective-permute-done((f32[112,128]{1,0:T(8,128)S(1)}, f32[112,128]{1,0:T(8,128)S(1)}, u32[]{:S(2)}, u32[]{:S(2)}) %collective-permute-start.4) | collective-permute-done | bytes 57376 | tf_op jit(solution)/shard_map/ppermute | solution.py:623
  24.1 1.2 %collective-permute-done.5.refs_2_ = f32[112,128]{1,0:T(8,128)S(1)} collective-permute-done((f32[112,128]{1,0:T(8,128)S(1)}, f32[112,128]{1,0:T(8,128)S(1)}, u32[]{:S(2)}, u32[]{:S(2)}) %collective-permute-start.5) | collective-permute-done | bytes 57376 | tf_op jit(solution)/shard_map/ppermute | solution.py:623
  25.3 2.0 %collective-permute-start.8 = (f32[112,128]{1,0:T(8,128)S(1)}, f32[112,128]{1,0:T(8,128)S(1)}, u32[]{:S(2)}, u32[]{:S(2)}) collective-permute-start(f32[112,128]{1,0:T(8,128)S(1)} %sum_chunks.1._.refs_0_), channel_id=1, source_target_pairs={{0,6},{1,7},{2,4},{3,5},{4,2},{5,3},{6,0},{7,1},{8,14},{9,15},{10,... | collective-permute-start | bytes 172040 | tf_op jit(solution)/shard_map/ppermute | solution.py:623
  27.3 0.2 collective-permute-start.7
  27.5 2.2 %collective-permute-start.6 = (f32[112,128]{1,0:T(8,128)S(1)}, f32[112,128]{1,0:T(8,128)S(1)}, u32[]{:S(2)}, u32[]{:S(2)}) collective-permute-start(f32[112,128]{1,0:T(8,128)S(1)} %sum_chunks.1._.refs_0_), channel_id=1, source_target_pairs={{0,2},{1,3},{2,0},{3,1},{4,6},{5,7},{6,4},{7,5},{8,10},{9,11},{10,... | collective-permute-start | bytes 172040 | tf_op jit(solution)/shard_map/ppermute | solution.py:623
  29.7 3.6 %in_grad_conv.1 = (bf16[8,64,512]{2,1,0:T(8,128)(2,1)}, f32[8,128]{1,0:T(8,128)S(1)}) custom-call(s32[8,26]{1,0:T(8,128)S(1)} %get-tuple-element.27.table_ref.far_table_ref, s32[8,26]{1,0:T(8,128)S(1)} %get-tuple-element.28.all_table_ref, s32[8,128]{1,0:T(8,128)S(1)} %get-tuple-element.29.flags_ref, f32[8,512]{1,0:T(8,128)S(1)} %get-tuple-element.30.occ_ref, ...), custom_call_target="tpu_custom_call" | custom-call | flops 1000000000 | bytes 2000000 | tf_op jit(solution)/shard_map/in_grad_conv/pallas_call | solution.py:511
  33.3 0.0 collective-permute-done.8.refs_3_
  33.3 0.0 collective-permute-done.7.refs_2_
  33.3 0.0 collective-permute-done.6.refs_1_
  33.4 0.1 collective-permute-start.9
  33.4 1.5 %collective-permute-done.9.other_ref = f32[448,128]{1,0:T(8,128)S(1)} collective-permute-done((f32[448,128]{1,0:T(8,128)S(1)}, f32[448,128]{1,0:T(8,128)S(1)}, u32[]{:S(2)}, u32[]{:S(2)}) %collective-permute-start.9) | collective-permute-done | bytes 229408 | tf_op jit(solution)/shard_map/ppermute | solution.py:623
  34.9 1.2 %unpack_grad.1 = f32[27,64,64]{2,1,0:T(8,128)} custom-call(f32[448,128]{1,0:T(8,128)S(1)} %join_chunks.1.own_ref, f32[448,128]{1,0:T(8,128)S(1)} %collective-permute-done.9.other_ref), custom_call_target="tpu_custom_call" | custom-call | flops 1000000 | bytes 1000000 | tf_op jit(solution)/shard_map/unpack_grad/pallas_call | solution.py:610
  (3 shorter events, 0.1 us)
Async XLA Ops:
  1.4 1.0 %copy-start.1 = (bf16[8,64,512]{2,1,0:T(8,128)(2,1)S(1)}, bf16[8,64,512]{2,1,0:T(8,128)(2,1)}, u32[]{:S(2)}) copy-start(bf16[8,64,512]{2,1,0:T(8,128)(2,1)} %x_ref.1) | copy-start | bytes 1572868
  2.5 1.0 %copy-start.2 = (bf16[8,64,512]{2,1,0:T(8,128)(2,1)S(1)}, bf16[8,64,512]{2,1,0:T(8,128)(2,1)}, u32[]{:S(2)}) copy-start(bf16[8,64,512]{2,1,0:T(8,128)(2,1)} %d_ref.1) | copy-start | bytes 1572868
  4.1 8.2 %collective-permute-start = (bf16[8,64,128]{2,1,0:T(8,128)(2,1)S(1)}, bf16[8,64,128]{2,1,0:T(8,128)(2,1)S(1)}, u32[]{:S(2)}, u32[]{:S(2)}) collective-permute-start(bf16[8,64,128]{2,1,0:T(8,128)(2,1)S(1)} %get-tuple-element.33), channel_id=1, source_target_pairs={{1,2},{3,4},{5,6},{2,1},{4,3},{6,5},{9,10},{11,12},{13,14},{10,9},... | collective-permute-start | bytes 393224 | tf_op jit(solution)/shard_map/ppermute | solution.py:635
  4.8 7.5 %collective-permute-start.1 = (bf16[8,64,128]{2,1,0:T(8,128)(2,1)S(1)}, bf16[8,64,128]{2,1,0:T(8,128)(2,1)S(1)}, u32[]{:S(2)}, u32[]{:S(2)}) collective-permute-start(bf16[8,64,128]{2,1,0:T(8,128)(2,1)S(1)} %get-tuple-element.34), channel_id=1, source_target_pairs={{0,1},{1,0},{2,3},{3,2},{4,5},{5,4},{6,7},{7,6},{8,9},{9,8},{10,11... | collective-permute-start | bytes 393224 | tf_op jit(solution)/shard_map/ppermute | solution.py:623
  9.2 10.6 %copy-start = (bf16[27,64,64]{2,1,0:T(8,128)(2,1)S(1)}, bf16[27,64,64]{2,1,0:T(8,128)(2,1)}, u32[]{:S(2)}) copy-start(bf16[27,64,64]{2,1,0:T(8,128)(2,1)} %w_ref.3) | copy-start | bytes 663556
  13.8 1.6 %collective-permute-start.2 = (f32[448,128]{1,0:T(8,128)S(1)}, f32[448,128]{1,0:T(8,128)S(1)}, u32[]{:S(2)}, u32[]{:S(2)}) collective-permute-start(f32[448,128]{1,0:T(8,128)S(1)} %get-tuple-element.41), channel_id=1, source_target_pairs={{0,1},{1,0},{2,3},{3,2},{4,5},{5,4},{6,7},{7,6},{8,9},{9,8},{10,11... | collective-permute-start | bytes 688136 | tf_op jit(solution)/shard_map/ppermute | solution.py:623
  15.4 7.9 %collective-permute-start.3 = (f32[112,128]{1,0:T(8,128)S(1)}, f32[112,128]{1,0:T(8,128)S(1)}, u32[]{:S(2)}, u32[]{:S(2)}) collective-permute-start(f32[112,128]{1,0:T(8,128)S(1)} %get-tuple-element.46), channel_id=1, source_target_pairs={{0,2},{1,3},{2,0},{3,1},{4,6},{5,7},{6,4},{7,5},{8,10},{9,11},{10,... | collective-permute-start | bytes 172040 | tf_op jit(solution)/shard_map/ppermute | solution.py:623
  17.0 7.0 %collective-permute-start.4 = (f32[112,128]{1,0:T(8,128)S(1)}, f32[112,128]{1,0:T(8,128)S(1)}, u32[]{:S(2)}, u32[]{:S(2)}) collective-permute-start(f32[112,128]{1,0:T(8,128)S(1)} %get-tuple-element.47), channel_id=1, source_target_pairs={{0,4},{1,5},{2,6},{3,7},{4,0},{5,1},{6,2},{7,3},{8,12},{9,13},{10,... | collective-permute-start | bytes 172040 | tf_op jit(solution)/shard_map/ppermute | solution.py:623
  19.2 6.1 %collective-permute-start.5 = (f32[112,128]{1,0:T(8,128)S(1)}, f32[112,128]{1,0:T(8,128)S(1)}, u32[]{:S(2)}, u32[]{:S(2)}) collective-permute-start(f32[112,128]{1,0:T(8,128)S(1)} %get-tuple-element.42._), channel_id=1, source_target_pairs={{0,6},{1,7},{2,4},{3,5},{4,2},{5,3},{6,0},{7,1},{8,14},{9,15},{10,... | collective-permute-start | bytes 172040 | tf_op jit(solution)/shard_map/ppermute | solution.py:623
  25.3 8.1 %collective-permute-start.8 = (f32[112,128]{1,0:T(8,128)S(1)}, f32[112,128]{1,0:T(8,128)S(1)}, u32[]{:S(2)}, u32[]{:S(2)}) collective-permute-start(f32[112,128]{1,0:T(8,128)S(1)} %sum_chunks.1._.refs_0_), channel_id=1, source_target_pairs={{0,6},{1,7},{2,4},{3,5},{4,2},{5,3},{6,0},{7,1},{8,14},{9,15},{10,... | collective-permute-start | bytes 172040 | tf_op jit(solution)/shard_map/ppermute | solution.py:623
  27.3 6.1 %collective-permute-start.7 = (f32[112,128]{1,0:T(8,128)S(1)}, f32[112,128]{1,0:T(8,128)S(1)}, u32[]{:S(2)}, u32[]{:S(2)}) collective-permute-start(f32[112,128]{1,0:T(8,128)S(1)} %sum_chunks.1._.refs_0_), channel_id=1, source_target_pairs={{0,4},{1,5},{2,6},{3,7},{4,0},{5,1},{6,2},{7,3},{8,12},{9,13},{10,... | collective-permute-start | bytes 172040 | tf_op jit(solution)/shard_map/ppermute | solution.py:623
  27.5 5.8 %collective-permute-start.6 = (f32[112,128]{1,0:T(8,128)S(1)}, f32[112,128]{1,0:T(8,128)S(1)}, u32[]{:S(2)}, u32[]{:S(2)}) collective-permute-start(f32[112,128]{1,0:T(8,128)S(1)} %sum_chunks.1._.refs_0_), channel_id=1, source_target_pairs={{0,2},{1,3},{2,0},{3,1},{4,6},{5,7},{6,4},{7,5},{8,10},{9,11},{10,... | collective-permute-start | bytes 172040 | tf_op jit(solution)/shard_map/ppermute | solution.py:623
  33.4 1.6 %collective-permute-start.9 = (f32[448,128]{1,0:T(8,128)S(1)}, f32[448,128]{1,0:T(8,128)S(1)}, u32[]{:S(2)}, u32[]{:S(2)}) collective-permute-start(f32[448,128]{1,0:T(8,128)S(1)} %join_chunks.1.own_ref), channel_id=1, source_target_pairs={{0,1},{1,0},{2,3},{3,2},{4,5},{5,4},{6,7},{7,6},{8,9},{9,8},{10,11... | collective-permute-start | bytes 688136 | tf_op jit(solution)/shard_map/ppermute | solution.py:623

commit v7 on v6

--- a/solution.py
+++ b/solution.py
@@ -592,31 +592,50 @@
     )(*parts, after)
 
 
-def unpack_kernel(scale, own_ref, other_ref, out_ref, total):
-    core = lax.rem(lax.axis_index("dom"), 2)
-    rows = own_ref.shape[0]
-    total[pl.ds(pl.multiple_of(core * rows, 8), rows), :] = own_ref[...] * scale
-    total[pl.ds(pl.multiple_of((1 - core) * rows, 8), rows), :] = other_ref[...] * scale
+def half_taps(half):
+    found = []
     for index, (p, q) in enumerate(SHIFTS):
         for r in (-1, 0, 1):
-            tap = (p + 1) * 9 + (q + 1) * 3 + r + 1
             row, side = index * CH, r + 1
             if r == 1:
                 row, side = third_part(row)
-            out_ref[tap] = total[row : row + CH, side * CH : (side + 1) * CH]
-
-
-def unpack(own, other, scale):
-    return pl.pallas_call(
-        functools.partial(unpack_kernel, scale),
+            if row // (7 * CH) == half:
+                found.append(((p + 1) * 9 + (q + 1) * 3 + r + 1, row - half * 7 * CH, side))
+    return found
+
+
+def unpack_kernel(scale, mine, half_ref, *refs):
+    *_, out_ref, taps, sem = refs
+    core = lax.rem(lax.axis_index("dom"), 2)
+
+    def write(half):
+        found = half_taps(half)
+        for i, (tap, row, side) in enumerate(found):
+            block = half_ref[row : row + CH, side * CH : (side + 1) * CH]
+            taps[i] = block * scale
+            pltpu.make_async_copy(taps.at[i], out_ref.at[tap], sem.at[i]).start()
+        for i, (tap, row, side) in enumerate(found):
+            pltpu.make_async_copy(taps.at[i], out_ref.at[tap], sem.at[i]).wait()
+
+    first = core == 0 if mine else core == 1
+    pl.when(first)(lambda: write(0))
+    pl.when(jnp.logical_not(first))(lambda: write(1))
+
+
+def unpack(half, scale, so_far=None):
+    rest = [] if so_far is None else [so_far]
+    hbm = pl.BlockSpec(memory_space=pltpu.HBM)
+    return pl.pallas_call(
+        functools.partial(unpack_kernel, scale, not rest),
         out_shape=jax.ShapeDtypeStruct((27, CH, CH), F32),
-        in_specs=[vmem_spec(), vmem_spec()],
-        out_specs=vmem_spec(),
-        scratch_shapes=[pltpu.VMEM((2 * own.shape[0], TILE), F32)],
+        in_specs=[vmem_spec()] + [hbm] * len(rest),
+        out_specs=hbm,
+        input_output_aliases={1: 0} if rest else {},
+        scratch_shapes=[pltpu.VMEM((14, CH, CH), F32), pltpu.SemaphoreType.DMA((14,))],
         cost_estimate=cost(10**6, 10**6),
         compiler_params=params(),
-        name="unpack_grad",
-    )(own, other)
+        name="unpack_other" if rest else "unpack_own",
+    )(half, *rest)
 
 
 def exchange(array, mask, size):
@@ -632,13 +651,13 @@
     )
     store, flip, store_dy, flip_dy = fields
     between = [(i, i + 1) for i in range(1, size - 1, 2)]
+    chip = exchange(to_chip, 1, size)
     cross = lax.ppermute(to_cross, "dom", between + [(j, i) for i, j in between])
-    chip = exchange(to_chip, 1, size)
 
     total, stack, stack_dy = grad_terms(own_table, flags, *fields)
     keep, send = grad_far(far_table, flags, store_dy, cross, chip, total)
     own, *to_send = split_chunks(keep, exchange(send, 1, size))
-    got = [exchange(part, 2 * m, size) for m, part in zip((1, 2, 3), to_send)]
+    got = [exchange(to_send[m - 1], 2 * m, size) for m in (2, 3, 1)]
     out_features, out_done = conv(
         far_table, all_table, flags, occ, store, flip, cross, chip, weight, stack,
         to_send[2], False,
@@ -655,7 +674,8 @@
     half = join_chunks([own] + back, in_done)
     other = exchange(half, 1, size)
     scale = float(size * leaves * voxels) ** -0.5
-    return (out_features, in_grad, unpack(half, other, scale))
+    weight_grad = unpack(other, scale, unpack(half, scale))
+    return (out_features, in_grad, weight_grad)
 
 
 def solution(mesh):

time: 36.3 us -> 36.1 us (level)
  waiting for transfers between devices: 4.89 us -> 3.83 us
  Pallas kernels: 13.4 us -> 14.1 us
    ppermute x9, waiting for transfers between devices: 4.89 us -> 3.82 us  [exchange(): return lax.ppermute(array, 'dom', [(i, i ^ mask) for i in range(size)])]
    pallas_call x1 -> x2, Pallas kernels: 1.16 us -> 1.84 us  [unpack(): pl.pallas_call(functools.partial(unpack_kernel, scale, not rest), out_sha...]
  transfers between devices with their start and end apart: 10 -> 10, of which waited for: 4 -> 3; matrix products, arithmetic and copies ran while one was open for 0% -> 0% of each run, Pallas kernels for 28% -> 31%
where the time goes in v7:
time: 36.1 us; the launch traced here: 35.9 us
  starting transfers between devices  14.2 us (39%)
  Pallas kernels  14.1 us (39%)
  waiting for transfers between devices  3.83 us (11%)
  local copies, waits for them, and re-layouts  2.09 us (6%)
  between operations  0.9 us (2%)
  other arithmetic  0.78 us (2%)
    ppermute x9, starting transfers between devices, exchange(): return lax.ppermute(array, 'dom', [(i, i ^ mask) for i in range(size)])  13.5 us
    pallas_call x2, Pallas kernels, conv(): pl.pallas_call(functools.partial(conv_kernel, turned), out_shape=(jax.Sha...  7.04 us
    ppermute x9, waiting for transfers between devices, exchange(): return lax.ppermute(array, 'dom', [(i, i ^ mask) for i in range(size)])  3.82 us
    pallas_call x1, Pallas kernels, grad_terms(): pl.pallas_call(grad_kernel, out_shape=(jax.ShapeDtypeStruct((KROWS, 3 * C...  3.05 us
    unnamed x6, local copies, waits for them, and re-layouts  2.09 us
    pallas_call x2, Pallas kernels, unpack(): pl.pallas_call(functools.partial(unpack_kernel, scale, not rest), out_sha...  1.84 us
    pallas_call x1, Pallas kernels, grad_far(): pl.pallas_call(grad_far_kernel, out_shape=(shape, shape), in_specs=[smem_...  1.45 us
    concatenate x1, other arithmetic, shards(): meta = jnp.concatenate([neighbors, mask_words], axis=1)  0.78 us
  transfers between devices with their start and end apart: 10, of which 3 were waited for; matrix products, arithmetic and copies ran while one was open for 0% of the time, Pallas kernels for 31%

profile of v7, /device:TPU:0, one launch (start us, length us, event | category | flops | bytes accessed | tf_op | source)
XLA Modules:
  0.0 35.9 jit_solution(9592369595388089774)
XLA Ops:
  0.6 0.8 %pad_add_fusion.meta_ref = s32[8,44]{1,0:T(8,128)S(1)} fusion(s32[8,18]{1,0:T(8,128)} %param.8, s32[8,26]{1,0:T(8,128)} %param.9), kind=kLoop, calls=%fused_computation | loop fusion | flops 352 | bytes 2816 | tf_op jit(solution)/shard_map/concatenate | solution.py:648
  1.4 0.0 copy-start.1
  1.4 1.0 %copy-done.1 = bf16[8,64,512]{2,1,0:T(8,128)(2,1)S(1)} copy-done((bf16[8,64,512]{2,1,0:T(8,128)(2,1)S(1)}, bf16[8,64,512]{2,1,0:T(8,128)(2,1)}, u32[]{:S(2)}) %copy-start.1) | copy-done | bytes 524312
  2.5 0.0 copy-start.2
  2.5 1.0 %copy-done.2 = bf16[8,64,512]{2,1,0:T(8,128)(2,1)S(1)} copy-done((bf16[8,64,512]{2,1,0:T(8,128)(2,1)S(1)}, bf16[8,64,512]{2,1,0:T(8,128)(2,1)}, u32[]{:S(2)}) %copy-start.2) | copy-done | bytes 524312
  3.5 0.6 %prepare.1 = (bf16[8,64,128]{2,1,0:T(8,128)(2,1)S(1)}, bf16[8,64,128]{2,1,0:T(8,128)(2,1)S(1)}, bf16[9,64,512]{2,1,0:T(8,128)(2,1)S(1)}, bf16[9,64,512]{2,1,0:T(...) custom-call(s32[8,44]{1,0:T(8,128)S(1)} %pad_add_fusion.meta_ref, ...), custom_call_target="tpu_custom_call" | custom-call | flops 1000000 | bytes 4000000 | tf_op jit(solution)/shard_map/prepare/pallas_call | solution.py:179
  4.1 0.7 %collective-permute-start = (bf16[8,64,128]{2,1,0:T(8,128)(2,1)S(1)}, bf16[8,64,128]{2,1,0:T(8,128)(2,1)S(1)}, u32[]{:S(2)}, u32[]{:S(2)}) collective-permute-start(bf16[8,64,128]{2,1,0:T(8,128)(2,1)S(1)} %get-tuple-element.33), channel_id=1, source_target_pairs={{1,2},{3,4},{5,6},{2,1},{4,3},{6,5},{9,10},{11,12},{13,14},{10,9},... | collective-permute-start | bytes 393224 | tf_op jit(solution)/shard_map/ppermute | solution.py:655
  4.8 4.4 %collective-permute-start.1 = (bf16[8,64,128]{2,1,0:T(8,128)(2,1)S(1)}, bf16[8,64,128]{2,1,0:T(8,128)(2,1)S(1)}, u32[]{:S(2)}, u32[]{:S(2)}) collective-permute-start(bf16[8,64,128]{2,1,0:T(8,128)(2,1)S(1)} %get-tuple-element.34), channel_id=1, source_target_pairs={{0,1},{1,0},{2,3},{3,2},{4,5},{5,4},{6,7},{7,6},{8,9},{9,8},{10,11... | collective-permute-start | bytes 393224 | tf_op jit(solution)/shard_map/ppermute | solution.py:642
  9.2 0.0 copy-start
  9.2 3.1 %grad_terms.1 = (f32[576,192]{1,0:T(8,128)S(1)}, bf16[8,192,768]{2,1,0:T(8,128)(2,1)S(1)}, bf16[8,192,768]{2,1,0:T(8,128)(2,1)S(1)}) custom-call(s32[8,26]{1,0:T(8,128)S(1)} %get-tuple-element.35.table_ref, s32[8,128]{1,0:T(8,128)S(1)} %get-tuple-element.29.flags_ref, bf16[9,64,512]{2,1,0:T(8,128)(2,1)S(1)} %get-tuple-element.31.store.own, ...), custom_call_target="tpu_custom_call" | custom-call | flops 1000000000 | bytes 2000000 | tf_op jit(solution)/shard_map/grad_terms/pallas_call | solution.py:302
  12.3 0.0 collective-permute-done.cross_ref
  12.3 0.0 collective-permute-done.1.chip_ref
  12.3 1.5 %grad_far.1 = (f32[448,128]{1,0:T(8,128)S(1)}, f32[448,128]{1,0:T(8,128)S(1)}) custom-call(s32[8,26]{1,0:T(8,128)S(1)} %get-tuple-element.27.table_ref.far_table_ref, s32[8,128]{1,0:T(8,128)S(1)} %get-tuple-element.29.flags_ref, bf16[9,64,512]{2,1,0:T(8,128)(2,1)S(1)} %get-tuple-element.36.store_dy.own, ...), custom_call_target="tpu_custom_call" | custom-call | flops 100000000 | bytes 2000000 | tf_op jit(solution)/shard_map/grad_far/pallas_call | solution.py:389
  13.8 0.1 collective-permute-start.2
  13.9 1.5 %collective-permute-done.2.got_ref = f32[448,128]{1,0:T(8,128)S(1)} collective-permute-done((f32[448,128]{1,0:T(8,128)S(1)}, f32[448,128]{1,0:T(8,128)S(1)}, u32[]{:S(2)}, u32[]{:S(2)}) %collective-permute-start.2) | collective-permute-done | bytes 229408 | tf_op jit(solution)/shard_map/ppermute | solution.py:642
  15.4 2.7 %collective-permute-start.3 = (f32[112,128]{1,0:T(8,128)S(1)}, f32[112,128]{1,0:T(8,128)S(1)}, u32[]{:S(2)}, u32[]{:S(2)}) collective-permute-start(f32[112,128]{1,0:T(8,128)S(1)} %get-tuple-element.46), channel_id=1, source_target_pairs={{0,4},{1,5},{2,6},{3,7},{4,0},{5,1},{6,2},{7,3},{8,12},{9,13},{10,... | collective-permute-start | bytes 172040 | tf_op jit(solution)/shard_map/ppermute | solution.py:642
  18.1 1.1 %collective-permute-start.5 = (f32[112,128]{1,0:T(8,128)S(1)}, f32[112,128]{1,0:T(8,128)S(1)}, u32[]{:S(2)}, u32[]{:S(2)}) collective-permute-start(f32[112,128]{1,0:T(8,128)S(1)} %get-tuple-element.47), channel_id=1, source_target_pairs={{0,2},{1,3},{2,0},{3,1},{4,6},{5,7},{6,4},{7,5},{8,10},{9,11},{10,... | collective-permute-start | bytes 172040 | tf_op jit(solution)/shard_map/ppermute | solution.py:642
  19.2 0.7 %collective-permute-start.4 = (f32[112,128]{1,0:T(8,128)S(1)}, f32[112,128]{1,0:T(8,128)S(1)}, u32[]{:S(2)}, u32[]{:S(2)}) collective-permute-start(f32[112,128]{1,0:T(8,128)S(1)} %get-tuple-element.42._), channel_id=1, source_target_pairs={{0,6},{1,7},{2,4},{3,5},{4,2},{5,3},{6,0},{7,1},{8,14},{9,15},{10,... | collective-permute-start | bytes 172040 | tf_op jit(solution)/shard_map/ppermute | solution.py:642
  19.9 0.0 copy-done
  19.9 3.4 %out_conv.1 = (bf16[8,64,512]{2,1,0:T(8,128)(2,1)}, f32[8,128]{1,0:T(8,128)S(1)}) custom-call(s32[8,26]{1,0:T(8,128)S(1)} %get-tuple-element.27.table_ref.far_table_ref, s32[8,26]{1,0:T(8,128)S(1)} %get-tuple-element.28.all_table_ref, s32[8,128]{1,0:T(8,128)S(1)} %get-tuple-element.29.flags_ref, f32[8,512]{1,0:T(8,128)S(1)} %get-tuple-element.30.occ_ref, ...), custom_call_target="tpu_custom_call" | custom-call | flops 1000000000 | bytes 2000000 | tf_op jit(solution)/shard_map/out_conv/pallas_call | solution.py:511
  23.3 0.0 collective-permute-done.3.refs_0_
  23.3 0.0 collective-permute-done.5.refs_2_
  23.3 1.8 %collective-permute-done.4.refs_1_ = f32[112,128]{1,0:T(8,128)S(1)} collective-permute-done((f32[112,128]{1,0:T(8,128)S(1)}, f32[112,128]{1,0:T(8,128)S(1)}, u32[]{:S(2)}, u32[]{:S(2)}) %collective-permute-start.4) | collective-permute-done | bytes 57376 | tf_op jit(solution)/shard_map/ppermute | solution.py:642
  25.2 1.5 %collective-permute-start.8 = (f32[112,128]{1,0:T(8,128)S(1)}, f32[112,128]{1,0:T(8,128)S(1)}, u32[]{:S(2)}, u32[]{:S(2)}) collective-permute-start(f32[112,128]{1,0:T(8,128)S(1)} %sum_chunks.1._.refs_0_), channel_id=1, source_target_pairs={{0,6},{1,7},{2,4},{3,5},{4,2},{5,3},{6,0},{7,1},{8,14},{9,15},{10,... | collective-permute-start | bytes 172040 | tf_op jit(solution)/shard_map/ppermute | solution.py:642
  26.6 0.0 collective-permute-start.7
  26.6 3.0 %collective-permute-start.6 = (f32[112,128]{1,0:T(8,128)S(1)}, f32[112,128]{1,0:T(8,128)S(1)}, u32[]{:S(2)}, u32[]{:S(2)}) collective-permute-start(f32[112,128]{1,0:T(8,128)S(1)} %sum_chunks.1._.refs_0_), channel_id=1, source_target_pairs={{0,2},{1,3},{2,0},{3,1},{4,6},{5,7},{6,4},{7,5},{8,10},{9,11},{10,... | collective-permute-start | bytes 172040 | tf_op jit(solution)/shard_map/ppermute | solution.py:642
  29.6 3.6 %in_grad_conv.1 = (bf16[8,64,512]{2,1,0:T(8,128)(2,1)}, f32[8,128]{1,0:T(8,128)S(1)}) custom-call(s32[8,26]{1,0:T(8,128)S(1)} %get-tuple-element.27.table_ref.far_table_ref, s32[8,26]{1,0:T(8,128)S(1)} %get-tuple-element.28.all_table_ref, s32[8,128]{1,0:T(8,128)S(1)} %get-tuple-element.29.flags_ref, f32[8,512]{1,0:T(8,128)S(1)} %get-tuple-element.30.occ_ref, ...), custom_call_target="tpu_custom_call" | custom-call | flops 1000000000 | bytes 2000000 | tf_op jit(solution)/shard_map/in_grad_conv/pallas_call | solution.py:511
  33.2 0.0 collective-permute-done.8.refs_3_
  33.2 0.0 collective-permute-done.7.refs_2_
  33.2 0.0 collective-permute-done.6.refs_1_
  33.3 0.1 collective-permute-start.9
  33.3 1.0 %unpack_own.1.refs_0_ = f32[27,64,64]{2,1,0:T(8,128)} custom-call(f32[448,128]{1,0:T(8,128)S(1)} %join_chunks.1.half_ref), custom_call_target="tpu_custom_call" | custom-call | flops 1000000 | bytes 1000000 | tf_op jit(solution)/shard_map/unpack_own/pallas_call | solution.py:628
  34.3 0.5 %collective-permute-done.9.half_ref = f32[448,128]{1,0:T(8,128)S(1)} collective-permute-done((f32[448,128]{1,0:T(8,128)S(1)}, f32[448,128]{1,0:T(8,128)S(1)}, u32[]{:S(2)}, u32[]{:S(2)}) %collective-permute-start.9) | collective-permute-done | bytes 229408 | tf_op jit(solution)/shard_map/ppermute | solution.py:642
  34.8 0.9 %unpack_other.1 = f32[27,64,64]{2,1,0:T(8,128)} custom-call(f32[448,128]{1,0:T(8,128)S(1)} %collective-permute-done.9.half_ref, f32[27,64,64]{2,1,0:T(8,128)} %unpack_own.1.refs_0_), custom_call_target="tpu_custom_call", output_to_operand_aliasing={{}: (1, {})} | custom-call | flops 1000000 | bytes 1000000 | tf_op jit(solution)/shard_map/unpack_other/pallas_call | solution.py:628
  (3 shorter events, 0.1 us)
Async XLA Ops:
  1.4 1.0 %copy-start.1 = (bf16[8,64,512]{2,1,0:T(8,128)(2,1)S(1)}, bf16[8,64,512]{2,1,0:T(8,128)(2,1)}, u32[]{:S(2)}) copy-start(bf16[8,64,512]{2,1,0:T(8,128)(2,1)} %x_ref.1) | copy-start | bytes 1572868
  2.5 1.0 %copy-start.2 = (bf16[8,64,512]{2,1,0:T(8,128)(2,1)S(1)}, bf16[8,64,512]{2,1,0:T(8,128)(2,1)}, u32[]{:S(2)}) copy-start(bf16[8,64,512]{2,1,0:T(8,128)(2,1)} %d_ref.1) | copy-start | bytes 1572868
  4.1 8.2 %collective-permute-start = (bf16[8,64,128]{2,1,0:T(8,128)(2,1)S(1)}, bf16[8,64,128]{2,1,0:T(8,128)(2,1)S(1)}, u32[]{:S(2)}, u32[]{:S(2)}) collective-permute-start(bf16[8,64,128]{2,1,0:T(8,128)(2,1)S(1)} %get-tuple-element.33), channel_id=1, source_target_pairs={{1,2},{3,4},{5,6},{2,1},{4,3},{6,5},{9,10},{11,12},{13,14},{10,9},... | collective-permute-start | bytes 393224 | tf_op jit(solution)/shard_map/ppermute | solution.py:655
  4.8 7.5 %collective-permute-start.1 = (bf16[8,64,128]{2,1,0:T(8,128)(2,1)S(1)}, bf16[8,64,128]{2,1,0:T(8,128)(2,1)S(1)}, u32[]{:S(2)}, u32[]{:S(2)}) collective-permute-start(bf16[8,64,128]{2,1,0:T(8,128)(2,1)S(1)} %get-tuple-element.34), channel_id=1, source_target_pairs={{0,1},{1,0},{2,3},{3,2},{4,5},{5,4},{6,7},{7,6},{8,9},{9,8},{10,11... | collective-permute-start | bytes 393224 | tf_op jit(solution)/shard_map/ppermute | solution.py:642
  9.2 10.6 %copy-start = (bf16[27,64,64]{2,1,0:T(8,128)(2,1)S(1)}, bf16[27,64,64]{2,1,0:T(8,128)(2,1)}, u32[]{:S(2)}) copy-start(bf16[27,64,64]{2,1,0:T(8,128)(2,1)} %w_ref.3) | copy-start | bytes 663556
  13.8 1.6 %collective-permute-start.2 = (f32[448,128]{1,0:T(8,128)S(1)}, f32[448,128]{1,0:T(8,128)S(1)}, u32[]{:S(2)}, u32[]{:S(2)}) collective-permute-start(f32[448,128]{1,0:T(8,128)S(1)} %get-tuple-element.41), channel_id=1, source_target_pairs={{0,1},{1,0},{2,3},{3,2},{4,5},{5,4},{6,7},{7,6},{8,9},{9,8},{10,11... | collective-permute-start | bytes 688136 | tf_op jit(solution)/shard_map/ppermute | solution.py:642
  15.4 7.9 %collective-permute-start.3 = (f32[112,128]{1,0:T(8,128)S(1)}, f32[112,128]{1,0:T(8,128)S(1)}, u32[]{:S(2)}, u32[]{:S(2)}) collective-permute-start(f32[112,128]{1,0:T(8,128)S(1)} %get-tuple-element.46), channel_id=1, source_target_pairs={{0,4},{1,5},{2,6},{3,7},{4,0},{5,1},{6,2},{7,3},{8,12},{9,13},{10,... | collective-permute-start | bytes 172040 | tf_op jit(solution)/shard_map/ppermute | solution.py:642
  18.1 5.2 %collective-permute-start.5 = (f32[112,128]{1,0:T(8,128)S(1)}, f32[112,128]{1,0:T(8,128)S(1)}, u32[]{:S(2)}, u32[]{:S(2)}) collective-permute-start(f32[112,128]{1,0:T(8,128)S(1)} %get-tuple-element.47), channel_id=1, source_target_pairs={{0,2},{1,3},{2,0},{3,1},{4,6},{5,7},{6,4},{7,5},{8,10},{9,11},{10,... | collective-permute-start | bytes 172040 | tf_op jit(solution)/shard_map/ppermute | solution.py:642
  19.2 6.0 %collective-permute-start.4 = (f32[112,128]{1,0:T(8,128)S(1)}, f32[112,128]{1,0:T(8,128)S(1)}, u32[]{:S(2)}, u32[]{:S(2)}) collective-permute-start(f32[112,128]{1,0:T(8,128)S(1)} %get-tuple-element.42._), channel_id=1, source_target_pairs={{0,6},{1,7},{2,4},{3,5},{4,2},{5,3},{6,0},{7,1},{8,14},{9,15},{10,... | collective-permute-start | bytes 172040 | tf_op jit(solution)/shard_map/ppermute | solution.py:642
  25.2 8.1 %collective-permute-start.8 = (f32[112,128]{1,0:T(8,128)S(1)}, f32[112,128]{1,0:T(8,128)S(1)}, u32[]{:S(2)}, u32[]{:S(2)}) collective-permute-start(f32[112,128]{1,0:T(8,128)S(1)} %sum_chunks.1._.refs_0_), channel_id=1, source_target_pairs={{0,6},{1,7},{2,4},{3,5},{4,2},{5,3},{6,0},{7,1},{8,14},{9,15},{10,... | collective-permute-start | bytes 172040 | tf_op jit(solution)/shard_map/ppermute | solution.py:642
  26.6 6.6 %collective-permute-start.7 = (f32[112,128]{1,0:T(8,128)S(1)}, f32[112,128]{1,0:T(8,128)S(1)}, u32[]{:S(2)}, u32[]{:S(2)}) collective-permute-start(f32[112,128]{1,0:T(8,128)S(1)} %sum_chunks.1._.refs_0_), channel_id=1, source_target_pairs={{0,4},{1,5},{2,6},{3,7},{4,0},{5,1},{6,2},{7,3},{8,12},{9,13},{10,... | collective-permute-start | bytes 172040 | tf_op jit(solution)/shard_map/ppermute | solution.py:642
  26.6 6.6 %collective-permute-start.6 = (f32[112,128]{1,0:T(8,128)S(1)}, f32[112,128]{1,0:T(8,128)S(1)}, u32[]{:S(2)}, u32[]{:S(2)}) collective-permute-start(f32[112,128]{1,0:T(8,128)S(1)} %sum_chunks.1._.refs_0_), channel_id=1, source_target_pairs={{0,2},{1,3},{2,0},{3,1},{4,6},{5,7},{6,4},{7,5},{8,10},{9,11},{10,... | collective-permute-start | bytes 172040 | tf_op jit(solution)/shard_map/ppermute | solution.py:642
  33.3 1.6 %collective-permute-start.9 = (f32[448,128]{1,0:T(8,128)S(1)}, f32[448,128]{1,0:T(8,128)S(1)}, u32[]{:S(2)}, u32[]{:S(2)}) collective-permute-start(f32[448,128]{1,0:T(8,128)S(1)} %join_chunks.1.half_ref), channel_id=1, source_target_pairs={{0,1},{1,0},{2,3},{3,2},{4,5},{5,4},{6,7},{7,6},{8,9},{9,8},{10,11... | collective-permute-start | bytes 688136 | tf_op jit(solution)/shard_map/ppermute | solution.py:642

commit v8 on v7

--- a/solution.py
+++ b/solution.py
@@ -270,7 +270,7 @@
 
 
 def grad_kernel(
-    table_ref, flags_ref, store, flip, store_dy, flip_dy, total, stack_ref, stack_dy_ref
+    table_ref, flags_ref, store, flip, store_dy, flip_dy, _, total, stack_ref, stack_dy_ref
 ):
     leaves = stack_ref.shape[0]
     for leaf in range(leaves):
@@ -296,18 +296,18 @@
                     total[:, (z + 1) * CH : (z + 2) * CH] += dot_lanes(unstack(stack), edge)
 
 
-def grad_terms(table, flags, store, flip, store_dy, flip_dy):
+def grad_terms(table, flags, store, flip, store_dy, flip_dy, after):
     leaves = store.shape[0] - 1
     stack = jax.ShapeDtypeStruct((leaves,) + STACK, BF)
     return pl.pallas_call(
         grad_kernel,
         out_shape=(jax.ShapeDtypeStruct((KROWS, 3 * CH), F32), stack, stack),
-        in_specs=[smem_spec()] * 2 + [vmem_spec()] * 4,
+        in_specs=[smem_spec()] * 2 + [vmem_spec()] * 4 + [any_spec()],
         out_specs=(vmem_spec(),) * 3,
         cost_estimate=cost(10**9, 2 * 10**6),
         compiler_params=params(),
         name="grad_terms",
-    )(table, flags, store, flip, store_dy, flip_dy)
+    )(table, flags, store, flip, store_dy, flip_dy, after)
 
 
 def third_part(row):
@@ -654,13 +654,13 @@
     chip = exchange(to_chip, 1, size)
     cross = lax.ppermute(to_cross, "dom", between + [(j, i) for i, j in between])
 
-    total, stack, stack_dy = grad_terms(own_table, flags, *fields)
+    total, stack, stack_dy = grad_terms(own_table, flags, *fields, to_cross)
     keep, send = grad_far(far_table, flags, store_dy, cross, chip, total)
     own, *to_send = split_chunks(keep, exchange(send, 1, size))
-    got = [exchange(to_send[m - 1], 2 * m, size) for m in (2, 3, 1)]
+    got = [exchange(to_send[m - 1], 2 * m, size) for m in (3, 2, 1)]
     out_features, out_done = conv(
         far_table, all_table, flags, occ, store, flip, cross, chip, weight, stack,
-        to_send[2], False,
+        to_send[0], False,
     )
     own = sum_chunks(own, got, out_done)
     if size > GROUP:

time: 36.1 us -> 35.4 us (0.981)
  waiting for transfers between devices: 3.83 us -> 3.14 us
    ppermute x9, waiting for transfers between devices: 3.82 us -> 3.14 us  [exchange(): return lax.ppermute(array, 'dom', [(i, i ^ mask) for i in range(size)])]
  transfers between devices with their start and end apart: 10 -> 10, of which waited for: 3 -> 4; matrix products, arithmetic and copies ran while one was open for 0% -> 0% of each run, Pallas kernels for 31% -> 31%
where the time goes in v8:
time: 35.4 us; the launch traced here: 35.2 us
  starting transfers between devices  14.2 us (40%)
  Pallas kernels  14.1 us (40%)
  waiting for transfers between devices  3.14 us (9%)
  local copies, waits for them, and re-layouts  2.09 us (6%)
  between operations  0.91 us (3%)
  other arithmetic  0.78 us (2%)
    ppermute x9, starting transfers between devices, exchange(): return lax.ppermute(array, 'dom', [(i, i ^ mask) for i in range(size)])  13.5 us
    pallas_call x2, Pallas kernels, conv(): pl.pallas_call(functools.partial(conv_kernel, turned), out_shape=(jax.Sha...  7.04 us
    ppermute x9, waiting for transfers between devices, exchange(): return lax.ppermute(array, 'dom', [(i, i ^ mask) for i in range(size)])  3.14 us
    pallas_call x1, Pallas kernels, grad_terms(): pl.pallas_call(grad_kernel, out_shape=(jax.ShapeDtypeStruct((KROWS, 3 * C...  3.03 us
    unnamed x6, local copies, waits for them, and re-layouts  2.09 us
    pallas_call x2, Pallas kernels, unpack(): pl.pallas_call(functools.partial(unpack_kernel, scale, not rest), out_sha...  1.84 us
    pallas_call x1, Pallas kernels, grad_far(): pl.pallas_call(grad_far_kernel, out_shape=(shape, shape), in_specs=[smem_...  1.46 us
    concatenate x1, other arithmetic, shards(): meta = jnp.concatenate([neighbors, mask_words], axis=1)  0.78 us
  transfers between devices with their start and end apart: 10, of which 4 were waited for; matrix products, arithmetic and copies ran while one was open for 0% of the time, Pallas kernels for 31%

profile of v8, /device:TPU:0, one launch (start us, length us, event | category | flops | bytes accessed | tf_op | source)
XLA Modules:
  0.0 35.2 jit_solution(1617359884570110327)
XLA Ops:
  0.6 0.8 %pad_add_fusion.meta_ref = s32[8,44]{1,0:T(8,128)S(1)} fusion(s32[8,18]{1,0:T(8,128)} %param.8, s32[8,26]{1,0:T(8,128)} %param.9), kind=kLoop, calls=%fused_computation | loop fusion | flops 352 | bytes 2816 | tf_op jit(solution)/shard_map/concatenate | solution.py:648
  1.4 0.0 copy-start.1
  1.4 1.0 %copy-done.1 = bf16[8,64,512]{2,1,0:T(8,128)(2,1)S(1)} copy-done((bf16[8,64,512]{2,1,0:T(8,128)(2,1)S(1)}, bf16[8,64,512]{2,1,0:T(8,128)(2,1)}, u32[]{:S(2)}) %copy-start.1) | copy-done | bytes 524312
  2.5 0.0 copy-start.2
  2.5 1.0 %copy-done.2 = bf16[8,64,512]{2,1,0:T(8,128)(2,1)S(1)} copy-done((bf16[8,64,512]{2,1,0:T(8,128)(2,1)S(1)}, bf16[8,64,512]{2,1,0:T(8,128)(2,1)}, u32[]{:S(2)}) %copy-start.2) | copy-done | bytes 524312
  3.5 0.6 %prepare.1 = (bf16[8,64,128]{2,1,0:T(8,128)(2,1)S(1)}, bf16[8,64,128]{2,1,0:T(8,128)(2,1)S(1)}, bf16[9,64,512]{2,1,0:T(8,128)(2,1)S(1)}, bf16[9,64,512]{2,1,0:T(...) custom-call(s32[8,44]{1,0:T(8,128)S(1)} %pad_add_fusion.meta_ref, ...), custom_call_target="tpu_custom_call" | custom-call | flops 1000000 | bytes 4000000 | tf_op jit(solution)/shard_map/prepare/pallas_call | solution.py:179
  4.1 0.5 %collective-permute-start.1 = (bf16[8,64,128]{2,1,0:T(8,128)(2,1)S(1)}, bf16[8,64,128]{2,1,0:T(8,128)(2,1)S(1)}, u32[]{:S(2)}, u32[]{:S(2)}) collective-permute-start(bf16[8,64,128]{2,1,0:T(8,128)(2,1)S(1)} %get-tuple-element.34), channel_id=1, source_target_pairs={{0,1},{1,0},{2,3},{3,2},{4,5},{5,4},{6,7},{7,6},{8,9},{9,8},{10,11... | collective-permute-start | bytes 393224 | tf_op jit(solution)/shard_map/ppermute | solution.py:642
  4.6 0.7 %collective-permute-start = (bf16[8,64,128]{2,1,0:T(8,128)(2,1)S(1)}, bf16[8,64,128]{2,1,0:T(8,128)(2,1)S(1)}, u32[]{:S(2)}, u32[]{:S(2)}) collective-permute-start(bf16[8,64,128]{2,1,0:T(8,128)(2,1)S(1)} %get-tuple-element.33._), channel_id=1, source_target_pairs={{1,2},{3,4},{5,6},{2,1},{4,3},{6,5},{9,10},{11,12},{13,14},{10,9},... | collective-permute-start | bytes 393224 | tf_op jit(solution)/shard_map/ppermute | solution.py:655
  5.3 0.0 copy-start
  5.3 3.0 %grad_terms.1 = (f32[576,192]{1,0:T(8,128)S(1)}, bf16[8,192,768]{2,1,0:T(8,128)(2,1)S(1)}, bf16[8,192,768]{2,1,0:T(8,128)(2,1)S(1)}) custom-call(s32[8,26]{1,0:T(8,128)S(1)} %get-tuple-element.35.table_ref, s32[8,128]{1,0:T(8,128)S(1)} %get-tuple-element.29.flags_ref, bf16[9,64,512]{2,1,0:T(8,128)(2,1)S(1)} %get-tuple-element.31.store.own, ...), custom_call_target="tpu_custom_call" | custom-call | flops 1000000000 | bytes 2000000 | tf_op jit(solution)/shard_map/grad_terms/pallas_call | solution.py:302
  8.4 0.0 collective-permute-done.1.chip_ref
  8.4 0.0 collective-permute-done.cross_ref
  8.4 1.5 %grad_far.1 = (f32[448,128]{1,0:T(8,128)S(1)}, f32[448,128]{1,0:T(8,128)S(1)}) custom-call(s32[8,26]{1,0:T(8,128)S(1)} %get-tuple-element.27.table_ref.far_table_ref, s32[8,128]{1,0:T(8,128)S(1)} %get-tuple-element.29.flags_ref, bf16[9,64,512]{2,1,0:T(8,128)(2,1)S(1)} %get-tuple-element.36.store_dy.own, ...), custom_call_target="tpu_custom_call" | custom-call | flops 100000000 | bytes 2000000 | tf_op jit(solution)/shard_map/grad_far/pallas_call | solution.py:389
  9.8 4.0 %collective-permute-start.2 = (f32[448,128]{1,0:T(8,128)S(1)}, f32[448,128]{1,0:T(8,128)S(1)}, u32[]{:S(2)}, u32[]{:S(2)}) collective-permute-start(f32[448,128]{1,0:T(8,128)S(1)} %get-tuple-element.41), channel_id=1, source_target_pairs={{0,1},{1,0},{2,3},{3,2},{4,5},{5,4},{6,7},{7,6},{8,9},{9,8},{10,11... | collective-permute-start | bytes 688136 | tf_op jit(solution)/shard_map/ppermute | solution.py:642
  13.9 1.1 %collective-permute-done.2.got_ref = f32[448,128]{1,0:T(8,128)S(1)} collective-permute-done((f32[448,128]{1,0:T(8,128)S(1)}, f32[448,128]{1,0:T(8,128)S(1)}, u32[]{:S(2)}, u32[]{:S(2)}) %collective-permute-start.2) | collective-permute-done | bytes 229408 | tf_op jit(solution)/shard_map/ppermute | solution.py:642
  15.0 3.6 %collective-permute-start.3 = (f32[112,128]{1,0:T(8,128)S(1)}, f32[112,128]{1,0:T(8,128)S(1)}, u32[]{:S(2)}, u32[]{:S(2)}) collective-permute-start(f32[112,128]{1,0:T(8,128)S(1)} %get-tuple-element.46), channel_id=1, source_target_pairs={{0,6},{1,7},{2,4},{3,5},{4,2},{5,3},{6,0},{7,1},{8,14},{9,15},{10,... | collective-permute-start | bytes 172040 | tf_op jit(solution)/shard_map/ppermute | solution.py:642
  18.7 0.0 collective-permute-start.4
  18.7 0.8 %collective-permute-start.5 = (f32[112,128]{1,0:T(8,128)S(1)}, f32[112,128]{1,0:T(8,128)S(1)}, u32[]{:S(2)}, u32[]{:S(2)}) collective-permute-start(f32[112,128]{1,0:T(8,128)S(1)} %get-tuple-element.42._), channel_id=1, source_target_pairs={{0,2},{1,3},{2,0},{3,1},{4,6},{5,7},{6,4},{7,5},{8,10},{9,11},{10,... | collective-permute-start | bytes 172040 | tf_op jit(solution)/shard_map/ppermute | solution.py:642
  19.5 0.0 copy-done
  19.5 3.4 %out_conv.1 = (bf16[8,64,512]{2,1,0:T(8,128)(2,1)}, f32[8,128]{1,0:T(8,128)S(1)}) custom-call(s32[8,26]{1,0:T(8,128)S(1)} %get-tuple-element.27.table_ref.far_table_ref, s32[8,26]{1,0:T(8,128)S(1)} %get-tuple-element.28.all_table_ref, s32[8,128]{1,0:T(8,128)S(1)} %get-tuple-element.29.flags_ref, f32[8,512]{1,0:T(8,128)S(1)} %get-tuple-element.30.occ_ref, ...), custom_call_target="tpu_custom_call" | custom-call | flops 1000000000 | bytes 2000000 | tf_op jit(solution)/shard_map/out_conv/pallas_call | solution.py:511
  22.9 0.0 collective-permute-done.3.refs_0_
  23.0 1.1 %collective-permute-done.4.refs_1_ = f32[112,128]{1,0:T(8,128)S(1)} collective-permute-done((f32[112,128]{1,0:T(8,128)S(1)}, f32[112,128]{1,0:T(8,128)S(1)}, u32[]{:S(2)}, u32[]{:S(2)}) %collective-permute-start.4) | collective-permute-done | bytes 57376 | tf_op jit(solution)/shard_map/ppermute | solution.py:642
  24.1 0.0 collective-permute-done.5.refs_2_
  24.1 2.5 %collective-permute-start.8 = (f32[112,128]{1,0:T(8,128)S(1)}, f32[112,128]{1,0:T(8,128)S(1)}, u32[]{:S(2)}, u32[]{:S(2)}) collective-permute-start(f32[112,128]{1,0:T(8,128)S(1)} %sum_chunks.1._.refs_0_), channel_id=1, source_target_pairs={{0,6},{1,7},{2,4},{3,5},{4,2},{5,3},{6,0},{7,1},{8,14},{9,15},{10,... | collective-permute-start | bytes 172040 | tf_op jit(solution)/shard_map/ppermute | solution.py:642
  26.6 0.0 collective-permute-start.7
  26.7 1.9 %collective-permute-start.6 = (f32[112,128]{1,0:T(8,128)S(1)}, f32[112,128]{1,0:T(8,128)S(1)}, u32[]{:S(2)}, u32[]{:S(2)}) collective-permute-start(f32[112,128]{1,0:T(8,128)S(1)} %sum_chunks.1._.refs_0_), channel_id=1, source_target_pairs={{0,2},{1,3},{2,0},{3,1},{4,6},{5,7},{6,4},{7,5},{8,10},{9,11},{10,... | collective-permute-start | bytes 172040 | tf_op jit(solution)/shard_map/ppermute | solution.py:642
  28.6 3.6 %in_grad_conv.1 = (bf16[8,64,512]{2,1,0:T(8,128)(2,1)}, f32[8,128]{1,0:T(8,128)S(1)}) custom-call(s32[8,26]{1,0:T(8,128)S(1)} %get-tuple-element.27.table_ref.far_table_ref, s32[8,26]{1,0:T(8,128)S(1)} %get-tuple-element.28.all_table_ref, s32[8,128]{1,0:T(8,128)S(1)} %get-tuple-element.29.flags_ref, f32[8,512]{1,0:T(8,128)S(1)} %get-tuple-element.30.occ_ref, ...), custom_call_target="tpu_custom_call" | custom-call | flops 1000000000 | bytes 2000000 | tf_op jit(solution)/shard_map/in_grad_conv/pallas_call | solution.py:511
  32.2 0.0 collective-permute-done.8.refs_3_
  32.2 0.4 %collective-permute-done.7.refs_2_ = f32[112,128]{1,0:T(8,128)S(1)} collective-permute-done((f32[112,128]{1,0:T(8,128)S(1)}, f32[112,128]{1,0:T(8,128)S(1)}, u32[]{:S(2)}, u32[]{:S(2)}) %collective-permute-start.7) | collective-permute-done | bytes 57376 | tf_op jit(solution)/shard_map/ppermute | solution.py:642
  32.5 0.0 collective-permute-done.6.refs_1_
  32.6 0.1 collective-permute-start.9
  32.6 1.0 %unpack_own.1.refs_0_ = f32[27,64,64]{2,1,0:T(8,128)} custom-call(f32[448,128]{1,0:T(8,128)S(1)} %join_chunks.1.half_ref), custom_call_target="tpu_custom_call" | custom-call | flops 1000000 | bytes 1000000 | tf_op jit(solution)/shard_map/unpack_own/pallas_call | solution.py:628
  33.6 0.5 %collective-permute-done.9.half_ref = f32[448,128]{1,0:T(8,128)S(1)} collective-permute-done((f32[448,128]{1,0:T(8,128)S(1)}, f32[448,128]{1,0:T(8,128)S(1)}, u32[]{:S(2)}, u32[]{:S(2)}) %collective-permute-start.9) | collective-permute-done | bytes 229408 | tf_op jit(solution)/shard_map/ppermute | solution.py:642
  34.1 0.9 %unpack_other.1 = f32[27,64,64]{2,1,0:T(8,128)} custom-call(f32[448,128]{1,0:T(8,128)S(1)} %collective-permute-done.9.half_ref, f32[27,64,64]{2,1,0:T(8,128)} %unpack_own.1.refs_0_), custom_call_target="tpu_custom_call", output_to_operand_aliasing={{}: (1, {})} | custom-call | flops 1000000 | bytes 1000000 | tf_op jit(solution)/shard_map/unpack_other/pallas_call | solution.py:628
  (3 shorter events, 0.1 us)
Async XLA Ops:
  1.4 1.0 %copy-start.1 = (bf16[8,64,512]{2,1,0:T(8,128)(2,1)S(1)}, bf16[8,64,512]{2,1,0:T(8,128)(2,1)}, u32[]{:S(2)}) copy-start(bf16[8,64,512]{2,1,0:T(8,128)(2,1)} %x_ref.1) | copy-start | bytes 1572868
  2.5 1.0 %copy-start.2 = (bf16[8,64,512]{2,1,0:T(8,128)(2,1)S(1)}, bf16[8,64,512]{2,1,0:T(8,128)(2,1)}, u32[]{:S(2)}) copy-start(bf16[8,64,512]{2,1,0:T(8,128)(2,1)} %d_ref.1) | copy-start | bytes 1572868
  4.1 4.2 %collective-permute-start.1 = (bf16[8,64,128]{2,1,0:T(8,128)(2,1)S(1)}, bf16[8,64,128]{2,1,0:T(8,128)(2,1)S(1)}, u32[]{:S(2)}, u32[]{:S(2)}) collective-permute-start(bf16[8,64,128]{2,1,0:T(8,128)(2,1)S(1)} %get-tuple-element.34), channel_id=1, source_target_pairs={{0,1},{1,0},{2,3},{3,2},{4,5},{5,4},{6,7},{7,6},{8,9},{9,8},{10,11... | collective-permute-start | bytes 393224 | tf_op jit(solution)/shard_map/ppermute | solution.py:642
  4.6 3.7 %collective-permute-start = (bf16[8,64,128]{2,1,0:T(8,128)(2,1)S(1)}, bf16[8,64,128]{2,1,0:T(8,128)(2,1)S(1)}, u32[]{:S(2)}, u32[]{:S(2)}) collective-permute-start(bf16[8,64,128]{2,1,0:T(8,128)(2,1)S(1)} %get-tuple-element.33._), channel_id=1, source_target_pairs={{1,2},{3,4},{5,6},{2,1},{4,3},{6,5},{9,10},{11,12},{13,14},{10,9},... | collective-permute-start | bytes 393224 | tf_op jit(solution)/shard_map/ppermute | solution.py:655
  5.3 14.2 %copy-start = (bf16[27,64,64]{2,1,0:T(8,128)(2,1)S(1)}, bf16[27,64,64]{2,1,0:T(8,128)(2,1)}, u32[]{:S(2)}) copy-start(bf16[27,64,64]{2,1,0:T(8,128)(2,1)} %w_ref.3) | copy-start | bytes 663556
  9.8 5.1 %collective-permute-start.2 = (f32[448,128]{1,0:T(8,128)S(1)}, f32[448,128]{1,0:T(8,128)S(1)}, u32[]{:S(2)}, u32[]{:S(2)}) collective-permute-start(f32[448,128]{1,0:T(8,128)S(1)} %get-tuple-element.41), channel_id=1, source_target_pairs={{0,1},{1,0},{2,3},{3,2},{4,5},{5,4},{6,7},{7,6},{8,9},{9,8},{10,11... | collective-permute-start | bytes 688136 | tf_op jit(solution)/shard_map/ppermute | solution.py:642
  15.0 7.9 %collective-permute-start.3 = (f32[112,128]{1,0:T(8,128)S(1)}, f32[112,128]{1,0:T(8,128)S(1)}, u32[]{:S(2)}, u32[]{:S(2)}) collective-permute-start(f32[112,128]{1,0:T(8,128)S(1)} %get-tuple-element.46), channel_id=1, source_target_pairs={{0,6},{1,7},{2,4},{3,5},{4,2},{5,3},{6,0},{7,1},{8,14},{9,15},{10,... | collective-permute-start | bytes 172040 | tf_op jit(solution)/shard_map/ppermute | solution.py:642
  18.7 5.4 %collective-permute-start.4 = (f32[112,128]{1,0:T(8,128)S(1)}, f32[112,128]{1,0:T(8,128)S(1)}, u32[]{:S(2)}, u32[]{:S(2)}) collective-permute-start(f32[112,128]{1,0:T(8,128)S(1)} %get-tuple-element.47), channel_id=1, source_target_pairs={{0,4},{1,5},{2,6},{3,7},{4,0},{5,1},{6,2},{7,3},{8,12},{9,13},{10,... | collective-permute-start | bytes 172040 | tf_op jit(solution)/shard_map/ppermute | solution.py:642
  18.7 5.4 %collective-permute-start.5 = (f32[112,128]{1,0:T(8,128)S(1)}, f32[112,128]{1,0:T(8,128)S(1)}, u32[]{:S(2)}, u32[]{:S(2)}) collective-permute-start(f32[112,128]{1,0:T(8,128)S(1)} %get-tuple-element.42._), channel_id=1, source_target_pairs={{0,2},{1,3},{2,0},{3,1},{4,6},{5,7},{6,4},{7,5},{8,10},{9,11},{10,... | collective-permute-start | bytes 172040 | tf_op jit(solution)/shard_map/ppermute | solution.py:642
  24.1 8.1 %collective-permute-start.8 = (f32[112,128]{1,0:T(8,128)S(1)}, f32[112,128]{1,0:T(8,128)S(1)}, u32[]{:S(2)}, u32[]{:S(2)}) collective-permute-start(f32[112,128]{1,0:T(8,128)S(1)} %sum_chunks.1._.refs_0_), channel_id=1, source_target_pairs={{0,6},{1,7},{2,4},{3,5},{4,2},{5,3},{6,0},{7,1},{8,14},{9,15},{10,... | collective-permute-start | bytes 172040 | tf_op jit(solution)/shard_map/ppermute | solution.py:642
  26.6 5.9 %collective-permute-start.7 = (f32[112,128]{1,0:T(8,128)S(1)}, f32[112,128]{1,0:T(8,128)S(1)}, u32[]{:S(2)}, u32[]{:S(2)}) collective-permute-start(f32[112,128]{1,0:T(8,128)S(1)} %sum_chunks.1._.refs_0_), channel_id=1, source_target_pairs={{0,4},{1,5},{2,6},{3,7},{4,0},{5,1},{6,2},{7,3},{8,12},{9,13},{10,... | collective-permute-start | bytes 172040 | tf_op jit(solution)/shard_map/ppermute | solution.py:642
  26.7 5.8 %collective-permute-start.6 = (f32[112,128]{1,0:T(8,128)S(1)}, f32[112,128]{1,0:T(8,128)S(1)}, u32[]{:S(2)}, u32[]{:S(2)}) collective-permute-start(f32[112,128]{1,0:T(8,128)S(1)} %sum_chunks.1._.refs_0_), channel_id=1, source_target_pairs={{0,2},{1,3},{2,0},{3,1},{4,6},{5,7},{6,4},{7,5},{8,10},{9,11},{10,... | collective-permute-start | bytes 172040 | tf_op jit(solution)/shard_map/ppermute | solution.py:642
  32.6 1.6 %collective-permute-start.9 = (f32[448,128]{1,0:T(8,128)S(1)}, f32[448,128]{1,0:T(8,128)S(1)}, u32[]{:S(2)}, u32[]{:S(2)}) collective-permute-start(f32[448,128]{1,0:T(8,128)S(1)} %join_chunks.1.half_ref), channel_id=1, source_target_pairs={{0,1},{1,0},{2,3},{3,2},{4,5},{5,4},{6,7},{7,6},{8,9},{9,8},{10,11... | collective-permute-start | bytes 688136 | tf_op jit(solution)/shard_map/ppermute | solution.py:642

commit v9 on v8

--- a/solution.py
+++ b/solution.py
@@ -650,11 +650,14 @@
         meta, features, cotangent
     )
     store, flip, store_dy, flip_dy = fields
-    between = [(i, i + 1) for i in range(1, size - 1, 2)]
+    forward = exchange(to_cross, 1, size)
     chip = exchange(to_chip, 1, size)
-    cross = lax.ppermute(to_cross, "dom", between + [(j, i) for i, j in between])
-
-    total, stack, stack_dy = grad_terms(own_table, flags, *fields, to_cross)
+    steps = range(0, size - 2, 2)
+    cross = lax.ppermute(
+        forward, "dom", [(i, i + 2) for i in steps] + [(i + 3, i + 1) for i in steps]
+    )
+
+    total, stack, stack_dy = grad_terms(own_table, flags, *fields, forward)
     keep, send = grad_far(far_table, flags, store_dy, cross, chip, total)
     own, *to_send = split_chunks(keep, exchange(send, 1, size))
     got = [exchange(to_send[m - 1], 2 * m, size) for m in (3, 2, 1)]

time: 35.4 us -> 37.2 us (1.051)
  waiting for transfers between devices: 3.14 us -> 4.47 us
  starting transfers between devices: 14.2 us -> 14.6 us
    ppermute x1, starting transfers between devices: 0.66 us -> 4.83 us  [shards(): lax.ppermute(forward, 'dom', [(i, i + 2) for i in steps] + [(i + 3, i + 1...]
    ppermute x9 -> x10, starting transfers between devices: 13.5 us -> 9.76 us  [exchange(): return lax.ppermute(array, 'dom', [(i, i ^ mask) for i in range(size)])]
    ppermute x9 -> x10, waiting for transfers between devices: 3.14 us -> 4.47 us  [exchange(): return lax.ppermute(array, 'dom', [(i, i ^ mask) for i in range(size)])]
  transfers between devices with their start and end apart: 10 -> 11, of which waited for: 4 -> 5; matrix products, arithmetic and copies ran while one was open for 0% -> 0% of each run, Pallas kernels for 31% -> 30%
where the time goes in v9:
time: 37.2 us; the launch traced here: 37 us
  starting transfers between devices  14.6 us (39%)
  Pallas kernels  14.1 us (38%)
  waiting for transfers between devices  4.47 us (12%)
  local copies, waits for them, and re-layouts  2.09 us (6%)
  between operations  0.92 us (2%)
  other arithmetic  0.78 us (2%)
    ppermute x10, starting transfers between devices, exchange(): return lax.ppermute(array, 'dom', [(i, i ^ mask) for i in range(size)])  9.76 us
    pallas_call x2, Pallas kernels, conv(): pl.pallas_call(functools.partial(conv_kernel, turned), out_shape=(jax.Sha...  7.05 us
    ppermute x1, starting transfers between devices, shards(): lax.ppermute(forward, 'dom', [(i, i + 2) for i in steps] + [(i + 3, i + 1...  4.83 us
    ppermute x10, waiting for transfers between devices, exchange(): return lax.ppermute(array, 'dom', [(i, i ^ mask) for i in range(size)])  4.47 us
    pallas_call x1, Pallas kernels, grad_terms(): pl.pallas_call(grad_kernel, out_shape=(jax.ShapeDtypeStruct((KROWS, 3 * C...  3.06 us
    unnamed x6, local copies, waits for them, and re-layouts  2.09 us
    pallas_call x2, Pallas kernels, unpack(): pl.pallas_call(functools.partial(unpack_kernel, scale, not rest), out_sha...  1.84 us
    pallas_call x1, Pallas kernels, grad_far(): pl.pallas_call(grad_far_kernel, out_shape=(shape, shape), in_specs=[smem_...  1.46 us
  transfers between devices with their start and end apart: 11, of which 5 were waited for; matrix products, arithmetic and copies ran while one was open for 0% of the time, Pallas kernels for 30%

profile of v9, /device:TPU:0, one launch (start us, length us, event | category | flops | bytes accessed | tf_op | source)
XLA Modules:
  0.0 37.0 jit_solution(1272194787739310169)
XLA Ops:
  0.6 0.8 %pad_add_fusion.meta_ref = s32[8,44]{1,0:T(8,128)S(1)} fusion(s32[8,18]{1,0:T(8,128)} %param.8, s32[8,26]{1,0:T(8,128)} %param.9), kind=kLoop, calls=%fused_computation | loop fusion | flops 352 | bytes 2816 | tf_op jit(solution)/shard_map/concatenate | solution.py:648
  1.4 0.0 copy-start.1
  1.4 1.0 %copy-done.1 = bf16[8,64,512]{2,1,0:T(8,128)(2,1)S(1)} copy-done((bf16[8,64,512]{2,1,0:T(8,128)(2,1)S(1)}, bf16[8,64,512]{2,1,0:T(8,128)(2,1)}, u32[]{:S(2)}) %copy-start.1) | copy-done | bytes 524312
  2.5 0.0 copy-start.2
  2.5 1.0 %copy-done.2 = bf16[8,64,512]{2,1,0:T(8,128)(2,1)S(1)} copy-done((bf16[8,64,512]{2,1,0:T(8,128)(2,1)S(1)}, bf16[8,64,512]{2,1,0:T(8,128)(2,1)}, u32[]{:S(2)}) %copy-start.2) | copy-done | bytes 524312
  3.5 0.6 %prepare.1 = (bf16[8,64,128]{2,1,0:T(8,128)(2,1)S(1)}, bf16[8,64,128]{2,1,0:T(8,128)(2,1)S(1)}, bf16[9,64,512]{2,1,0:T(8,128)(2,1)S(1)}, bf16[9,64,512]{2,1,0:T(...) custom-call(s32[8,44]{1,0:T(8,128)S(1)} %pad_add_fusion.meta_ref, ...), custom_call_target="tpu_custom_call" | custom-call | flops 1000000 | bytes 4000000 | tf_op jit(solution)/shard_map/prepare/pallas_call | solution.py:179
  4.1 0.5 %collective-permute-start = (bf16[8,64,128]{2,1,0:T(8,128)(2,1)S(1)}, bf16[8,64,128]{2,1,0:T(8,128)(2,1)S(1)}, u32[]{:S(2)}, u32[]{:S(2)}) collective-permute-start(bf16[8,64,128]{2,1,0:T(8,128)(2,1)S(1)} %get-tuple-element.33), channel_id=1, source_target_pairs={{0,1},{1,0},{2,3},{3,2},{4,5},{5,4},{6,7},{7,6},{8,9},{9,8},{10,11... | collective-permute-start | bytes 393224 | tf_op jit(solution)/shard_map/ppermute | solution.py:642
  4.6 0.1 collective-permute-start.2
  4.7 0.9 %collective-permute-done._ = bf16[8,64,128]{2,1,0:T(8,128)(2,1)S(1)} collective-permute-done((bf16[8,64,128]{2,1,0:T(8,128)(2,1)S(1)}, bf16[8,64,128]{2,1,0:T(8,128)(2,1)S(1)}, u32[]{:S(2)}, u32[]{:S(2)}) %collective-permute-start) | collective-permute-done | bytes 131104 | tf_op jit(solution)/shard_map/ppermute | solution.py:642
  5.6 4.8 %collective-permute-start.1 = (bf16[8,64,128]{2,1,0:T(8,128)(2,1)S(1)}, bf16[8,64,128]{2,1,0:T(8,128)(2,1)S(1)}, u32[]{:S(2)}, u32[]{:S(2)}) collective-permute-start(bf16[8,64,128]{2,1,0:T(8,128)(2,1)S(1)} %collective-permute-done._), channel_id=1, source_target_pairs={{0,2},{2,4},{4,6},{3,1},{5,3},{7,5},{8,10},{10,12},{12,14},{11,9},... | collective-permute-start | bytes 393224 | tf_op jit(solution)/shard_map/ppermute | solution.py:656
  10.5 0.0 copy-start
  10.5 3.1 %grad_terms.1 = (f32[576,192]{1,0:T(8,128)S(1)}, bf16[8,192,768]{2,1,0:T(8,128)(2,1)S(1)}, bf16[8,192,768]{2,1,0:T(8,128)(2,1)S(1)}) custom-call(s32[8,26]{1,0:T(8,128)S(1)} %get-tuple-element.35.table_ref, s32[8,128]{1,0:T(8,128)S(1)} %get-tuple-element.29.flags_ref, bf16[9,64,512]{2,1,0:T(8,128)(2,1)S(1)} %get-tuple-element.31.store.own, ...), custom_call_target="tpu_custom_call" | custom-call | flops 1000000000 | bytes 2000000 | tf_op jit(solution)/shard_map/grad_terms/pallas_call | solution.py:302
  13.5 0.0 collective-permute-done.2.chip_ref
  13.6 0.0 collective-permute-done.1.cross_ref
  13.6 1.5 %grad_far.1 = (f32[448,128]{1,0:T(8,128)S(1)}, f32[448,128]{1,0:T(8,128)S(1)}) custom-call(s32[8,26]{1,0:T(8,128)S(1)} %get-tuple-element.27.table_ref.far_table_ref, s32[8,128]{1,0:T(8,128)S(1)} %get-tuple-element.29.flags_ref, bf16[9,64,512]{2,1,0:T(8,128)(2,1)S(1)} %get-tuple-element.36.store_dy.own, ...), custom_call_target="tpu_custom_call" | custom-call | flops 100000000 | bytes 2000000 | tf_op jit(solution)/shard_map/grad_far/pallas_call | solution.py:389
  15.0 0.1 collective-permute-start.3
  15.1 1.5 %collective-permute-done.3.got_ref = f32[448,128]{1,0:T(8,128)S(1)} collective-permute-done((f32[448,128]{1,0:T(8,128)S(1)}, f32[448,128]{1,0:T(8,128)S(1)}, u32[]{:S(2)}, u32[]{:S(2)}) %collective-permute-start.3) | collective-permute-done | bytes 229408 | tf_op jit(solution)/shard_map/ppermute | solution.py:642
  16.6 3.9 %collective-permute-start.4 = (f32[112,128]{1,0:T(8,128)S(1)}, f32[112,128]{1,0:T(8,128)S(1)}, u32[]{:S(2)}, u32[]{:S(2)}) collective-permute-start(f32[112,128]{1,0:T(8,128)S(1)} %get-tuple-element.46), channel_id=1, source_target_pairs={{0,6},{1,7},{2,4},{3,5},{4,2},{5,3},{6,0},{7,1},{8,14},{9,15},{10,... | collective-permute-start | bytes 172040 | tf_op jit(solution)/shard_map/ppermute | solution.py:642
  20.6 0.0 collective-permute-start.5
  20.6 0.6 %collective-permute-start.6 = (f32[112,128]{1,0:T(8,128)S(1)}, f32[112,128]{1,0:T(8,128)S(1)}, u32[]{:S(2)}, u32[]{:S(2)}) collective-permute-start(f32[112,128]{1,0:T(8,128)S(1)} %get-tuple-element.42._), channel_id=1, source_target_pairs={{0,2},{1,3},{2,0},{3,1},{4,6},{5,7},{6,4},{7,5},{8,10},{9,11},{10,... | collective-permute-start | bytes 172040 | tf_op jit(solution)/shard_map/ppermute | solution.py:642
  21.2 0.0 copy-done
  21.2 3.5 %out_conv.1 = (bf16[8,64,512]{2,1,0:T(8,128)(2,1)}, f32[8,128]{1,0:T(8,128)S(1)}) custom-call(s32[8,26]{1,0:T(8,128)S(1)} %get-tuple-element.27.table_ref.far_table_ref, s32[8,26]{1,0:T(8,128)S(1)} %get-tuple-element.28.all_table_ref, s32[8,128]{1,0:T(8,128)S(1)} %get-tuple-element.29.flags_ref, f32[8,512]{1,0:T(8,128)S(1)} %get-tuple-element.30.occ_ref, ...), custom_call_target="tpu_custom_call" | custom-call | flops 1000000000 | bytes 2000000 | tf_op jit(solution)/shard_map/out_conv/pallas_call | solution.py:511
  24.7 0.0 collective-permute-done.4.refs_0_
  24.7 1.3 %collective-permute-done.5.refs_1_ = f32[112,128]{1,0:T(8,128)S(1)} collective-permute-done((f32[112,128]{1,0:T(8,128)S(1)}, f32[112,128]{1,0:T(8,128)S(1)}, u32[]{:S(2)}, u32[]{:S(2)}) %collective-permute-start.5) | collective-permute-done | bytes 57376 | tf_op jit(solution)/shard_map/ppermute | solution.py:642
  26.0 0.0 collective-permute-done.6.refs_2_
  26.0 2.5 %collective-permute-start.9 = (f32[112,128]{1,0:T(8,128)S(1)}, f32[112,128]{1,0:T(8,128)S(1)}, u32[]{:S(2)}, u32[]{:S(2)}) collective-permute-start(f32[112,128]{1,0:T(8,128)S(1)} %sum_chunks.1._.refs_0_), channel_id=1, source_target_pairs={{0,6},{1,7},{2,4},{3,5},{4,2},{5,3},{6,0},{7,1},{8,14},{9,15},{10,... | collective-permute-start | bytes 172040 | tf_op jit(solution)/shard_map/ppermute | solution.py:642
  28.5 0.1 collective-permute-start.8
  28.6 1.9 %collective-permute-start.7 = (f32[112,128]{1,0:T(8,128)S(1)}, f32[112,128]{1,0:T(8,128)S(1)}, u32[]{:S(2)}, u32[]{:S(2)}) collective-permute-start(f32[112,128]{1,0:T(8,128)S(1)} %sum_chunks.1._.refs_0_), channel_id=1, source_target_pairs={{0,2},{1,3},{2,0},{3,1},{4,6},{5,7},{6,4},{7,5},{8,10},{9,11},{10,... | collective-permute-start | bytes 172040 | tf_op jit(solution)/shard_map/ppermute | solution.py:642
  30.4 3.6 %in_grad_conv.1 = (bf16[8,64,512]{2,1,0:T(8,128)(2,1)}, f32[8,128]{1,0:T(8,128)S(1)}) custom-call(s32[8,26]{1,0:T(8,128)S(1)} %get-tuple-element.27.table_ref.far_table_ref, s32[8,26]{1,0:T(8,128)S(1)} %get-tuple-element.28.all_table_ref, s32[8,128]{1,0:T(8,128)S(1)} %get-tuple-element.29.flags_ref, f32[8,512]{1,0:T(8,128)S(1)} %get-tuple-element.30.occ_ref, ...), custom_call_target="tpu_custom_call" | custom-call | flops 1000000000 | bytes 2000000 | tf_op jit(solution)/shard_map/in_grad_conv/pallas_call | solution.py:511
  34.0 0.0 collective-permute-done.9.refs_3_
  34.0 0.3 collective-permute-done.8.refs_2_
  34.3 0.0 collective-permute-done.7.refs_1_
  34.4 0.1 collective-permute-start.10
  34.4 1.0 %unpack_own.1.refs_0_ = f32[27,64,64]{2,1,0:T(8,128)} custom-call(f32[448,128]{1,0:T(8,128)S(1)} %join_chunks.1.half_ref), custom_call_target="tpu_custom_call" | custom-call | flops 1000000 | bytes 1000000 | tf_op jit(solution)/shard_map/unpack_own/pallas_call | solution.py:628
  35.4 0.5 %collective-permute-done.10.half_ref = f32[448,128]{1,0:T(8,128)S(1)} collective-permute-done((f32[448,128]{1,0:T(8,128)S(1)}, f32[448,128]{1,0:T(8,128)S(1)}, u32[]{:S(2)}, u32[]{:S(2)}) %collective-permute-start.10) | collective-permute-done | bytes 229408 | tf_op jit(solution)/shard_map/ppermute | solution.py:642
  35.9 0.9 %unpack_other.1 = f32[27,64,64]{2,1,0:T(8,128)} custom-call(f32[448,128]{1,0:T(8,128)S(1)} %collective-permute-done.10.half_ref, f32[27,64,64]{2,1,0:T(8,128)} %unpack_own.1.refs_0_), custom_call_target="tpu_custom_call", output_to_operand_aliasing={{}: (1, {})} | custom-call | flops 1000000 | bytes 1000000 | tf_op jit(solution)/shard_map/unpack_other/pallas_call | solution.py:628
  (3 shorter events, 0.1 us)
Async XLA Ops:
  1.4 1.0 %copy-start.1 = (bf16[8,64,512]{2,1,0:T(8,128)(2,1)S(1)}, bf16[8,64,512]{2,1,0:T(8,128)(2,1)}, u32[]{:S(2)}) copy-start(bf16[8,64,512]{2,1,0:T(8,128)(2,1)} %x_ref.1) | copy-start | bytes 1572868
  2.5 1.0 %copy-start.2 = (bf16[8,64,512]{2,1,0:T(8,128)(2,1)S(1)}, bf16[8,64,512]{2,1,0:T(8,128)(2,1)}, u32[]{:S(2)}) copy-start(bf16[8,64,512]{2,1,0:T(8,128)(2,1)} %d_ref.1) | copy-start | bytes 1572868
  4.1 1.5 %collective-permute-start = (bf16[8,64,128]{2,1,0:T(8,128)(2,1)S(1)}, bf16[8,64,128]{2,1,0:T(8,128)(2,1)S(1)}, u32[]{:S(2)}, u32[]{:S(2)}) collective-permute-start(bf16[8,64,128]{2,1,0:T(8,128)(2,1)S(1)} %get-tuple-element.33), channel_id=1, source_target_pairs={{0,1},{1,0},{2,3},{3,2},{4,5},{5,4},{6,7},{7,6},{8,9},{9,8},{10,11... | collective-permute-start | bytes 393224 | tf_op jit(solution)/shard_map/ppermute | solution.py:642
  4.6 8.9 %collective-permute-start.2 = (bf16[8,64,128]{2,1,0:T(8,128)(2,1)S(1)}, bf16[8,64,128]{2,1,0:T(8,128)(2,1)S(1)}, u32[]{:S(2)}, u32[]{:S(2)}) collective-permute-start(bf16[8,64,128]{2,1,0:T(8,128)(2,1)S(1)} %get-tuple-element.34), channel_id=1, source_target_pairs={{0,1},{1,0},{2,3},{3,2},{4,5},{5,4},{6,7},{7,6},{8,9},{9,8},{10,11... | collective-permute-start | bytes 393224 | tf_op jit(solution)/shard_map/ppermute | solution.py:642
  5.6 7.9 %collective-permute-start.1 = (bf16[8,64,128]{2,1,0:T(8,128)(2,1)S(1)}, bf16[8,64,128]{2,1,0:T(8,128)(2,1)S(1)}, u32[]{:S(2)}, u32[]{:S(2)}) collective-permute-start(bf16[8,64,128]{2,1,0:T(8,128)(2,1)S(1)} %collective-permute-done._), channel_id=1, source_target_pairs={{0,2},{2,4},{4,6},{3,1},{5,3},{7,5},{8,10},{10,12},{12,14},{11,9},... | collective-permute-start | bytes 393224 | tf_op jit(solution)/shard_map/ppermute | solution.py:656
  10.5 10.8 %copy-start = (bf16[27,64,64]{2,1,0:T(8,128)(2,1)S(1)}, bf16[27,64,64]{2,1,0:T(8,128)(2,1)}, u32[]{:S(2)}) copy-start(bf16[27,64,64]{2,1,0:T(8,128)(2,1)} %w_ref.3) | copy-start | bytes 663556
  15.0 1.6 %collective-permute-start.3 = (f32[448,128]{1,0:T(8,128)S(1)}, f32[448,128]{1,0:T(8,128)S(1)}, u32[]{:S(2)}, u32[]{:S(2)}) collective-permute-start(f32[448,128]{1,0:T(8,128)S(1)} %get-tuple-element.41), channel_id=1, source_target_pairs={{0,1},{1,0},{2,3},{3,2},{4,5},{5,4},{6,7},{7,6},{8,9},{9,8},{10,11... | collective-permute-start | bytes 688136 | tf_op jit(solution)/shard_map/ppermute | solution.py:642
  16.6 8.0 %collective-permute-start.4 = (f32[112,128]{1,0:T(8,128)S(1)}, f32[112,128]{1,0:T(8,128)S(1)}, u32[]{:S(2)}, u32[]{:S(2)}) collective-permute-start(f32[112,128]{1,0:T(8,128)S(1)} %get-tuple-element.46), channel_id=1, source_target_pairs={{0,6},{1,7},{2,4},{3,5},{4,2},{5,3},{6,0},{7,1},{8,14},{9,15},{10,... | collective-permute-start | bytes 172040 | tf_op jit(solution)/shard_map/ppermute | solution.py:642
  20.6 5.4 %collective-permute-start.5 = (f32[112,128]{1,0:T(8,128)S(1)}, f32[112,128]{1,0:T(8,128)S(1)}, u32[]{:S(2)}, u32[]{:S(2)}) collective-permute-start(f32[112,128]{1,0:T(8,128)S(1)} %get-tuple-element.47), channel_id=1, source_target_pairs={{0,4},{1,5},{2,6},{3,7},{4,0},{5,1},{6,2},{7,3},{8,12},{9,13},{10,... | collective-permute-start | bytes 172040 | tf_op jit(solution)/shard_map/ppermute | solution.py:642
  20.6 5.4 %collective-permute-start.6 = (f32[112,128]{1,0:T(8,128)S(1)}, f32[112,128]{1,0:T(8,128)S(1)}, u32[]{:S(2)}, u32[]{:S(2)}) collective-permute-start(f32[112,128]{1,0:T(8,128)S(1)} %get-tuple-element.42._), channel_id=1, source_target_pairs={{0,2},{1,3},{2,0},{3,1},{4,6},{5,7},{6,4},{7,5},{8,10},{9,11},{10,... | collective-permute-start | bytes 172040 | tf_op jit(solution)/shard_map/ppermute | solution.py:642
  26.0 8.1 %collective-permute-start.9 = (f32[112,128]{1,0:T(8,128)S(1)}, f32[112,128]{1,0:T(8,128)S(1)}, u32[]{:S(2)}, u32[]{:S(2)}) collective-permute-start(f32[112,128]{1,0:T(8,128)S(1)} %sum_chunks.1._.refs_0_), channel_id=1, source_target_pairs={{0,6},{1,7},{2,4},{3,5},{4,2},{5,3},{6,0},{7,1},{8,14},{9,15},{10,... | collective-permute-start | bytes 172040 | tf_op jit(solution)/shard_map/ppermute | solution.py:642
  28.5 5.8 %collective-permute-start.8 = (f32[112,128]{1,0:T(8,128)S(1)}, f32[112,128]{1,0:T(8,128)S(1)}, u32[]{:S(2)}, u32[]{:S(2)}) collective-permute-start(f32[112,128]{1,0:T(8,128)S(1)} %sum_chunks.1._.refs_0_), channel_id=1, source_target_pairs={{0,4},{1,5},{2,6},{3,7},{4,0},{5,1},{6,2},{7,3},{8,12},{9,13},{10,... | collective-permute-start | bytes 172040 | tf_op jit(solution)/shard_map/ppermute | solution.py:642
  28.6 5.7 %collective-permute-start.7 = (f32[112,128]{1,0:T(8,128)S(1)}, f32[112,128]{1,0:T(8,128)S(1)}, u32[]{:S(2)}, u32[]{:S(2)}) collective-permute-start(f32[112,128]{1,0:T(8,128)S(1)} %sum_chunks.1._.refs_0_), channel_id=1, source_target_pairs={{0,2},{1,3},{2,0},{3,1},{4,6},{5,7},{6,4},{7,5},{8,10},{9,11},{10,... | collective-permute-start | bytes 172040 | tf_op jit(solution)/shard_map/ppermute | solution.py:642
  34.4 1.6 %collective-permute-start.10 = (f32[448,128]{1,0:T(8,128)S(1)}, f32[448,128]{1,0:T(8,128)S(1)}, u32[]{:S(2)}, u32[]{:S(2)}) collective-permute-start(f32[448,128]{1,0:T(8,128)S(1)} %join_chunks.1.half_ref), channel_id=1, source_target_pairs={{0,1},{1,0},{2,3},{3,2},{4,5},{5,4},{6,7},{7,6},{8,9},{9,8},{10,11... | collective-permute-start | bytes 688136 | tf_op jit(solution)/shard_map/ppermute | solution.py:642
